TPU v7x, 256 devices: a whole 4x4x8 slice. The times are simulated.
256 devices in a mesh: grp: 4 (over x), own: 64 (over y, z, core).
Axes of the slice: x: 4, y: 4, z: 8, core: 2. Of those that a mesh axis runs over, the one named last changes fastest.
Arguments:
- head_rows: bfloat16 [196608, 400], P(('grp', 'own'))
- tail_rows: bfloat16 [196608, 400], P(('grp', 'own'))
- rel_ids: int32 [196608], P(('grp', 'own')), may hold values from 0 to 1499
- neg_rows: bfloat16 [65536, 400], P(('grp', 'own'))
- rel_table: float32 [1500, 400], replicated
- owner_counts: int32 [256, 64], P(('grp', 'own')), may hold values from 1 to 16, as said below
- unique_ids: int32 [256, 1024], P(('grp', 'own')), may hold values from 0 to 1023, as said below
- head_slot: int32 [196608], P(('grp', 'own')), may hold values from 0 to 1023, as said below
- tail_slot: int32 [196608], P(('grp', 'own')), may hold values from 0 to 1023, as said below
- negative_slot: int32 [65536], P(('grp', 'own')), may hold values from 0 to 1023, as said below
Outputs:
- entity_grad: float32 [65536, 400], P('own', 'grp')
- rel_grad: float32 [1500, 400], replicated
Inputs may be any that keep to these rules, and one draw needn't show every extreme that they name: `owner_counts`: every device's counts lie in 1 to 16; in every draw some partition receives exactly 16 entities from every device, and some device has all its counts equal to 16. `unique_ids`: within one device's list, the entries of one partition are distinct; entries past the sum of the device's counts are unused. `head_slot`: every slot points below the sum of its device's counts, and every such slot of a device is named by some head, tail or negative slot of that device. `tail_slot`: as for head_slot. `negative_slot`: as for head_slot.
All inputs are finite; a program needn't handle non-finite values.
Results may differ from a plain program's by a relative error of at most 0.0039.
Values may be sent and summed in bfloat16 or wider, within the bound.
No kernel may reach another device: no remote copies, remote signals or barrier semaphores. Data moves between devices by JAX's collectives and lax.ppermute only.
A program may use at most 64 MiB of HBM per device.

v0:
```python
import jax
import jax.numpy as jnp
from jax import lax
from jax.sharding import PartitionSpec as P

ENT_DEV = 1024


def complex_mul(left, right):
    half_width = left.shape[-1] // 2
    left_re, left_im = (left[..., :half_width], left[..., half_width:])
    right_re, right_im = (right[..., :half_width], right[..., half_width:])
    return jnp.concatenate(
        [left_re * right_re - left_im * right_im, left_re * right_im + left_im * right_re], -1
    )


def conjugate(value):
    half_width = value.shape[-1] // 2
    return jnp.concatenate([value[..., :half_width], -value[..., half_width:]], -1)


def one_side(query_rows, positive_rows, negatives):
    positive = jnp.sum(query_rows.astype(jnp.float32) * positive_rows.astype(jnp.float32), -1)
    scores = jnp.dot(query_rows, negatives.T, preferred_element_type=jnp.float32)
    top_score = jnp.maximum(positive, jnp.max(scores, -1))
    pos_weight = jnp.exp(positive - top_score)
    neg_weight = jnp.exp(scores - top_score[:, None])
    denominator = pos_weight + jnp.sum(neg_weight, -1)
    first_term = pos_weight / denominator - 1.0
    probs_bf = (neg_weight / denominator[:, None]).astype(jnp.bfloat16)
    return (first_term, probs_bf)


def local_grads(heads, tails, relations, negatives):
    head_f = heads.astype(jnp.float32)
    tail_f = tails.astype(jnp.float32)
    query = complex_mul(head_f, relations).astype(jnp.bfloat16)
    mirror = complex_mul(conjugate(relations), tail_f).astype(jnp.bfloat16)
    first_tail, probs_tail = one_side(query, tails, negatives)
    first_head, probs_head = one_side(mirror, heads, negatives)
    d_query = first_tail[:, None] * tail_f + jnp.dot(
        probs_tail, negatives, preferred_element_type=jnp.float32
    )
    d_mirror = first_head[:, None] * head_f + jnp.dot(
        probs_head, negatives, preferred_element_type=jnp.float32
    )
    d_heads = first_head[:, None] * mirror.astype(jnp.float32) + complex_mul(
        conjugate(relations), d_query
    )
    d_tails = first_tail[:, None] * query.astype(jnp.float32) + complex_mul(relations, d_mirror)
    d_rel = complex_mul(conjugate(head_f), d_query) + complex_mul(tail_f, conjugate(d_mirror))
    d_group = jnp.dot(probs_tail.T, query, preferred_element_type=jnp.float32) + jnp.dot(
        probs_head.T, mirror, preferred_element_type=jnp.float32
    )
    return (d_heads, d_tails, d_rel, d_group)


def shards(
    head_rows,
    tail_rows,
    rel_ids,
    neg_rows,
    rel_table,
    owner_counts,
    unique_ids,
    head_slot,
    tail_slot,
    negative_slot,
):
    negatives = lax.all_gather(neg_rows, "grp", axis=0, tiled=True)
    relations = jnp.take(rel_table, rel_ids, axis=0)
    d_heads, d_tails, d_rel, d_group = local_grads(head_rows, tail_rows, relations, negatives)
    rel_terms = jax.ops.segment_sum(d_rel, rel_ids, num_segments=rel_table.shape[0])
    rel_grad = lax.psum(rel_terms, ("grp", "own"))
    own_negative = lax.psum_scatter(
        d_group.astype(jnp.bfloat16), "grp", scatter_dimension=0, tiled=True
    ).astype(jnp.float32)
    rows = jnp.concatenate([d_heads, d_tails, own_negative], 0)
    slot_entries = jnp.concatenate([head_slot, tail_slot, negative_slot], 0)
    list_width = unique_ids.shape[1]
    owners = lax.axis_size("own")
    capacity = list_width // owners
    depth = rows.shape[1]
    slot_sum = jax.ops.segment_sum(rows, slot_entries, num_segments=list_width)
    counts = owner_counts[0]
    starts = jnp.cumsum(counts) - counts
    lanes = jnp.arange(capacity, dtype=jnp.int32)
    valid = lanes[None, :] < counts[:, None]
    picks = jnp.minimum(starts[:, None] + lanes[None, :], list_width - 1)
    local_rows = jnp.where(valid, unique_ids[0][picks], ENT_DEV)
    sending = jnp.where(valid[:, :, None], slot_sum[picks], 0.0)
    received, rows_in = (
        lax.all_to_all(sending, "own", split_axis=0, concat_axis=0, tiled=True),
        lax.all_to_all(local_rows, "own", split_axis=0, concat_axis=0, tiled=True),
    )
    partition_sum = jax.ops.segment_sum(
        received.reshape(-1, depth), rows_in.reshape(-1), num_segments=ENT_DEV + 1
    )[:ENT_DEV]
    entity_grad = lax.psum_scatter(partition_sum, "grp", scatter_dimension=1, tiled=True)
    return (entity_grad, rel_grad)


def solution(mesh):
    in_specs = (
        P(("grp", "own"), None),
        P(("grp", "own"), None),
        P(("grp", "own")),
        P(("grp", "own"), None),
        P(),
        P(("grp", "own"), None),
        P(("grp", "own"), None),
        P(("grp", "own")),
        P(("grp", "own")),
        P(("grp", "own")),
    )
    out_specs = (P("own", "grp"), P())
    return jax.shard_map(shards, mesh=mesh, in_specs=in_specs, out_specs=out_specs, check_vma=False)
```

profile of v0, /device:TPU:1, one launch (start us, length us, event | category | flops | bytes accessed | tf_op | source)
XLA Modules:
  0.0 468.5 jit_solution(15285969375920469319)
XLA Ops:
  8.1 0.7 compare_select_fusion.1
  8.8 0.7 compare_and_fusion
  9.4 2.5 copy.25
  12.0 3.1 gather_fusion.1
  15.1 2.9 copy.26
  18.1 1.0 copy-done.12
  19.2 13.1 %all_gather.3 = bf16[1024,400]{0,1:T(8,128)(2,1)S(1)} all-gather(bf16[256,400]{0,1:T(8,128)(2,1)S(1)} %copy-done.19), channel_id=1, replica_groups=mesh['grp'=4,'own'=64] {'grp'}, dimensions={0}, use_global_device_ids=true | all-gather | bytes 1024000 | tf_op jit(solution)/shard_map/all_gather | solution.py:71
  32.5 0.4 subtract_convert_fusion.1
  32.9 1.1 fusion.18
  34.5 1.1 fusion.19
  35.6 0.9 fusion.1
  36.5 0.6 divide_convert_fusion.1
  37.2 0.9 fusion
  38.1 0.6 divide_convert_fusion
  38.7 0.8 fusion.15
  39.8 1.7 add_convert_fusion
  42.1 4.5 gather_fusion
  46.7 0.7 fusion.12
  47.4 13.9 %all-to-all-start = ((s32[64,1,16]{2,1,0:T(1,128)}), s32[64,1,16]{2,1,0:T(1,128)S(1)}, u32[]{:S(2)}, u32[]{:S(2)}) async-start(s32[64,1,16]{2,1,0:T(1,128)} %bitcast.3), calls=%async_computation | async-start | bytes 65536 | tf_op jit(solution)/shard_map/all_to_all | solution.py:95
  61.3 2.8 convolution_add_fusion.1
  64.2 1.3 multiply_subtract_fusion.1
  65.6 1.2 fusion.5
  66.8 0.9 copy-done.15
  67.8 0.9 convolution_add_fusion
  68.7 1.5 multiply_subtract_fusion
  70.2 1.2 fusion.7
  71.3 1.0 convert_element_type.37
  72.3 1.8 pad_maximum_fusion
  74.2 3.1 copy.27
  77.2 13.7 %scatter_custom_fusion = f32[1024,400]{1,0:T(8,128)S(1)} fusion(s32[1792]{0:T(1024)S(1)} %pad_add_fusion, f32[1792,400]{1,0:T(8,128)} %copy.27, f32[]{:T(128)} %constant.10.clone.1), kind=kCustom, calls=%fused_computation.30 | custom fusion | flops 716800 | bytes 1638912 | tf_op jit(solution)/shard_map/scatter-add | solution.py:85
  91.0 4.9 %gather_fusion.2 = f32[1024,400]{1,0:T(8,128)} fusion(f32[1024,400]{1,0:T(8,128)S(1)} %scatter_custom_fusion, s32[1024]{0:T(1024)S(1)} %broadcast_clamp_fusion), kind=kCustom, calls=%fused_computation.2 | custom fusion | bytes 3280896 | tf_op jit(solution)/shard_map/gather | solution.py:92
  95.8 3.1 broadcast_select_fusion
  99.0 11.3 %all-to-all-start.1 = ((f32[64,16,400]{2,1,0:T(8,128)}), f32[64,16,400]{2,1,0:T(8,128)}, u32[]{:S(2)}, u32[]{:S(2)}) async-start(f32[64,16,400]{2,1,0:T(8,128)} %broadcast_select_fusion), calls=%async_computation.2 | async-start | bytes 4194304 | tf_op jit(solution)/shard_map/all_to_all | solution.py:94
  110.6 1.3 maximum_add_fusion
  111.8 0.5 copy.28
  112.3 8.5 %scatter_custom_fusion.2 = f32[1500,400]{1,0:T(8,128)} fusion(s32[768]{0:T(1024)} %param.12, f32[768,400]{1,0:T(8,128)S(1)} %copy.28, f32[]{:T(128)} %constant.10.clone.1), kind=kCustom, calls=%fused_computation.14 | custom fusion | flops 307200 | bytes 2400512 | tf_op jit(solution)/shard_map/scatter-add | solution.py:74
  120.9 0.5 broadcast.129
  121.4 0.7 reduce.4
  122.2 42.7 %all-to-all-done.1 = f32[64,16,400]{2,1,0:T(8,128)} async-done(((f32[64,16,400]{2,1,0:T(8,128)}), f32[64,16,400]{2,1,0:T(8,128)}, u32[]{:S(2)}, u32[]{:S(2)}) %all-to-all-start.1) | async-done | bytes 1638432 | tf_op jit(solution)/shard_map/all_to_all | solution.py:94
  164.9 7.8 %scatter_custom_fusion.1 = f32[1025,400]{1,0:T(8,128)S(1)} fusion(s32[1024]{0:T(1024)S(1)} %reshape.235, f32[1024,400]{1,0:T(8,128)} %bitcast.5, f32[]{:T(128)} %constant.10.clone.1), kind=kCustom, calls=%fused_computation.27 | custom fusion | flops 409600 | bytes 1640512 | tf_op jit(solution)/shard_map/scatter-add | solution.py:97
  172.7 1.6 slice.74
  174.3 0.6 copy-done.24
  174.9 0.6 dynamic-slice
  176.2 216.3 %all-reduce.4.cloned.1.call-done = f32[1500,400]{1,0:T(8,128)} async-done(((f32[1500,400]{1,0:T(8,128)}), f32[1500,400]{1,0:T(8,128)}) %all-reduce.4.cloned.1.call-update) | async-done | bytes 2400016 | tf_op jit(solution)/shard_map/psum | solution.py:75
  392.5 3.3 copy.30
  395.8 62.8 %all-reduce.6.cloned.1.call-done = f32[1024,400]{1,0:T(8,128)} async-done(((f32[1024,400]{1,0:T(8,128)}), f32[1024,400]{1,0:T(8,128)}) %all-reduce.6.cloned.1.call-update) | async-done | bytes 1638416
  458.6 1.4 constant_dynamic-slice_fusion
  460.1 1.0 copy.29
  (75 shorter events, 2.4 us)
Async XLA Ops:
  8.0 34.1 %copy-start = (s32[1,1024]{1,0:T(1,128)S(1)}, s32[1,1024]{1,0:T(1,128)}, u32[]{:S(2)}) copy-start(s32[1,1024]{1,0:T(1,128)} %param.16) | copy-start | bytes 12292
  8.0 63.3 %reduce-scatter.3.cloned.1.call-start = ((), (), s32[]{:S(2)}) async-start(), calls=%async_computation.3 | async-start | bytes 1024000 | tf_op jit(solution)/shard_map/reduce_scatter | solution.py:76
  15.1 2.9 copy-start.10
  18.0 1.1 copy-start.12
  18.0 1.2 copy-start.19
  19.1 13.3 %copy-start.4 = (f32[768,400]{0,1:T(8,128)S(1)}, f32[768,400]{0,1:T(8,128)}, u32[]{:S(2)}) copy-start(f32[768,400]{0,1:T(8,128)} %copy.26) | copy-start | bytes 3686404
  19.2 13.3 %copy-start.2 = (f32[768,400]{0,1:T(8,128)}, f32[768,400]{0,1:T(8,128)S(1)}, u32[]{:S(2)}) copy-start(f32[768,400]{0,1:T(8,128)S(1)} %convert_element_type.32) | copy-start | bytes 3686404
  32.4 2.1 copy-start.17
  32.9 6.6 %copy-start.5 = (bf16[768,200]{0,1:T(8,128)(2,1)}, bf16[768,200]{0,1:T(8,128)(2,1)S(1)}, u32[]{:S(2)}) copy-start(bf16[768,200]{0,1:T(8,128)(2,1)S(1)} %get-tuple-element.15) | copy-start | bytes 921604
  32.9 1.2 copy-start.11
  37.1 1.5 copy-start.16
  38.7 1.1 copy-start.14
  39.8 1.8 copy-start.20
  47.4 51.6 %all-to-all-start = ((s32[64,1,16]{2,1,0:T(1,128)}), s32[64,1,16]{2,1,0:T(1,128)S(1)}, u32[]{:S(2)}, u32[]{:S(2)}) async-start(s32[64,1,16]{2,1,0:T(1,128)} %bitcast.3), calls=%async_computation | async-start | bytes 65536 | tf_op jit(solution)/shard_map/all_to_all | solution.py:95
  61.3 2.9 copy-start.21
  61.3 2.9 copy-start.22
  61.3 2.9 copy-start.23
  61.3 2.9 copy-start.3
  64.2 1.4 copy-start.6
  65.6 1.2 copy-start.13
  65.6 2.1 copy-start.15
  65.6 2.3 copy-start.18
  99.0 11.6 %copy-start.7 = (f32[768,200]{0,1:T(8,128)S(1)}, f32[768,200]{0,1:T(8,128)}, u32[]{:S(2)}) copy-start(f32[768,200]{0,1:T(8,128)} %get-tuple-element.8) | copy-start | bytes 1843204
  99.0 11.6 %copy-start.8 = (f32[768,200]{0,1:T(8,128)S(1)}, f32[768,200]{0,1:T(8,128)}, u32[]{:S(2)}) copy-start(f32[768,200]{0,1:T(8,128)} %get-tuple-element.9) | copy-start | bytes 1843204
  99.0 11.6 %copy-start.9 = (f32[768,200]{0,1:T(8,128)S(1)}, f32[768,200]{0,1:T(8,128)}, u32[]{:S(2)}) copy-start(f32[768,200]{0,1:T(8,128)} %get-tuple-element.6) | copy-start | bytes 1843204
  99.0 65.9 %all-to-all-start.1 = ((f32[64,16,400]{2,1,0:T(8,128)}), f32[64,16,400]{2,1,0:T(8,128)}, u32[]{:S(2)}, u32[]{:S(2)}) async-start(f32[64,16,400]{2,1,0:T(8,128)} %broadcast_select_fusion), calls=%async_computation.2 | async-start | bytes 4194304 | tf_op jit(solution)/shard_map/all_to_all | solution.py:94
  110.3 282.2 %all-reduce.4.cloned.1.call-start = ((), (), s32[]{:S(2)}) async-start(), calls=%async_computation.4 | async-start | bytes 6160384 | tf_op jit(solution)/shard_map/psum | solution.py:75
  120.9 337.8 %all-reduce.6.cloned.1.call-start = ((), (), s32[]{:S(2)}) async-start(), calls=%async_computation.5 | async-start | bytes 4194304
  174.2 0.7 copy-start.24
  392.5 68.5 %copy-start.1 = (s32[1,1024]{1,0:T(1,128)S(1)}, s32[1,1024]{1,0:T(1,128)}, u32[]{:S(2)}) copy-start(s32[1,1024]{1,0:T(1,128)} %param.16) | copy-start | bytes 12292
Sparse Core Ops, SparseCore 0:
  41.7 28.6 reduce-scatter.2
Sparse Core Ops, SparseCore 1:
  120.9 271.5 all-reduce.3
  394.8 63.7 all-reduce.5
where the time goes:
time: 469 us; the launch traced here: 468 us
  waiting for transfers between devices  322 us (69%)
  other arithmetic  49.7 us (11%)
  local copies, waits for them, and re-layouts  33.4 us (7%)
  starting transfers between devices  25.5 us (5%)
  between operations  16.6 us (4%)
  blocking collectives  13.1 us (3%)
  matrix products  8.38 us (2%)
    psum x1, waiting for transfers between devices, shards(): rel_grad = lax.psum(rel_terms, ('grp', 'own'))  216 us
    unnamed x4, waiting for transfers between devices  62.8 us
    all_to_all x1, waiting for transfers between devices, shards(): lax.all_to_all(sending, 'own', split_axis=0, concat_axis=0, tiled=True)  42.7 us
    all_to_all x1, starting transfers between devices, shards(): lax.all_to_all(local_rows, 'own', split_axis=0, concat_axis=0, tiled=True)  13.9 us
    scatter-add x1, other arithmetic, shards(): slot_sum = jax.ops.segment_sum(rows, slot_entries, num_segments=list_width)  13.7 us
    all_gather x1, blocking collectives, shards(): negatives = lax.all_gather(neg_rows, 'grp', axis=0, tiled=True)  13.1 us
    unnamed x55, local copies, waits for them, and re-layouts  12 us
    all_to_all x1, starting transfers between devices, shards(): lax.all_to_all(sending, 'own', split_axis=0, concat_axis=0, tiled=True)  11.3 us
  transfers between devices with their start and end apart: 5, of which 3 were waited for; matrix products, arithmetic and copies ran while one was open for 14% of the time, Pallas kernels for 0%

commit v1 on v0

v1 whole, which is shorter than its diff:
```python
import jax
import jax.numpy as jnp
from jax import lax
from jax.experimental import pallas as pl
from jax.experimental.pallas import tpu as pltpu
from jax.sharding import Mesh
from jax.sharding import PartitionSpec as P

D = 400
RELS = 1500
E_DEV = 768
ENT_DEV = 1024
NEG_DEV = 256
CAP = 16
NEG = 1024
U_CAP = 1024
N_GRP = 4
N_OWN = 64
N_YZ = 32
LANES = 128
USED = 100
W = N_GRP * LANES
HALF = W // 2
REL_PAD = 1536
REL_HALF = REL_PAD // 2
BLK = 256
ROWS = 2 * E_DEV
ALL = ("x", "y", "z", "c")
F32 = jnp.float32
BF16 = jnp.bfloat16
I32 = jnp.int32
VMEM_BYTES = 48 * 1024 * 1024


def dot(a, b):
    return lax.dot_general(a, b, (((1,), (0,)), ((), ())), preferred_element_type=F32)


def dot_nt(a, b):
    return lax.dot_general(a, b, (((1,), (1,)), ((), ())), preferred_element_type=F32)


def split2(value):
    high = value.astype(BF16)
    return high, (value - high.astype(F32)).astype(BF16)


def spread_t():
    row = lax.broadcasted_iota(I32, (W, D), 0)
    col = lax.broadcasted_iota(I32, (W, D), 1)
    lane = row & (LANES - 1)
    hit = (lane < USED) & (col == (row >> 7) * USED + lane)
    return jnp.where(hit, 1.0, 0.0).astype(BF16)


def spread():
    row = lax.broadcasted_iota(I32, (D, W), 0)
    col = lax.broadcasted_iota(I32, (D, W), 1)
    lane = col & (LANES - 1)
    hit = (lane < USED) & (row == (col >> 7) * USED + lane)
    return jnp.where(hit, 1.0, 0.0).astype(BF16)


def one_hot(ids_row, rows):
    spot = lax.broadcasted_iota(I32, (rows, ids_row.shape[1]), 0)
    return jnp.where(spot == ids_row, 1.0, 0.0).astype(BF16)


def params():
    return pltpu.CompilerParams(vmem_limit_bytes=VMEM_BYTES)


def full(shape):
    return pl.BlockSpec(shape, lambda i: (0,) * len(shape))


def edge_cols(rows):
    return pl.BlockSpec((rows, BLK), lambda i: (0, i))


def prep_kernel(head_ref, tail_ref, rid_ref, table_ref, counts_ref, uid_ref, slots_ref,
                h_ref, t_ref, r_ref, q_ref, m_ref, pos_ref, target_ref, code_ref,
                pad_ref, high_ref, mid_ref, low_ref):
    put = spread_t()

    @pl.when(pl.program_id(0) == 0)
    def _():
        pad_ref[pl.ds(REL_PAD - 40, 40), :] = jnp.zeros((40, D), F32)
        pad_ref[pl.ds(0, RELS), :] = table_ref[...]
        table = pad_ref[...]
        high = table.astype(BF16)
        rest = table - high.astype(F32)
        mid = rest.astype(BF16)
        low = (rest - mid.astype(F32)).astype(BF16)
        high_ref[...] = dot_nt(put, high).astype(BF16)
        mid_ref[...] = dot_nt(put, mid).astype(BF16)
        low_ref[...] = dot_nt(put, low).astype(BF16)

        counts = jnp.broadcast_to(counts_ref[...], (N_OWN, N_OWN)).astype(F32)
        part = lax.broadcasted_iota(I32, (N_OWN, N_OWN), 0)
        other = lax.broadcasted_iota(I32, (N_OWN, N_OWN), 1)
        ends = jnp.sum(jnp.where(other <= part, counts, 0.0), 1, keepdims=True).astype(I32)
        own = jnp.sum(jnp.where(other == part, counts, 0.0), 1, keepdims=True).astype(I32)
        slots = slots_ref[...]
        target_ref[...] = slots + jnp.sum(jnp.where(slots >= ends, CAP - own, 0), 0, keepdims=True)

        place = lax.broadcasted_iota(I32, (U_CAP, N_OWN), 0)
        lane = (place & (CAP - 1)).astype(F32)
        owner = lax.broadcasted_iota(I32, (U_CAP, N_OWN), 1)
        counts_all = jnp.broadcast_to(counts_ref[...], (U_CAP, N_OWN)).astype(F32)
        start = jnp.sum(jnp.where(owner < (place >> 4), counts_all, 0.0), 1, keepdims=True)
        count = jnp.sum(jnp.where(owner == (place >> 4), counts_all, 0.0), 1, keepdims=True)
        spot = (start + lane[:, :1]).astype(I32)
        column = lax.broadcasted_iota(I32, (U_CAP, U_CAP), 1)
        uid = uid_ref[...].astype(F32)
        picked = jnp.sum(jnp.where(column == spot, uid, 0.0), 1, keepdims=True)
        picked = jnp.where(lane[:, :1] < count, picked, float(ENT_DEV)).astype(I32)
        lanes = lax.broadcasted_iota(I32, (U_CAP, LANES), 1)
        code = jnp.where(lanes == USED, picked >> 5, jnp.where(lanes == USED + 1, picked & 31, 0))
        code_ref[...] = code.astype(F32)

    hit = one_hot(rid_ref[...], REL_PAD)
    rel = dot(high_ref[...], hit) + dot(mid_ref[...], hit) + dot(low_ref[...], hit)
    r_ref[...] = rel
    head = dot_nt(put, head_ref[...])
    tail = dot_nt(put, tail_ref[...])
    h_ref[...] = head.astype(BF16)
    t_ref[...] = tail.astype(BF16)
    hr, hi, tr, ti, rr, ri = head[:HALF], head[HALF:], tail[:HALF], tail[HALF:], rel[:HALF], rel[HALF:]
    qr = (hr * rr - hi * ri).astype(BF16)
    qi = (hr * ri + hi * rr).astype(BF16)
    mr = (rr * tr + ri * ti).astype(BF16)
    mi = (rr * ti - ri * tr).astype(BF16)
    q_ref[pl.ds(0, HALF), :] = qr
    q_ref[pl.ds(HALF, HALF), :] = qi
    m_ref[pl.ds(0, HALF), :] = mr
    m_ref[pl.ds(HALF, HALF), :] = mi
    pos_t = jnp.sum(qr.astype(F32) * tr + qi.astype(F32) * ti, 0, keepdims=True)
    pos_h = jnp.sum(mr.astype(F32) * hr + mi.astype(F32) * hi, 0, keepdims=True)
    side = lax.broadcasted_iota(I32, (8, BLK), 0)
    pos_ref[...] = jnp.where(side == 0, pos_t, pos_h)


def prep(heads, tails, rid, table, counts, uid, slots):
    cols = lambda dt: jax.ShapeDtypeStruct((W, E_DEV), dt)
    return pl.pallas_call(
        prep_kernel,
        name="prep",
        grid=(E_DEV // BLK,),
        in_specs=[
            pl.BlockSpec((BLK, D), lambda i: (i, 0)),
            pl.BlockSpec((BLK, D), lambda i: (i, 0)),
            edge_cols(1),
            full((RELS, D)),
            full((1, N_OWN)),
            full((1, U_CAP)),
            full((1, ROWS + NEG_DEV)),
        ],
        out_specs=[edge_cols(W)] * 5 + [edge_cols(8), full((1, ROWS + NEG_DEV)), full((U_CAP, LANES))],
        out_shape=[
            cols(BF16), cols(BF16), cols(F32), cols(BF16), cols(BF16),
            jax.ShapeDtypeStruct((8, E_DEV), F32),
            jax.ShapeDtypeStruct((1, ROWS + NEG_DEV), I32),
            jax.ShapeDtypeStruct((U_CAP, LANES), F32),
        ],
        scratch_shapes=[pltpu.VMEM((REL_PAD, D), F32)] + [pltpu.VMEM((W, REL_PAD), BF16)] * 3,
        compiler_params=params(),
        cost_estimate=pl.CostEstimate(flops=8 * 10**9, bytes_accessed=8 * 10**6, transcendentals=0),
    )(heads, tails, rid, table, counts, uid, slots)


def score_kernel(n0_ref, n1_ref, n2_ref, n3_ref, q_ref, m_ref, pos_ref,
                 pt_ref, ph_ref, first_ref, own_ref, g1_ref, g2_ref, g3_ref, neg_ref, acc_ref):
    step = pl.program_id(0)

    @pl.when(step == 0)
    def _():
        put = spread()
        for k, ref in enumerate((n0_ref, n1_ref, n2_ref, n3_ref)):
            neg_ref[pl.ds(k * NEG_DEV, NEG_DEV), :] = dot(ref[...], put).astype(BF16)

    neg = neg_ref[...]
    firsts = []
    terms = []
    for side, (query_ref, prob_ref) in enumerate(((q_ref, pt_ref), (m_ref, ph_ref))):
        query = query_ref[...]
        positive = pos_ref[pl.ds(side, 1), :]
        scores = dot(neg, query)
        top = jnp.maximum(positive, jnp.max(scores, 0, keepdims=True))
        weight = jnp.exp(scores - top)
        pos_weight = jnp.exp(positive - top)
        total = pos_weight + jnp.sum(weight, 0, keepdims=True)
        firsts.append(pos_weight / total - 1.0)
        probs = (weight * (1.0 / total)).astype(BF16)
        prob_ref[...] = probs
        terms.append(dot_nt(probs, query))
    row = lax.broadcasted_iota(I32, (8, BLK), 0)
    first_ref[...] = jnp.where(row == 0, firsts[0], firsts[1])
    term = terms[0] + terms[1]

    @pl.when(step == 0)
    def _():
        acc_ref[...] = term

    @pl.when(step > 0)
    def _():
        acc_ref[...] += term

    @pl.when(step == E_DEV // BLK - 1)
    def _():
        own_ref[...] = acc_ref[pl.ds(0, NEG_DEV), :]
        for k, ref in enumerate((g1_ref, g2_ref, g3_ref)):
            ref[...] = acc_ref[pl.ds((k + 1) * NEG_DEV, NEG_DEV), :].astype(BF16)


def score(negs, q, m, pos):
    part = jax.ShapeDtypeStruct((NEG_DEV, W), BF16)
    return pl.pallas_call(
        score_kernel,
        name="score",
        grid=(E_DEV // BLK,),
        in_specs=[full((NEG_DEV, D))] * 4 + [edge_cols(W), edge_cols(W), edge_cols(8)],
        out_specs=[edge_cols(NEG), edge_cols(NEG), edge_cols(8)] + [full((NEG_DEV, W))] * 4,
        out_shape=[
            jax.ShapeDtypeStruct((NEG, E_DEV), BF16),
            jax.ShapeDtypeStruct((NEG, E_DEV), BF16),
            jax.ShapeDtypeStruct((8, E_DEV), F32),
            jax.ShapeDtypeStruct((NEG_DEV, W), F32),
            part, part, part,
        ],
        scratch_shapes=[pltpu.VMEM((NEG, W), BF16), pltpu.VMEM((NEG, W), F32)],
        compiler_params=params(),
        cost_estimate=pl.CostEstimate(flops=5 * 10**9, bytes_accessed=8 * 10**6, transcendentals=2 * 10**6),
    )(*negs, q, m, pos)


def edge_kernel(core_ref, n0_ref, n1_ref, n2_ref, n3_ref, pt_ref, ph_ref, first_ref,
                h_ref, t_ref, r_ref, q_ref, m_ref, rid_ref,
                dhh_ref, dhl_ref, dth_ref, dtl_ref, mine_ref, other_ref, neg_ref):
    step = pl.program_id(0)

    @pl.when(step == 0)
    def _():
        put = spread_t()
        for k, ref in enumerate((n0_ref, n1_ref, n2_ref, n3_ref)):
            neg_ref[:, pl.ds(k * NEG_DEV, NEG_DEV)] = dot_nt(put, ref[...]).astype(BF16)

    neg = neg_ref[...]
    first_t = first_ref[pl.ds(0, 1), :]
    first_h = first_ref[pl.ds(1, 1), :]
    head = h_ref[...].astype(F32)
    tail = t_ref[...].astype(F32)
    rel = r_ref[...]
    query = q_ref[...].astype(F32)
    mirror = m_ref[...].astype(F32)
    dq = first_t * tail + dot(neg, pt_ref[...])
    dm = first_h * head + dot(neg, ph_ref[...])
    hr, hi, tr, ti, rr, ri = head[:HALF], head[HALF:], tail[:HALF], tail[HALF:], rel[:HALF], rel[HALF:]
    qr, qi, mr, mi = dq[:HALF], dq[HALF:], dm[:HALF], dm[HALF:]
    pieces = (
        (dhh_ref, dhl_ref, 0, first_h * mirror[:HALF] + (rr * qr + ri * qi)),
        (dhh_ref, dhl_ref, HALF, first_h * mirror[HALF:] + (rr * qi - ri * qr)),
        (dth_ref, dtl_ref, 0, first_t * query[:HALF] + (rr * mr - ri * mi)),
        (dth_ref, dtl_ref, HALF, first_t * query[HALF:] + (rr * mi + ri * mr)),
    )
    for high_ref, low_ref, at, value in pieces:
        high, low = split2(value)
        high_ref[pl.ds(at, HALF), :] = high
        low_ref[pl.ds(at, HALF), :] = low
    drr = (hr * qr + hi * qi) + (tr * mr + ti * mi)
    dri = (hr * qi - hi * qr) + (ti * mr - tr * mi)
    ids = rid_ref[...] - REL_HALF * core_ref[0]
    ids = jnp.where(ids < 0, ids + REL_PAD, ids)
    hit = one_hot(ids, REL_PAD)
    for at, value in ((0, drr), (HALF, dri)):
        high, low = split2(value)
        term = dot_nt(hit, high) + dot_nt(hit, low)
        for ref, row in ((mine_ref, 0), (other_ref, REL_HALF)):
            @pl.when(step == 0)
            def _(ref=ref, row=row):
                ref[:, pl.ds(at, HALF)] = term[row:row + REL_HALF]

            @pl.when(step > 0)
            def _(ref=ref, row=row):
                ref[:, pl.ds(at, HALF)] += term[row:row + REL_HALF]


def edge(core, negs, pt, ph, first, h, t, r, q, m, rid):
    cols = jax.ShapeDtypeStruct((W, E_DEV), BF16)
    half = jax.ShapeDtypeStruct((REL_HALF, W), F32)
    return pl.pallas_call(
        edge_kernel,
        name="edge",
        grid=(E_DEV // BLK,),
        in_specs=[pl.BlockSpec(memory_space=pltpu.SMEM)] + [full((NEG_DEV, D))] * 4
        + [edge_cols(NEG), edge_cols(NEG), edge_cols(8)] + [edge_cols(W)] * 5 + [edge_cols(1)],
        out_specs=[edge_cols(W)] * 4 + [full((REL_HALF, W))] * 2,
        out_shape=[cols] * 4 + [half] * 2,
        scratch_shapes=[pltpu.VMEM((W, NEG), BF16)],
        compiler_params=params(),
        cost_estimate=pl.CostEstimate(flops=5 * 10**9, bytes_accessed=12 * 10**6, transcendentals=0),
    )(core, *negs, pt, ph, first, h, t, r, q, m, rid)


def slot_kernel(target_h_ref, target_t_ref, dhh_ref, dhl_ref, dth_ref, dtl_ref, out_ref):
    hit_h = one_hot(target_h_ref[...], U_CAP)
    hit_t = one_hot(target_t_ref[...], U_CAP)
    term = (dot_nt(hit_h, dhh_ref[...]) + dot_nt(hit_h, dhl_ref[...])) + (
        dot_nt(hit_t, dth_ref[...]) + dot_nt(hit_t, dtl_ref[...]))

    @pl.when(pl.program_id(0) == 0)
    def _():
        out_ref[...] = term

    @pl.when(pl.program_id(0) > 0)
    def _():
        out_ref[...] += term


def slot(target, dhh, dhl, dth, dtl):
    return pl.pallas_call(
        slot_kernel,
        name="slot",
        grid=(E_DEV // BLK,),
        in_specs=[edge_cols(1), pl.BlockSpec((1, BLK), lambda i: (0, E_DEV // BLK + i))] + [edge_cols(W)] * 4,
        out_specs=full((U_CAP, W)),
        out_shape=jax.ShapeDtypeStruct((U_CAP, W), F32),
        compiler_params=params(),
        cost_estimate=pl.CostEstimate(flops=4 * 10**9, bytes_accessed=5 * 10**6, transcendentals=0),
    )(target, target, dhh, dhl, dth, dtl)


def pack_kernel(target_ref, own_ref, g1_ref, g2_ref, g3_ref, part_ref, code_ref, out_ref):
    rows = own_ref[...] + g1_ref[...].astype(F32) + g2_ref[...].astype(F32) + g3_ref[...].astype(F32)
    high, low = split2(rows)
    hit = one_hot(target_ref[...], U_CAP)
    total = part_ref[...] + (dot(hit, high) + dot(hit, low))
    code = code_ref[...]
    for k in range(N_GRP):
        out_ref[k] = (total[:, k * LANES:(k + 1) * LANES] + code).astype(BF16)


def pack(target, own, g1, g2, g3, part, code):
    return pl.pallas_call(
        pack_kernel,
        name="pack",
        grid=(1,),
        in_specs=[pl.BlockSpec((1, NEG_DEV), lambda i: (0, ROWS // NEG_DEV))] + [full((NEG_DEV, W))] * 4
        + [full((U_CAP, W)), full((U_CAP, LANES))],
        out_specs=full((N_GRP, U_CAP, LANES)),
        out_shape=jax.ShapeDtypeStruct((N_GRP, U_CAP, LANES), BF16),
        compiler_params=params(),
        cost_estimate=pl.CostEstimate(flops=10**9, bytes_accessed=5 * 10**6, transcendentals=0),
    )(target, own, g1, g2, g3, part, code)


def partition_kernel(rows_ref, out_ref, acc_ref):
    step = pl.program_id(0)
    rows = rows_ref[...]
    lane = lax.broadcasted_iota(I32, (8, LANES), 1)
    weight = jnp.where(lane == USED, 32.0, jnp.where(lane == USED + 1, 1.0, 0.0)).astype(BF16)
    ids = dot_nt(weight, rows)[:1].astype(I32)
    term = dot(one_hot(ids, ENT_DEV), rows)

    @pl.when(step == 0)
    def _():
        acc_ref[...] = term

    @pl.when(step > 0)
    def _():
        acc_ref[...] += term

    @pl.when(step == pl.num_programs(0) - 1)
    def _():
        out_ref[...] = acc_ref[:, :USED]


def partition(rows):
    block = 1024
    return pl.pallas_call(
        partition_kernel,
        name="partition",
        grid=(rows.shape[0] // block,),
        in_specs=[pl.BlockSpec((block, LANES), lambda i: (i, 0))],
        out_specs=full((ENT_DEV, USED)),
        out_shape=jax.ShapeDtypeStruct((ENT_DEV, USED), F32),
        scratch_shapes=[pltpu.VMEM((ENT_DEV, LANES), F32)],
        compiler_params=params(),
        cost_estimate=pl.CostEstimate(flops=2 * 10**9, bytes_accessed=2 * 10**6, transcendentals=0),
    )(rows)


def rel_x_kernel(grp_ref, mine_ref, other_ref, own_ref, o1_ref, o2_ref, o3_ref):
    for k, ref in enumerate((own_ref, o1_ref, o2_ref, o3_ref)):
        at = pl.multiple_of(((grp_ref[0] + k) & (N_GRP - 1)) * LANES, LANES)
        total = mine_ref[:, pl.ds(at, LANES)] + other_ref[:, pl.ds(at, LANES)]
        ref[...] = total.astype(ref.dtype)


def rel_x(grp, mine, other):
    part = jax.ShapeDtypeStruct((REL_HALF, LANES), BF16)
    return pl.pallas_call(
        rel_x_kernel,
        name="rel_x",
        grid=(1,),
        in_specs=[pl.BlockSpec(memory_space=pltpu.SMEM)] + [full((REL_HALF, W))] * 2,
        out_specs=[full((REL_HALF, LANES))] * 4,
        out_shape=[jax.ShapeDtypeStruct((REL_HALF, LANES), F32), part, part, part],
        compiler_params=params(),
        cost_estimate=pl.CostEstimate(flops=10**6, bytes_accessed=4 * 10**6, transcendentals=0),
    )(grp, mine, other)


def rel_yz_kernel(own_ref, i1_ref, i2_ref, i3_ref, out_ref):
    out_ref[...] = own_ref[...] + i1_ref[...].astype(F32) + i2_ref[...].astype(F32) + i3_ref[...].astype(F32)


def rel_yz(own, i1, i2, i3):
    return pl.pallas_call(
        rel_yz_kernel,
        name="rel_yz",
        grid=(1,),
        in_specs=[full((REL_HALF, LANES))] * 4,
        out_specs=full((REL_HALF, LANES)),
        out_shape=jax.ShapeDtypeStruct((REL_HALF, LANES), F32),
        compiler_params=params(),
        cost_estimate=pl.CostEstimate(flops=10**6, bytes_accessed=2 * 10**6, transcendentals=0),
    )(own, i1, i2, i3)


def rel_sum_kernel(in_ref, out_ref):
    total = jnp.sum(in_ref[...], 0).astype(BF16)
    out_ref[...] = jnp.broadcast_to(total[None], out_ref.shape)


def rel_sum(parts):
    return pl.pallas_call(
        rel_sum_kernel,
        name="rel_sum",
        grid=(1,),
        in_specs=[full(parts.shape)],
        out_specs=full(parts.shape),
        out_shape=jax.ShapeDtypeStruct(parts.shape, BF16),
        compiler_params=params(),
        cost_estimate=pl.CostEstimate(flops=10**6, bytes_accessed=10**6, transcendentals=0),
    )(parts)


def table_kernel(place_ref, *refs):
    out_ref = refs[-1]
    core = place_ref[0]
    grp = place_ref[1]
    row = lax.broadcasted_iota(I32, (LANES, D), 0)
    col = lax.broadcasted_iota(I32, (LANES, D), 1)
    for half in range(2):
        total = jnp.zeros((REL_HALF, D), F32)
        for k in range(N_GRP):
            at = ((grp - k) & (N_GRP - 1)) * USED
            put = jnp.where((row < USED) & (col == row + at), 1.0, 0.0).astype(BF16)
            total = total + dot(refs[half * N_GRP + k][...], put)

        @pl.when(core == half)
        def _():
            out_ref[pl.ds(0, REL_HALF), :] = total

        @pl.when(core != half)
        def _():
            out_ref[pl.ds(REL_HALF, RELS - REL_HALF), :] = total[:RELS - REL_HALF]


def table(place, blocks):
    return pl.pallas_call(
        table_kernel,
        name="table",
        grid=(1,),
        in_specs=[pl.BlockSpec(memory_space=pltpu.SMEM)] + [full((REL_HALF, LANES))] * 8,
        out_specs=full((RELS, D)),
        out_shape=jax.ShapeDtypeStruct((RELS, D), F32),
        compiler_params=params(),
        cost_estimate=pl.CostEstimate(flops=10**9, bytes_accessed=4 * 10**6, transcendentals=0),
    )(place, *blocks)


def ring(value, k):
    return lax.ppermute(value, "x", [(i, (i + k) % N_GRP) for i in range(N_GRP)])


def pair(value):
    return lax.ppermute(value, "c", [(0, 1), (1, 0)])


def shards(head_rows, tail_rows, rel_ids, neg_rows, rel_table, owner_counts, unique_ids, head_slot, tail_slot, negative_slot):
    core = lax.axis_index("c").astype(I32)
    grp = lax.axis_index("x").astype(I32)
    negs = [neg_rows] + [ring(neg_rows, k) for k in (1, 2, 3)]
    rid = rel_ids.reshape(1, -1)
    slots = jnp.concatenate([head_slot, tail_slot, negative_slot]).reshape(1, -1)
    h, t, r, q, m, pos, target, code = prep(head_rows, tail_rows, rid, rel_table, owner_counts, unique_ids, slots)
    pt, ph, first, own, g1, g2, g3 = score(negs, q, m, pos)
    back = [ring(g, N_GRP - k) for k, g in ((1, g1), (2, g2), (3, g3))]
    dhh, dhl, dth, dtl, mine, other = edge(core.reshape(1), negs, pt, ph, first, h, t, r, q, m, rid)
    other = pair(other)
    part = slot(target, dhh, dhl, dth, dtl)
    rel_own, o1, o2, o3 = rel_x(grp.reshape(1), mine, other)
    arrived = [ring(o, k) for k, o in ((1, o1), (2, o2), (3, o3))]
    packed = pack(target, own, *back, part, code)
    received = lax.all_to_all(packed.reshape(N_GRP * N_OWN, CAP, LANES), ALL, 0, 0, tiled=True)
    chip = rel_yz(rel_own, *arrived).reshape(N_YZ, REL_HALF // N_YZ, LANES)
    chip = rel_sum(lax.all_to_all(chip, ("y", "z"), 0, 0, tiled=True))
    chip = lax.all_to_all(chip, ("y", "z"), 0, 0, tiled=True).reshape(REL_HALF, LANES)
    quarter = [chip] + [ring(chip, k) for k in (1, 2, 3)]
    blocks = quarter + [pair(value) for value in quarter]
    rel_grad = table(jnp.stack([core, grp]), blocks)
    entity_grad = partition(received.reshape(-1, LANES))
    return entity_grad, rel_grad


def solution(mesh):
    split = Mesh(mesh.devices.reshape(N_GRP, 4, 8, 2), ALL)
    edges = P(ALL)
    rows = P(ALL, None)
    in_specs = (rows, rows, edges, rows, P(), rows, rows, edges, edges, edges)
    out_specs = (P(("y", "z", "c"), "x"), P())
    return jax.shard_map(shards, mesh=split, in_specs=in_specs, out_specs=out_specs, check_vma=False)
```

time: 469 us -> 190 us (0.41)
  waiting for transfers between devices: 322 us -> 38.9 us
  Pallas kernels: 0 us -> 50.1 us
  other arithmetic: 49.7 us -> 0.08 us
  starting transfers between devices: 25.5 us -> 60.6 us
  between operations: 16.6 us -> 0.91 us
  blocking collectives: 13.1 us -> 0 us
  matrix products: 8.38 us -> 0 us
  local copies, waits for them, and re-layouts: 33.4 us -> 38.7 us
    psum x1 -> x0, waiting for transfers between devices: 216 us -> none  [shards(): rel_grad = lax.psum(rel_terms, ('grp', 'own'))]
    unnamed x4 -> x0, waiting for transfers between devices: 62.8 us -> none
    pallas_call x0 -> x10, Pallas kernels: none -> 50.1 us  [the longest x1 14.7 us: edge(): pl.pallas_call(edge_kernel, name='edge', grid=(E_DEV // BLK,), in_specs=[...]
    scatter-add x3 -> x0, other arithmetic: 30.1 us -> none  [the longest x1 13.7 us: shards(): slot_sum = jax.ops.segment_sum(rows, slot_entries, num_segments=list_width)]
    unnamed x55 -> x90, local copies, waits for them, and re-layouts: 12 us -> 38.7 us
    ppermute x0 -> x17, starting transfers between devices: none -> 26.5 us  [the longest x12 18.6 us: ring(): lax.ppermute(value, 'x', [(i, (i + k) % N_GRP) for i in range(N_GRP)])]
    all_to_all x2 -> x3, waiting for transfers between devices: 42.7 us -> 19.2 us  [the longest x1 12.4 us: shards(): lax.all_to_all(packed.reshape(N_GRP * N_OWN, CAP, LANES), ALL, 0, 0, tile...]
    ppermute x0 -> x17, waiting for transfers between devices: none -> 19.7 us  [the longest x12 16.4 us: ring(): lax.ppermute(value, 'x', [(i, (i + k) % N_GRP) for i in range(N_GRP)])]
  transfers between devices with their start and end apart: 5 -> 20, of which waited for: 3 -> 8; matrix products, arithmetic and copies ran while one was open for 14% -> 4% of each run, Pallas kernels for 0% -> 12%
where the time goes in v1:
time: 190 us; the launch traced here: 189 us
  starting transfers between devices  60.6 us (32%)
  Pallas kernels  50.1 us (26%)
  waiting for transfers between devices  38.9 us (20%)
  local copies, waits for them, and re-layouts  38.7 us (20%)
    unnamed x90, local copies, waits for them, and re-layouts  38.7 us
    ppermute x12, starting transfers between devices, ring(): lax.ppermute(value, 'x', [(i, (i + k) % N_GRP) for i in range(N_GRP)])  18.6 us
    ppermute x12, waiting for transfers between devices, ring(): lax.ppermute(value, 'x', [(i, (i + k) % N_GRP) for i in range(N_GRP)])  16.4 us
    all_to_all x1, starting transfers between devices, shards(): lax.all_to_all(packed.reshape(N_GRP * N_OWN, CAP, LANES), ALL, 0, 0, tile...  15.4 us
    pallas_call x1, Pallas kernels, edge(): pl.pallas_call(edge_kernel, name='edge', grid=(E_DEV // BLK,), in_specs=[...  14.7 us
    all_to_all x1, waiting for transfers between devices, shards(): lax.all_to_all(packed.reshape(N_GRP * N_OWN, CAP, LANES), ALL, 0, 0, tile...  12.4 us
    pallas_call x1, Pallas kernels, prep(): pl.pallas_call(prep_kernel, name='prep', grid=(E_DEV // BLK,), in_specs=[...  12.4 us
    all_to_all x1, starting transfers between devices, shards(): chip = rel_sum(lax.all_to_all(chip, ('y', 'z'), 0, 0, tiled=True))  11.3 us
  transfers between devices with their start and end apart: 20, of which 8 were waited for; matrix products, arithmetic and copies ran while one was open for 4% of the time, Pallas kernels for 12%

profile of v1, /device:TPU:1, one launch (start us, length us, event | category | flops | bytes accessed | tf_op | source)
XLA Modules:
  0.0 189.3 jit_solution(64068284944685732)
XLA Ops:
  0.6 1.1 copy.18.n0_ref
  1.7 2.1 %collective-permute-start = (bf16[256,400]{1,0:T(8,128)(2,1)S(1)}, bf16[256,400]{1,0:T(8,128)(2,1)S(1)}, u32[]{:S(2)}, u32[]{:S(2)}) collective-permute-start(bf16[256,400]{1,0:T(8,128)(2,1)S(1)} %copy.18.n0_ref), channel_id=1, source_target_pairs={{0,64},{64,128},{128,192},{192,0},{1,65},{65,129},{129,193},{193,1... | collective-permute-start | bytes 614408 | tf_op jit(solution)/shard_map/ppermute | solution.py:485
  3.8 2.5 %collective-permute-start.1 = (bf16[256,400]{1,0:T(8,128)(2,1)S(1)}, bf16[256,400]{1,0:T(8,128)(2,1)S(1)}, u32[]{:S(2)}, u32[]{:S(2)}) collective-permute-start(bf16[256,400]{1,0:T(8,128)(2,1)S(1)} %copy.18.n0_ref), channel_id=1, source_target_pairs={{0,128},{64,192},{128,0},{192,64},{1,129},{65,193},{129,1},{193,65... | collective-permute-start | bytes 614408 | tf_op jit(solution)/shard_map/ppermute | solution.py:485
  6.3 1.2 collective-permute-start.2
  7.4 1.3 copy.12.head_ref
  8.8 1.3 copy.13.tail_ref
  10.2 3.6 %copy.14.table_ref = f32[1500,400]{1,0:T(8,128)} copy(f32[1500,400]{0,1:T(8,128)} %param.14) | data formatting | bytes 4800000 | tf_op args[4]
  13.8 12.4 %prep.1 = (bf16[512,768]{1,0:T(8,128)(2,1)S(1)}, bf16[512,768]{1,0:T(8,128)(2,1)S(1)}, f32[512,768]{1,0:T(8,128)}, bf16[512,768]{1,0:T(8,128)(2,1)S(1)}, bf16[51...) custom-call(bf16[768,400]{1,0:T(8,128)(2,1)S(1)} %copy.12.head_ref, ...), custom_call_target="tpu_custom_call" | custom-call | flops 8000000000 | bytes 8000000 | tf_op jit(solution)/shard_map/prep/pallas_call | solution.py:146
  28.9 1.0 copy-done.36
  31.3 0.9 copy-done.14
  32.3 0.9 copy-done.17
  33.2 1.1 copy-done.35
  34.3 1.1 copy-done.37
  35.5 8.1 %score.1 = (bf16[1024,768]{1,0:T(8,128)(2,1)S(1)}, bf16[1024,768]{1,0:T(8,128)(2,1)}, f32[8,768]{1,0:T(8,128)S(1)}, f32[256,512]{1,0:T(8,128)S(1)}, bf16[256,512...) custom-call(bf16[256,400]{1,0:T(8,128)(2,1)S(1)} %copy.18.n0_ref, ...), custom_call_target="tpu_custom_call" | custom-call | flops 5000000000 | bytes 8000000 | tf_op jit(solution)/shard_map/score/pallas_call | solution.py:218
  43.6 1.2 copy-done.21
  44.8 14.7 %edge.1 = (bf16[512,768]{1,0:T(8,128)(2,1)S(1)}, bf16[512,768]{1,0:T(8,128)(2,1)S(1)}, bf16[512,768]{1,0:T(8,128)(2,1)S(1)}, bf16[512,768]{1,0:T(8,128)(2,1)S(1)...) custom-call(s32[1]{0:T(128)} %bitcast.core_ref, bf16[256,400]{1,0:T(8,128)(2,1)S(1)} %copy.18.n0_ref, ...), custom_call_target="tpu_custom_call" | custom-call | flops 5000000000 | bytes 12000000 | tf_op jit(solution)/shard_map/edge/pallas_call | solution.py:291
  63.0 1.5 collective-permute-start.6
  64.6 3.2 %collective-permute-done.6.other_ref = f32[768,512]{1,0:T(8,128)S(1)} collective-permute-done((f32[768,512]{1,0:T(8,128)}, f32[768,512]{1,0:T(8,128)S(1)}, u32[]{:S(2)}, u32[]{:S(2)}) %collective-permute-start.6) | collective-permute-done | bytes 1572896 | tf_op jit(solution)/shard_map/ppermute | solution.py:489
  67.8 1.4 copy-done
  70.0 1.7 collective-permute-start.8
  71.8 2.0 %collective-permute-start.9 = (bf16[768,128]{1,0:T(8,128)(2,1)S(1)}, bf16[768,128]{1,0:T(8,128)(2,1)S(1)}, u32[]{:S(2)}, u32[]{:S(2)}) collective-permute-start(bf16[768,128]{1,0:T(8,128)(2,1)S(1)} %get-tuple-element.51), channel_id=1, source_target_pairs={{0,192},{64,0},{128,64},{192,128},{1,193},{65,1},{129,65},{193,129... | collective-permute-start | bytes 589832 | tf_op jit(solution)/shard_map/ppermute | solution.py:485
  73.7 3.7 %collective-permute-done.7.i1_ref = bf16[768,128]{1,0:T(8,128)(2,1)S(1)} collective-permute-done((bf16[768,128]{1,0:T(8,128)(2,1)S(1)}, bf16[768,128]{1,0:T(8,128)(2,1)S(1)}, u32[]{:S(2)}, u32[]{:S(2)}) %collective-permute-start.7) | collective-permute-done | bytes 196640 | tf_op jit(solution)/shard_map/ppermute | solution.py:485
  77.4 3.5 %collective-permute-done.8.i2_ref = bf16[768,128]{1,0:T(8,128)(2,1)S(1)} collective-permute-done((bf16[768,128]{1,0:T(8,128)(2,1)S(1)}, bf16[768,128]{1,0:T(8,128)(2,1)S(1)}, u32[]{:S(2)}, u32[]{:S(2)}) %collective-permute-start.8) | collective-permute-done | bytes 196640 | tf_op jit(solution)/shard_map/ppermute | solution.py:485
  82.4 11.3 %all-to-all-start.1 = ((f32[32,24,128]{2,1,0:T(8,128)}), f32[32,24,128]{2,1,0:T(8,128)S(1)}, u32[]{:S(2)}, u32[]{:S(2)}) async-start(f32[32,24,128]{2,1,0:T(8,128)} %bitcast.4), calls=%async_computation.1 | async-start | bytes 786432 | tf_op jit(solution)/shard_map/all_to_all | solution.py:509
  93.7 3.1 %collective-permute-start.3 = (bf16[256,512]{1,0:T(8,128)(2,1)}, bf16[256,512]{1,0:T(8,128)(2,1)S(1)}, u32[]{:S(2)}, u32[]{:S(2)}) collective-permute-start(bf16[256,512]{1,0:T(8,128)(2,1)} %get-tuple-element.32), channel_id=1, source_target_pairs={{0,192},{64,0},{128,64},{192,128},{1,193},{65,1},{129,65},{193,129... | collective-permute-start | bytes 786440 | tf_op jit(solution)/shard_map/ppermute | solution.py:485
  97.4 6.8 %all-to-all-done.1.in_ref = f32[32,24,128]{2,1,0:T(8,128)S(1)} async-done(((f32[32,24,128]{2,1,0:T(8,128)}), f32[32,24,128]{2,1,0:T(8,128)S(1)}, u32[]{:S(2)}, u32[]{:S(2)}) %all-to-all-start.1) | async-done | bytes 393248 | tf_op jit(solution)/shard_map/all_to_all | solution.py:509
  104.9 7.4 %all-to-all-start.2 = ((bf16[32,24,128]{2,1,0:T(8,128)(2,1)}), bf16[32,24,128]{2,1,0:T(8,128)(2,1)S(1)}, u32[]{:S(2)}, u32[]{:S(2)}) async-start(bf16[32,24,128]{2,1,0:T(8,128)(2,1)} %rel_sum.1), calls=%async_computation.2 | async-start | bytes 393216 | tf_op jit(solution)/shard_map/all_to_all | solution.py:510
  112.3 1.1 copy-done.23
  113.4 1.1 copy-done.25
  114.5 1.1 copy-done.27
  115.7 1.1 copy-done.29
  116.8 4.7 %slot.1.part_ref = f32[1024,512]{1,0:T(8,128)S(1)} custom-call(s32[1,1792]{1,0:T(1,128)S(1)} %get-tuple-element.27.target_h_ref.target_t_ref.target_ref, s32[1,1792]{1,0:T(1,128)S(1)} %get-tuple-element.27.target_h_ref.target_t_ref.target_ref, bf16[512,768]{1,0:T(8,128)(2,1)S(1)} %copy-done.23, bf16[512,768]{1,0:T(8,128)(2,1)S(1)} %copy-done.25, ...), custom_call_target="tpu_custom_call" | custom-call | flops 4000000000 | bytes 5000000 | tf_op jit(solution)/shard_map/slot/pallas_call | solution.py:321
  121.6 1.8 pack.1
  123.4 15.4 %all-to-all-start = ((bf16[256,16,128]{2,1,0:T(8,128)(2,1)}), bf16[256,16,128]{2,1,0:T(8,128)(2,1)S(1)}, u32[]{:S(2)}, u32[]{:S(2)}) async-start(bf16[256,16,128]{2,1,0:T(8,128)(2,1)} %bitcast.1), calls=%async_computation | async-start | bytes 2097152 | tf_op jit(solution)/shard_map/all_to_all | solution.py:507
  138.9 1.5 collective-permute-start.10
  140.3 2.4 %collective-permute-start.11 = (bf16[768,128]{1,0:T(8,128)(2,1)S(1)}, bf16[768,128]{1,0:T(8,128)(2,1)S(1)}, u32[]{:S(2)}, u32[]{:S(2)}) collective-permute-start(bf16[768,128]{1,0:T(8,128)(2,1)S(1)} %bitcast.8), channel_id=1, source_target_pairs={{0,128},{64,192},{128,0},{192,64},{1,129},{65,193},{129,1},{193,65... | collective-permute-start | bytes 589832 | tf_op jit(solution)/shard_map/ppermute | solution.py:485
  142.7 1.2 collective-permute-start.12
  143.9 1.2 collective-permute-start.13
  145.1 2.0 %collective-permute-done.10.refs_1_ = bf16[768,128]{1,0:T(8,128)(2,1)S(1)} collective-permute-done((bf16[768,128]{1,0:T(8,128)(2,1)S(1)}, bf16[768,128]{1,0:T(8,128)(2,1)S(1)}, u32[]{:S(2)}, u32[]{:S(2)}) %collective-permute-start.10) | collective-permute-done | bytes 196640 | tf_op jit(solution)/shard_map/ppermute | solution.py:485
  147.1 3.3 %collective-permute-start.14 = (bf16[768,128]{1,0:T(8,128)(2,1)S(1)}, bf16[768,128]{1,0:T(8,128)(2,1)S(1)}, u32[]{:S(2)}, u32[]{:S(2)}) collective-permute-start(bf16[768,128]{1,0:T(8,128)(2,1)S(1)} %collective-permute-done.10.refs_1_), channel_id=1, source_target_pairs={{0,1},{1,0},{2,3},{3,2},{4,5},{5,4},{6,7},{7,6},{8,9},{9,8},{10,11... | collective-permute-start | bytes 589832 | tf_op jit(solution)/shard_map/ppermute | solution.py:489
  150.5 6.6 %collective-permute-done.11.refs_2_ = bf16[768,128]{1,0:T(8,128)(2,1)S(1)} collective-permute-done((bf16[768,128]{1,0:T(8,128)(2,1)S(1)}, bf16[768,128]{1,0:T(8,128)(2,1)S(1)}, u32[]{:S(2)}, u32[]{:S(2)}) %collective-permute-start.11) | collective-permute-done | bytes 196640 | tf_op jit(solution)/shard_map/ppermute | solution.py:485
  157.0 1.7 collective-permute-start.15
  158.9 12.4 %all-to-all-done = bf16[256,16,128]{2,1,0:T(8,128)(2,1)S(1)} async-done(((bf16[256,16,128]{2,1,0:T(8,128)(2,1)}), bf16[256,16,128]{2,1,0:T(8,128)(2,1)S(1)}, u32[]{:S(2)}, u32[]{:S(2)}) %all-to-all-start) | async-done | bytes 1048608 | tf_op jit(solution)/shard_map/all_to_all | solution.py:507
  171.4 3.7 %partition.1 = f32[1024,100]{1,0:T(8,128)S(1)} custom-call(bf16[4096,128]{1,0:T(8,128)(2,1)S(1)} %bitcast.6), custom_call_target="tpu_custom_call" | custom-call | flops 2000000000 | bytes 2000000 | tf_op jit(solution)/shard_map/partition/pallas_call | solution.py:380
  175.1 1.0 copy.20
  178.8 0.9 copy-done.2
  184.3 2.7 %table.1 = f32[1500,400]{1,0:T(8,128)S(1)} custom-call(s32[2]{0:T(128)S(1)} %pad_add_fusion.1.place_ref, bf16[768,128]{1,0:T(8,128)(2,1)S(1)} %bitcast.11, bf16[768,128]{1,0:T(8,128)(2,1)S(1)} %collective-permute-done.10.refs_1_, bf16[768,128]{1,0:T(8,128)(2,1)S(1)} %copy-done.2, bf16[768,128]{1,0:T(8,128)(2,1)S(1)} %copy-done.4, ...), custom_call_target="tpu_custom_call" | custom-call | flops 1000000000 | bytes 4000000 | tf_op jit(solution)/shard_map/table/pallas_call | solution.py:472
  187.0 2.2 %copy.21 = f32[1500,400]{0,1:T(8,128)} copy(f32[1500,400]{1,0:T(8,128)S(1)} %table.1) | data formatting | bytes 4800000
  (96 shorter events, 19.0 us)
Async XLA Ops:
  0.6 9.5 %copy-start.40 = (s32[768]{0:T(1024)S(1)}, s32[768]{0:T(1024)}, u32[]{:S(2)}) copy-start(s32[768]{0:T(1024)} %param.12) | copy-start | bytes 9220
  1.7 28.2 %collective-permute-start = (bf16[256,400]{1,0:T(8,128)(2,1)S(1)}, bf16[256,400]{1,0:T(8,128)(2,1)S(1)}, u32[]{:S(2)}, u32[]{:S(2)}) collective-permute-start(bf16[256,400]{1,0:T(8,128)(2,1)S(1)} %copy.18.n0_ref), channel_id=1, source_target_pairs={{0,64},{64,128},{128,192},{192,0},{1,65},{65,129},{129,193},{193,1... | collective-permute-start | bytes 614408 | tf_op jit(solution)/shard_map/ppermute | solution.py:485
  3.8 26.1 %collective-permute-start.1 = (bf16[256,400]{1,0:T(8,128)(2,1)S(1)}, bf16[256,400]{1,0:T(8,128)(2,1)S(1)}, u32[]{:S(2)}, u32[]{:S(2)}) collective-permute-start(bf16[256,400]{1,0:T(8,128)(2,1)S(1)} %copy.18.n0_ref), channel_id=1, source_target_pairs={{0,128},{64,192},{128,0},{192,64},{1,129},{65,193},{129,1},{193,65... | collective-permute-start | bytes 614408 | tf_op jit(solution)/shard_map/ppermute | solution.py:485
  6.3 24.3 %collective-permute-start.2 = (bf16[256,400]{1,0:T(8,128)(2,1)S(1)}, bf16[256,400]{1,0:T(8,128)(2,1)S(1)}, u32[]{:S(2)}, u32[]{:S(2)}) collective-permute-start(bf16[256,400]{1,0:T(8,128)(2,1)S(1)} %copy.18.n0_ref), channel_id=1, source_target_pairs={{0,192},{64,0},{128,64},{192,128},{1,193},{65,1},{129,65},{193,129... | collective-permute-start | bytes 614408 | tf_op jit(solution)/shard_map/ppermute | solution.py:485
  10.2 3.6 %copy-start.38 = (s32[768]{0:T(1024)S(1)}, s32[768]{0:T(1024)}, u32[]{:S(2)}) copy-start(s32[768]{0:T(1024)} %param.18) | copy-start | bytes 9220
  10.2 3.6 %copy-start.39 = (s32[768]{0:T(1024)S(1)}, s32[768]{0:T(1024)}, u32[]{:S(2)}) copy-start(s32[768]{0:T(1024)} %param.17) | copy-start | bytes 9220
  10.2 3.6 %copy-start.41 = (s32[256]{0:T(256)S(1)}, s32[256]{0:T(256)}, u32[]{:S(2)}) copy-start(s32[256]{0:T(256)} %param.19) | copy-start | bytes 3076
  10.2 3.6 %copy-start.19 = (s32[1,1024]{1,0:T(1,128)S(1)}, s32[1,1024]{1,0:T(1,128)}, u32[]{:S(2)}) copy-start(s32[1,1024]{1,0:T(1,128)} %uid_ref.1) | copy-start | bytes 12292
  10.2 3.6 %copy-start.20 = (s32[1,64]{1,0:T(1,128)S(1)}, s32[1,64]{1,0:T(1,128)}, u32[]{:S(2)}) copy-start(s32[1,64]{1,0:T(1,128)} %counts_ref.1) | copy-start | bytes 772
  28.9 1.0 copy-start.36
  31.3 0.9 copy-start.14
  32.3 0.9 copy-start.17
  33.2 1.1 copy-start.35
  34.3 1.1 copy-start.37
  35.5 9.3 %copy-start.15 = (bf16[256,400]{1,0:T(8,128)(2,1)S(1)}, bf16[256,400]{1,0:T(8,128)(2,1)}, u32[]{:S(2)}) copy-start(bf16[256,400]{1,0:T(8,128)(2,1)} %copy-done.13) | copy-start | bytes 614404
  35.5 9.3 %copy-start.18 = (bf16[256,400]{1,0:T(8,128)(2,1)S(1)}, bf16[256,400]{1,0:T(8,128)(2,1)}, u32[]{:S(2)}) copy-start(bf16[256,400]{1,0:T(8,128)(2,1)} %copy-done.16) | copy-start | bytes 614404
  35.5 9.3 %copy-start.31 = (bf16[512,768]{1,0:T(8,128)(2,1)S(1)}, bf16[512,768]{1,0:T(8,128)(2,1)}, u32[]{:S(2)}) copy-start(bf16[512,768]{1,0:T(8,128)(2,1)} %copy-done.30) | copy-start | bytes 2359300
  35.5 9.3 %copy-start.33 = (bf16[512,768]{1,0:T(8,128)(2,1)S(1)}, bf16[512,768]{1,0:T(8,128)(2,1)}, u32[]{:S(2)}) copy-start(bf16[512,768]{1,0:T(8,128)(2,1)} %copy-done.32) | copy-start | bytes 2359300
  43.6 1.2 copy-start.21
  63.0 4.8 %collective-permute-start.6 = (f32[768,512]{1,0:T(8,128)}, f32[768,512]{1,0:T(8,128)S(1)}, u32[]{:S(2)}, u32[]{:S(2)}) collective-permute-start(f32[768,512]{1,0:T(8,128)} %get-tuple-element.47), channel_id=1, source_target_pairs={{0,1},{1,0},{2,3},{3,2},{4,5},{5,4},{6,7},{7,6},{8,9},{9,8},{10,11... | collective-permute-start | bytes 4718600 | tf_op jit(solution)/shard_map/ppermute | solution.py:489
  67.8 1.4 copy-start
  69.6 7.8 %collective-permute-start.7 = (bf16[768,128]{1,0:T(8,128)(2,1)S(1)}, bf16[768,128]{1,0:T(8,128)(2,1)S(1)}, u32[]{:S(2)}, u32[]{:S(2)}) collective-permute-start(bf16[768,128]{1,0:T(8,128)(2,1)S(1)} %get-tuple-element.49), channel_id=1, source_target_pairs={{0,64},{64,128},{128,192},{192,0},{1,65},{65,129},{129,193},{193,1... | collective-permute-start | bytes 589832 | tf_op jit(solution)/shard_map/ppermute | solution.py:485
  70.0 10.9 %collective-permute-start.8 = (bf16[768,128]{1,0:T(8,128)(2,1)S(1)}, bf16[768,128]{1,0:T(8,128)(2,1)S(1)}, u32[]{:S(2)}, u32[]{:S(2)}) collective-permute-start(bf16[768,128]{1,0:T(8,128)(2,1)S(1)} %get-tuple-element.50), channel_id=1, source_target_pairs={{0,128},{64,192},{128,0},{192,64},{1,129},{65,193},{129,1},{193,65... | collective-permute-start | bytes 589832 | tf_op jit(solution)/shard_map/ppermute | solution.py:485
  71.8 9.8 %collective-permute-start.9 = (bf16[768,128]{1,0:T(8,128)(2,1)S(1)}, bf16[768,128]{1,0:T(8,128)(2,1)S(1)}, u32[]{:S(2)}, u32[]{:S(2)}) collective-permute-start(bf16[768,128]{1,0:T(8,128)(2,1)S(1)} %get-tuple-element.51), channel_id=1, source_target_pairs={{0,192},{64,0},{128,64},{192,128},{1,193},{65,1},{129,65},{193,129... | collective-permute-start | bytes 589832 | tf_op jit(solution)/shard_map/ppermute | solution.py:485
  82.4 21.8 %all-to-all-start.1 = ((f32[32,24,128]{2,1,0:T(8,128)}), f32[32,24,128]{2,1,0:T(8,128)S(1)}, u32[]{:S(2)}, u32[]{:S(2)}) async-start(f32[32,24,128]{2,1,0:T(8,128)} %bitcast.4), calls=%async_computation.1 | async-start | bytes 786432 | tf_op jit(solution)/shard_map/all_to_all | solution.py:509
  93.7 27.9 %collective-permute-start.3 = (bf16[256,512]{1,0:T(8,128)(2,1)}, bf16[256,512]{1,0:T(8,128)(2,1)S(1)}, u32[]{:S(2)}, u32[]{:S(2)}) collective-permute-start(bf16[256,512]{1,0:T(8,128)(2,1)} %get-tuple-element.32), channel_id=1, source_target_pairs={{0,192},{64,0},{128,64},{192,128},{1,193},{65,1},{129,65},{193,129... | collective-permute-start | bytes 786440 | tf_op jit(solution)/shard_map/ppermute | solution.py:485
  96.7 24.8 %collective-permute-start.4 = (bf16[256,512]{1,0:T(8,128)(2,1)}, bf16[256,512]{1,0:T(8,128)(2,1)S(1)}, u32[]{:S(2)}, u32[]{:S(2)}) collective-permute-start(bf16[256,512]{1,0:T(8,128)(2,1)} %get-tuple-element.33), channel_id=1, source_target_pairs={{0,128},{64,192},{128,0},{192,64},{1,129},{65,193},{129,1},{193,65... | collective-permute-start | bytes 786440 | tf_op jit(solution)/shard_map/ppermute | solution.py:485
  96.7 24.9 %collective-permute-start.5 = (bf16[256,512]{1,0:T(8,128)(2,1)S(1)}, bf16[256,512]{1,0:T(8,128)(2,1)S(1)}, u32[]{:S(2)}, u32[]{:S(2)}) collective-permute-start(bf16[256,512]{1,0:T(8,128)(2,1)S(1)} %get-tuple-element.34), channel_id=1, source_target_pairs={{0,64},{64,128},{128,192},{192,0},{1,65},{65,129},{129,193},{193,1... | collective-permute-start | bytes 786440 | tf_op jit(solution)/shard_map/ppermute | solution.py:485
  104.9 18.5 %all-to-all-start.2 = ((bf16[32,24,128]{2,1,0:T(8,128)(2,1)}), bf16[32,24,128]{2,1,0:T(8,128)(2,1)S(1)}, u32[]{:S(2)}, u32[]{:S(2)}) async-start(bf16[32,24,128]{2,1,0:T(8,128)(2,1)} %rel_sum.1), calls=%async_computation.2 | async-start | bytes 393216 | tf_op jit(solution)/shard_map/all_to_all | solution.py:510
  112.3 1.1 copy-start.23
  113.4 1.1 copy-start.25
  114.5 1.1 copy-start.27
  115.7 1.1 copy-start.29
  123.4 47.9 %all-to-all-start = ((bf16[256,16,128]{2,1,0:T(8,128)(2,1)}), bf16[256,16,128]{2,1,0:T(8,128)(2,1)S(1)}, u32[]{:S(2)}, u32[]{:S(2)}) async-start(bf16[256,16,128]{2,1,0:T(8,128)(2,1)} %bitcast.1), calls=%async_computation | async-start | bytes 2097152 | tf_op jit(solution)/shard_map/all_to_all | solution.py:507
  138.9 8.3 %collective-permute-start.10 = (bf16[768,128]{1,0:T(8,128)(2,1)S(1)}, bf16[768,128]{1,0:T(8,128)(2,1)S(1)}, u32[]{:S(2)}, u32[]{:S(2)}) collective-permute-start(bf16[768,128]{1,0:T(8,128)(2,1)S(1)} %bitcast.7), channel_id=1, source_target_pairs={{0,64},{64,128},{128,192},{192,0},{1,65},{65,129},{129,193},{193,1... | collective-permute-start | bytes 589832 | tf_op jit(solution)/shard_map/ppermute | solution.py:485
  140.3 16.7 %collective-permute-start.11 = (bf16[768,128]{1,0:T(8,128)(2,1)S(1)}, bf16[768,128]{1,0:T(8,128)(2,1)S(1)}, u32[]{:S(2)}, u32[]{:S(2)}) collective-permute-start(bf16[768,128]{1,0:T(8,128)(2,1)S(1)} %bitcast.8), channel_id=1, source_target_pairs={{0,128},{64,192},{128,0},{192,64},{1,129},{65,193},{129,1},{193,65... | collective-permute-start | bytes 589832 | tf_op jit(solution)/shard_map/ppermute | solution.py:485
  142.7 16.0 %collective-permute-start.12 = (bf16[768,128]{1,0:T(8,128)(2,1)S(1)}, bf16[768,128]{1,0:T(8,128)(2,1)S(1)}, u32[]{:S(2)}, u32[]{:S(2)}) collective-permute-start(bf16[768,128]{1,0:T(8,128)(2,1)S(1)} %bitcast.9), channel_id=1, source_target_pairs={{0,192},{64,0},{128,64},{192,128},{1,193},{65,1},{129,65},{193,129... | collective-permute-start | bytes 589832 | tf_op jit(solution)/shard_map/ppermute | solution.py:485
  143.9 32.1 %collective-permute-start.13 = (bf16[768,128]{1,0:T(8,128)(2,1)S(1)}, bf16[768,128]{1,0:T(8,128)(2,1)S(1)}, u32[]{:S(2)}, u32[]{:S(2)}) collective-permute-start(bf16[768,128]{1,0:T(8,128)(2,1)S(1)} %bitcast.10), channel_id=1, source_target_pairs={{0,1},{1,0},{2,3},{3,2},{4,5},{5,4},{6,7},{7,6},{8,9},{9,8},{10,11... | collective-permute-start | bytes 589832 | tf_op jit(solution)/shard_map/ppermute | solution.py:489
  147.1 29.6 %collective-permute-start.14 = (bf16[768,128]{1,0:T(8,128)(2,1)S(1)}, bf16[768,128]{1,0:T(8,128)(2,1)S(1)}, u32[]{:S(2)}, u32[]{:S(2)}) collective-permute-start(bf16[768,128]{1,0:T(8,128)(2,1)S(1)} %collective-permute-done.10.refs_1_), channel_id=1, source_target_pairs={{0,1},{1,0},{2,3},{3,2},{4,5},{5,4},{6,7},{7,6},{8,9},{9,8},{10,11... | collective-permute-start | bytes 589832 | tf_op jit(solution)/shard_map/ppermute | solution.py:489
  157.0 18.0 %copy-start.1 = (bf16[768,128]{1,0:T(8,128)(2,1)}, bf16[768,128]{1,0:T(8,128)(2,1)S(1)}, u32[]{:S(2)}) copy-start(bf16[768,128]{1,0:T(8,128)(2,1)S(1)} %collective-permute-done.11.refs_2_) | copy-start | bytes 589828
  157.0 20.4 %collective-permute-start.15 = (bf16[768,128]{1,0:T(8,128)(2,1)S(1)}, bf16[768,128]{1,0:T(8,128)(2,1)S(1)}, u32[]{:S(2)}, u32[]{:S(2)}) collective-permute-start(bf16[768,128]{1,0:T(8,128)(2,1)S(1)} %collective-permute-done.11.refs_2_), channel_id=1, source_target_pairs={{0,1},{1,0},{2,3},{3,2},{4,5},{5,4},{6,7},{7,6},{8,9},{9,8},{10,11... | collective-permute-start | bytes 589832 | tf_op jit(solution)/shard_map/ppermute | solution.py:489
  158.8 16.3 %copy-start.3 = (bf16[768,128]{1,0:T(8,128)(2,1)}, bf16[768,128]{1,0:T(8,128)(2,1)S(1)}, u32[]{:S(2)}) copy-start(bf16[768,128]{1,0:T(8,128)(2,1)S(1)} %collective-permute-done.12.refs_3_) | copy-start | bytes 589828
  158.8 19.3 %collective-permute-start.16 = (bf16[768,128]{1,0:T(8,128)(2,1)S(1)}, bf16[768,128]{1,0:T(8,128)(2,1)S(1)}, u32[]{:S(2)}, u32[]{:S(2)}) collective-permute-start(bf16[768,128]{1,0:T(8,128)(2,1)S(1)} %collective-permute-done.12.refs_3_), channel_id=1, source_target_pairs={{0,1},{1,0},{2,3},{3,2},{4,5},{5,4},{6,7},{7,6},{8,9},{9,8},{10,11... | collective-permute-start | bytes 589832 | tf_op jit(solution)/shard_map/ppermute | solution.py:489
  178.8 0.9 copy-start.2
  179.7 0.9 copy-start.4
  180.6 0.9 copy-start.6
  181.5 0.9 copy-start.8
  182.5 0.9 copy-start.10
  (14 other events, 11.3 us)

commit v2 on v0

v2 whole, which is shorter than its diff:
```python
import jax
import jax.numpy as jnp
from jax import lax
from jax.experimental import pallas as pl
from jax.experimental.pallas import tpu as pltpu
from jax.sharding import Mesh
from jax.sharding import PartitionSpec as P

D = 400
HALF = D // 2
RELS = 1500
E_DEV = 768
ENT_DEV = 1024
NEG_DEV = 256
CAP = 16
NEG = 1024
U_CAP = 1024
N_GRP = 4
N_OWN = 64
N_XY = 16
LANES = 128
USED = D // N_GRP
REL_PAD = 1536
REL_HALF = REL_PAD // 2
REL_TILES = REL_HALF // 128
REL_PART = 160
ROWS = 2 * E_DEV
ALL = ("x", "y", "z", "c")
F32 = jnp.float32
BF16 = jnp.bfloat16
I32 = jnp.int32


def dot(a, b):
    return lax.dot_general(a, b, (((1,), (0,)), ((), ())), preferred_element_type=F32)


def dot_nt(a, b):
    return lax.dot_general(a, b, (((1,), (1,)), ((), ())), preferred_element_type=F32)


def split2(value):
    high = value.astype(BF16)
    return high, (value - high.astype(F32)).astype(BF16)


def eye(size):
    row = lax.broadcasted_iota(I32, (size, size), 0)
    col = lax.broadcasted_iota(I32, (size, size), 1)
    return jnp.where(row == col, 1.0, 0.0).astype(BF16)


def one_hot(ids_row, rows):
    spot = lax.broadcasted_iota(I32, (LANES, ids_row.shape[1]), 0).astype(BF16)
    blocks = []
    for at in range(0, rows, LANES):
        here = jnp.clip(ids_row - at, -1, LANES).astype(BF16)
        blocks.append(jnp.where(spot == here, jnp.ones((), BF16), jnp.zeros((), BF16)))
    return jnp.concatenate(blocks, 0)


def full(shape):
    return pl.BlockSpec(shape, lambda i: (0,) * len(shape))


def arr(shape, dtype):
    return jax.ShapeDtypeStruct(shape, dtype)


def call(kernel, name, grid, in_specs, out_specs, out_shape, scratch=(), mib=60, flops=10**6):
    return pl.pallas_call(
        kernel,
        name=name,
        grid=(grid,),
        in_specs=in_specs,
        out_specs=out_specs,
        out_shape=out_shape,
        scratch_shapes=list(scratch),
        compiler_params=pltpu.CompilerParams(vmem_limit_bytes=mib * 1024 * 1024),
        cost_estimate=pl.CostEstimate(flops=flops, bytes_accessed=10**5, transcendentals=0),
    )


SMEM = pl.BlockSpec(memory_space=pltpu.SMEM)


def prep_kernel(head_ref, tail_ref, rid_ref, table_ref, counts_ref, uid_ref, hs_ref, ts_ref, ns_ref,
                r_ref, q_ref, m_ref, pos_ref, rids_ref, th_ref, tt_ref, tn_ref, code_ref,
                high_ref, mid_ref, low_ref):
    table = table_ref[...]
    high = table.astype(BF16)
    rest = table - high.astype(F32)
    mid = rest.astype(BF16)
    low = (rest - mid.astype(F32)).astype(BF16)
    for ref, value in ((high_ref, high), (mid_ref, mid), (low_ref, low)):
        ref[:, pl.ds(REL_PAD - LANES, LANES)] = jnp.zeros((D, LANES), BF16)
        ref[:, pl.ds(0, RELS)] = value

    rids_ref[...] = rid_ref[...].reshape(1, E_DEV)
    counts = jnp.broadcast_to(counts_ref[...], (N_OWN, N_OWN)).astype(F32)
    part = lax.broadcasted_iota(I32, (N_OWN, N_OWN), 0)
    other = lax.broadcasted_iota(I32, (N_OWN, N_OWN), 1)
    ends = jnp.sum(jnp.where(other <= part, counts, 0.0), 1, keepdims=True).astype(I32)
    own = jnp.sum(jnp.where(other == part, counts, 0.0), 1, keepdims=True).astype(I32)
    for out, ref in ((th_ref, hs_ref), (tt_ref, ts_ref), (tn_ref, ns_ref)):
        slots = ref[...].reshape(1, -1)
        out[...] = slots + jnp.sum(jnp.where(slots >= ends, CAP - own, 0), 0, keepdims=True)

    place = lax.broadcasted_iota(I32, (U_CAP, N_OWN), 0)
    lane = (place & (CAP - 1)).astype(F32)
    owner = lax.broadcasted_iota(I32, (U_CAP, N_OWN), 1)
    counts_all = jnp.broadcast_to(counts_ref[...], (U_CAP, N_OWN)).astype(F32)
    start = jnp.sum(jnp.where(owner < (place >> 4), counts_all, 0.0), 1, keepdims=True)
    count = jnp.sum(jnp.where(owner == (place >> 4), counts_all, 0.0), 1, keepdims=True)
    spot = (start + lane[:, :1]).astype(I32)
    column = lax.broadcasted_iota(I32, (U_CAP, U_CAP), 1)
    uid = uid_ref[...].astype(F32)
    picked = jnp.sum(jnp.where(column == spot, uid, 0.0), 1, keepdims=True)
    picked = jnp.where(lane[:, :1] < count, picked, float(ENT_DEV)).astype(I32)
    lanes = lax.broadcasted_iota(I32, (U_CAP, LANES), 1)
    code = jnp.where(lanes == USED, picked >> 5, jnp.where(lanes == USED + 1, picked & 31, 0))
    code_ref[...] = code.astype(F32)

    hit = one_hot(rids_ref[...], REL_PAD)
    rel = dot(high_ref[...], hit) + dot(mid_ref[...], hit) + dot(low_ref[...], hit)
    r_ref[...] = rel
    head = head_ref[...].astype(F32)
    tail = tail_ref[...].astype(F32)
    hr, hi, tr, ti, rr, ri = head[:HALF], head[HALF:], tail[:HALF], tail[HALF:], rel[:HALF], rel[HALF:]
    query = jnp.concatenate([hr * rr - hi * ri, hr * ri + hi * rr], 0).astype(BF16)
    mirror = jnp.concatenate([rr * tr + ri * ti, rr * ti - ri * tr], 0).astype(BF16)
    q_ref[...] = query
    m_ref[...] = mirror
    pos_t = jnp.sum(query.astype(F32) * tail, 0, keepdims=True)
    pos_h = jnp.sum(mirror.astype(F32) * head, 0, keepdims=True)
    side = lax.broadcasted_iota(I32, (8, E_DEV), 0)
    pos_ref[...] = jnp.where(side == 0, pos_t, pos_h)


def prep(heads, tails, rid, table, counts, uid, hs, ts, ns):
    cols = lambda dt: arr((D, E_DEV), dt)
    return call(
        prep_kernel, "prep", 1,
        [full((D, E_DEV)), full((D, E_DEV)), full((E_DEV,)), full((D, RELS)), full((1, N_OWN)), full((1, U_CAP)),
         full((E_DEV,)), full((E_DEV,)), full((NEG_DEV,))],
        [full((D, E_DEV))] * 3 + [full((8, E_DEV))] + [full((1, E_DEV))] * 3 + [full((1, NEG_DEV)), full((U_CAP, LANES))],
        [cols(F32), cols(BF16), cols(BF16), arr((8, E_DEV), F32),
         arr((1, E_DEV), I32), arr((1, E_DEV), I32), arr((1, E_DEV), I32), arr((1, NEG_DEV), I32), arr((U_CAP, LANES), F32)],
        [pltpu.VMEM((D, REL_PAD), BF16)] * 3,
    )(heads, tails, rid, table, counts, uid, hs, ts, ns)


def edge_kernel(core_ref, n0_ref, n1_ref, n2_ref, n3_ref, head_ref, tail_ref, r_ref, q_ref, m_ref, pos_ref, rid_ref,
                pt_ref, ph_ref, first_ref, dq_ref, dm_ref, mine_ref, other_ref, neg_ref, turned_ref):
    turn = eye(NEG_DEV)
    for k, ref in enumerate((n0_ref, n1_ref, n2_ref, n3_ref)):
        value = ref[...]
        neg_ref[:, pl.ds(k * NEG_DEV, NEG_DEV)] = value
        turned_ref[pl.ds(k * NEG_DEV, NEG_DEV), :] = dot_nt(turn, value).astype(BF16)

    head = head_ref[...].astype(F32)
    tail = tail_ref[...].astype(F32)
    firsts = []
    for side, (query_ref, positives, prob_ref, grad_ref) in enumerate((
            (q_ref, tail, pt_ref, dq_ref), (m_ref, head, ph_ref, dm_ref))):
        positive = pos_ref[pl.ds(side, 1), :]
        scores = dot(turned_ref[...], query_ref[...])
        top = jnp.maximum(positive, jnp.max(scores, 0, keepdims=True))
        weight = jnp.exp(scores - top)
        pos_weight = jnp.exp(positive - top)
        total = pos_weight + jnp.sum(weight, 0, keepdims=True)
        first = pos_weight / total - 1.0
        probs = (weight * (1.0 / total)).astype(BF16)
        prob_ref[...] = probs
        grad_ref[...] = first * positives + dot(neg_ref[...], probs)
        firsts.append(first)
    row = lax.broadcasted_iota(I32, (8, E_DEV), 0)
    first_ref[...] = jnp.where(row == 0, firsts[0], firsts[1])

    hr, hi, tr, ti = head[:HALF], head[HALF:], tail[:HALF], tail[HALF:]
    qr, qi, mr, mi = dq_ref[:HALF], dq_ref[HALF:], dm_ref[:HALF], dm_ref[HALF:]
    d_rel = jnp.concatenate([(hr * qr + hi * qi) + (tr * mr + ti * mi), (hr * qi - hi * qr) + (ti * mr - tr * mi)], 0)
    ids = rid_ref[...] - REL_HALF * core_ref[0]
    ids = jnp.where(ids < 0, ids + REL_PAD, ids)
    hit = one_hot(ids, REL_PAD)
    high, low = split2(d_rel)
    for ref, at in ((other_ref, REL_HALF), (mine_ref, 0)):
        part = hit[at:at + REL_HALF]
        ref[...] = (dot_nt(part, high) + dot_nt(part, low)).T


def edge(core, negs, h, t, r, q, m, pos, rid):
    part = (D, NEG_DEV)
    cols = (D, E_DEV)
    half = (D, REL_HALF)
    return call(
        edge_kernel, "edge", 1,
        [SMEM] + [full(part)] * 4 + [full(cols)] * 5 + [full((8, E_DEV)), full((1, E_DEV))],
        [full((NEG, E_DEV))] * 2 + [full((8, E_DEV))] + [full(cols)] * 2 + [full(half)] * 2,
        [arr((NEG, E_DEV), BF16)] * 2 + [arr((8, E_DEV), F32)] + [arr(cols, F32)] * 2 + [arr(half, F32)] * 2,
        [pltpu.VMEM((D, NEG), BF16), pltpu.VMEM((NEG, D), BF16)],
        flops=10**10,
    )(core, *negs, h, t, r, q, m, pos, rid)


def group_kernel(q_ref, m_ref, pt_ref, ph_ref, own_ref, g1_ref, g2_ref, g3_ref):
    term = dot_nt(q_ref[...], pt_ref[...]) + dot_nt(m_ref[...], ph_ref[...])
    own_ref[...] = term[:, :NEG_DEV]
    for k, ref in enumerate((g1_ref, g2_ref, g3_ref)):
        ref[...] = term[:, (k + 1) * NEG_DEV:(k + 2) * NEG_DEV].astype(BF16)


def group(q, m, pt, ph):
    part = (D, NEG_DEV)
    return call(
        group_kernel, "group", 1,
        [full((D, E_DEV))] * 2 + [full((NEG, E_DEV))] * 2, [full(part)] * 4, [arr(part, F32)] + [arr(part, BF16)] * 3,
        flops=4 * 10**9,
    )(q, m, pt, ph)


def slot_kernel(target_h_ref, target_t_ref, first_ref, dq_ref, dm_ref, r_ref, q_ref, m_ref, code_ref, out_ref):
    rel = r_ref[...]
    dq = dq_ref[...]
    dm = dm_ref[...]
    rr, ri, qr, qi, mr, mi = rel[:HALF], rel[HALF:], dq[:HALF], dq[HALF:], dm[:HALF], dm[HALF:]
    d_head = first_ref[pl.ds(1, 1), :] * m_ref[...].astype(F32) + jnp.concatenate([rr * qr + ri * qi, rr * qi - ri * qr], 0)
    d_tail = first_ref[pl.ds(0, 1), :] * q_ref[...].astype(F32) + jnp.concatenate([rr * mr - ri * mi, rr * mi + ri * mr], 0)
    hit_h = one_hot(target_h_ref[...], U_CAP)
    hit_t = one_hot(target_t_ref[...], U_CAP)
    head_high, head_low = split2(d_head)
    tail_high, tail_low = split2(d_tail)
    total = (dot_nt(hit_h, head_high) + dot_nt(hit_h, head_low)) + (dot_nt(hit_t, tail_high) + dot_nt(hit_t, tail_low))
    code = code_ref[:, USED:]
    for k in range(N_GRP):
        out_ref[k] = jnp.concatenate([total[:, k * USED:(k + 1) * USED], code], 1)


def slot(th, tt, first, dq, dm, r, q, m, code):
    cols = full((D, E_DEV))
    shape = (N_GRP, U_CAP, LANES)
    return call(
        slot_kernel, "slot", 1,
        [full((1, E_DEV))] * 2 + [full((8, E_DEV))] + [cols] * 5 + [full((U_CAP, LANES))],
        full(shape), arr(shape, F32),
        flops=8 * 10**9,
    )(th, tt, first, dq, dm, r, q, m, code)


def pack_kernel(target_ref, own_ref, g1_ref, g2_ref, g3_ref, part_ref, out_ref):
    rows = own_ref[...] + g1_ref[...].astype(F32) + g2_ref[...].astype(F32) + g3_ref[...].astype(F32)
    hit = one_hot(target_ref[...], U_CAP)
    rest = jnp.zeros((LANES - USED, NEG_DEV), F32)
    for k in range(N_GRP):
        high, low = split2(jnp.concatenate([rows[k * USED:(k + 1) * USED], rest], 0))
        out_ref[k] = (part_ref[k] + (dot_nt(hit, high) + dot_nt(hit, low))).astype(BF16)


def pack(tn, own, g1, g2, g3, part):
    shape = (N_GRP, U_CAP, LANES)
    return call(
        pack_kernel, "pack", 1,
        [full((1, NEG_DEV))] + [full((D, NEG_DEV))] * 4 + [full(shape)],
        full(shape), arr(shape, BF16),
        flops=3 * 10**9,
    )(tn, own, g1, g2, g3, part)


def partition_kernel(rows_ref, out_ref, acc_ref):
    step = pl.program_id(0)
    rows = rows_ref[...]
    lane = lax.broadcasted_iota(I32, (8, LANES), 1)
    weight = jnp.where(lane == USED, 32.0, jnp.where(lane == USED + 1, 1.0, 0.0)).astype(BF16)
    ids = dot_nt(weight, rows)[:1].astype(I32)
    term = dot(one_hot(ids, ENT_DEV), rows)

    @pl.when(step == 0)
    def _():
        acc_ref[...] = term

    @pl.when(step > 0)
    def _():
        acc_ref[...] += term

    @pl.when(step == pl.num_programs(0) - 1)
    def _():
        out_ref[...] = acc_ref[...].T[:USED]


def partition(rows):
    block = 1024
    return call(
        partition_kernel, "partition", rows.shape[0] // block,
        [pl.BlockSpec((block, LANES), lambda i: (i, 0))],
        full((USED, ENT_DEV)),
        arr((USED, ENT_DEV), F32),
        [pltpu.VMEM((ENT_DEV, LANES), F32)],
    )(rows)


def rel_chip_kernel(mine_ref, other_ref, out_ref):
    for k in range(REL_TILES):
        at = pl.ds(k * LANES, LANES)
        out_ref[pl.ds(k * D, D), :] = (mine_ref[:, at] + other_ref[:, at]).astype(BF16)
    rest = N_XY * REL_PART - REL_TILES * D
    out_ref[pl.ds(REL_TILES * D, rest), :] = jnp.zeros((rest, LANES), BF16)


def rel_chip(mine, other):
    shape = (N_XY * REL_PART, LANES)
    return call(rel_chip_kernel, "rel_chip", 1, [full((D, REL_HALF))] * 2, full(shape), arr(shape, BF16), mib=24)(mine, other)


def rel_xy_kernel(in_ref, out_ref):
    total = jnp.sum(in_ref[...].astype(F32), 0).astype(BF16)
    out_ref[...] = jnp.broadcast_to(total[None], out_ref.shape)


def rel_xy(parts):
    shape = (REL_PART, LANES)
    return call(rel_xy_kernel, "rel_xy", 1, [full((N_XY,) + shape)], full((8,) + shape), arr((8,) + shape, BF16), mib=24)(parts)


def rel_z_kernel(in_ref, out_ref):
    out_ref[...] = jnp.sum(in_ref[...].astype(F32), 0).astype(BF16)


def rel_z(parts):
    shape = (REL_PART, LANES)
    return call(rel_z_kernel, "rel_z", 1, [full((8,) + shape)], full(shape), arr(shape, BF16), mib=24)(parts)


def place_kernel(me_ref, *refs):
    out_ref = refs[-1]
    rows = refs[0].shape[0]
    for k, ref in enumerate(refs[:-1]):
        at = pl.multiple_of(((me_ref[0] - k) & (N_GRP - 1)) * rows, rows)
        out_ref[pl.ds(at, rows), :] = ref[...]


def place(me, blocks, name):
    rows = blocks[0].shape[0]
    shape = (rows * N_GRP, LANES)
    return call(
        place_kernel, name, 1, [SMEM] + [full((rows, LANES))] * N_GRP, full(shape), arr(shape, BF16), mib=24
    )(me, *blocks)


def table_kernel(core_ref, mine_ref, other_ref, out_ref):
    for half, ref in enumerate((mine_ref, other_ref)):
        for place in range(2):
            @pl.when((core_ref[0] == half) == (place == 0))
            def _(ref=ref, place=place):
                for k in range(REL_TILES):
                    at = place * REL_HALF + k * LANES
                    width = min(LANES, RELS - at)
                    out_ref[:, pl.ds(at, width)] = ref[pl.ds(k * D, D), :].astype(F32)[:, :width]


def table(core, mine, other):
    return call(
        table_kernel, "table", 1, [SMEM] + [full((N_XY * REL_PART, LANES))] * 2, full((D, RELS)), arr((D, RELS), F32)
    )(core, mine, other)


def shift(value, axis, k):
    return lax.ppermute(value, axis, [(i, (i + k) % N_GRP) for i in range(N_GRP)])


def pair(value):
    return lax.ppermute(value, "c", [(0, 1), (1, 0)])


def around(value, axis):
    return [value] + [shift(value, axis, k) for k in (1, 2, 3)]


def shards(head_rows, tail_rows, rel_ids, neg_rows, rel_table, owner_counts, unique_ids, head_slot, tail_slot, negative_slot):
    core = lax.axis_index("c").astype(I32).reshape(1)
    x = lax.axis_index("x").astype(I32).reshape(1)
    y = lax.axis_index("y").astype(I32).reshape(1)
    heads, tails = head_rows.T, tail_rows.T
    negs = around(neg_rows.T, "x")
    r, q, m, pos, rid, th, tt, tn, code = prep(
        heads, tails, rel_ids, rel_table.T, owner_counts, unique_ids, head_slot, tail_slot, negative_slot)
    pt, ph, first, dq, dm, mine, other = edge(core, negs, heads, tails, r, q, m, pos, rid)
    own, g1, g2, g3 = group(q, m, pt, ph)
    back = [shift(g, "x", N_GRP - k) for k, g in ((1, g1), (2, g2), (3, g3))]
    other = pair(other)
    mine, other, own = lax.optimization_barrier((mine, other, own))
    chip = rel_chip(mine, other).reshape(N_XY, REL_PART, LANES)
    part = slot(th, tt, first, dq, dm, r, q, m, code)
    chip = lax.all_to_all(chip, ("x", "y"), 0, 0, tiled=True)
    chip, part, *back = lax.optimization_barrier((chip, part, *back))
    column = lax.all_to_all(rel_xy(chip), "z", 0, 0, tiled=True)
    piece = rel_z(column)
    packed = pack(tn, own, *back, part)
    piece, packed = lax.optimization_barrier((piece, packed))
    received = lax.all_to_all(packed.reshape(N_GRP * N_OWN, CAP, LANES), ALL, 0, 0, tiled=True)
    quarter = place(y, around(piece, "y"), "place_y")
    half = place(x, around(quarter, "x"), "place_x")
    rel_grad = table(core, half, pair(half))
    entity_grad = partition(received.reshape(-1, LANES))
    return entity_grad.T, rel_grad.T


def solution(mesh):
    split = Mesh(mesh.devices.reshape(N_GRP, 4, 8, 2), ALL)
    edges = P(ALL)
    rows = P(ALL, None)
    in_specs = (rows, rows, edges, rows, P(), rows, rows, edges, edges, edges)
    out_specs = (P(("y", "z", "c"), "x"), P())
    return jax.shard_map(shards, mesh=split, in_specs=in_specs, out_specs=out_specs, check_vma=False)
```

time: 469 us -> 125 us (0.27)
  waiting for transfers between devices: 322 us -> 27.7 us
  other arithmetic: 49.7 us -> 0 us
  Pallas kernels: 0 us -> 47.7 us
  local copies, waits for them, and re-layouts: 33.4 us -> 2.64 us
  starting transfers between devices: 25.5 us -> 45.6 us
  between operations: 16.6 us -> 0.77 us
  blocking collectives: 13.1 us -> 0 us
  matrix products: 8.38 us -> 0 us
    psum x1 -> x0, waiting for transfers between devices: 216 us -> none  [shards(): rel_grad = lax.psum(rel_terms, ('grp', 'own'))]
    unnamed x4 -> x0, waiting for transfers between devices: 62.8 us -> none
    pallas_call x0 -> x12, Pallas kernels: none -> 47.7 us  [the longest x1 12.5 us: edge(): call(edge_kernel, 'edge', 1, [SMEM] + [full(part)] * 4 + [full(cols)] * 5...]
    all_to_all x2 -> x3, waiting for transfers between devices: 42.7 us -> 12.1 us  [the longest x1 6.29 us: shards(): column = lax.all_to_all(rel_xy(chip), 'z', 0, 0, tiled=True)]
    scatter-add x3 -> x0, other arithmetic: 30.1 us -> none  [the longest x1 13.7 us: shards(): slot_sum = jax.ops.segment_sum(rows, slot_entries, num_segments=list_width)]
    ppermute x0 -> x14, starting transfers between devices: none -> 22.4 us  [the longest x12 18.7 us: shift(): lax.ppermute(value, axis, [(i, (i + k) % N_GRP) for i in range(N_GRP)])]
    ppermute x0 -> x14, waiting for transfers between devices: none -> 15.6 us  [the longest x12 13.8 us: shift(): lax.ppermute(value, axis, [(i, (i + k) % N_GRP) for i in range(N_GRP)])]
    gather x5 -> x0, local copies, waits for them, and re-layouts: 15.5 us -> none  [the longest x2 6.04 us: shards(): relations = jnp.take(rel_table, rel_ids, axis=0)]
  transfers between devices with their start and end apart: 5 -> 17, of which waited for: 3 -> 8; matrix products, arithmetic and copies ran while one was open for 14% -> 0% of each run, Pallas kernels for 0% -> 23%
where the time goes in v2:
time: 125 us; the launch traced here: 124 us
  Pallas kernels  47.7 us (38%)
  starting transfers between devices  45.6 us (36%)
  waiting for transfers between devices  27.7 us (22%)
  local copies, waits for them, and re-layouts  2.64 us (2%)
    ppermute x12, starting transfers between devices, shift(): lax.ppermute(value, axis, [(i, (i + k) % N_GRP) for i in range(N_GRP)])  18.7 us
    ppermute x12, waiting for transfers between devices, shift(): lax.ppermute(value, axis, [(i, (i + k) % N_GRP) for i in range(N_GRP)])  13.8 us
    pallas_call x1, Pallas kernels, edge(): call(edge_kernel, 'edge', 1, [SMEM] + [full(part)] * 4 + [full(cols)] * 5...  12.5 us
    all_to_all x1, starting transfers between devices, shards(): lax.all_to_all(packed.reshape(N_GRP * N_OWN, CAP, LANES), ALL, 0, 0, tile...  8.74 us
    all_to_all x1, starting transfers between devices, shards(): column = lax.all_to_all(rel_xy(chip), 'z', 0, 0, tiled=True)  8.19 us
    pallas_call x1, Pallas kernels, slot(): call(slot_kernel, 'slot', 1, [full((1, E_DEV))] * 2 + [full((8, E_DEV))]...  8.01 us
    pallas_call x1, Pallas kernels, prep(): call(prep_kernel, 'prep', 1, [full((D, E_DEV)), full((D, E_DEV)), full((E...  7.93 us
    all_to_all x1, starting transfers between devices, shards(): chip = lax.all_to_all(chip, ('x', 'y'), 0, 0, tiled=True)  6.3 us
  transfers between devices with their start and end apart: 17, of which 8 were waited for; matrix products, arithmetic and copies ran while one was open for 0% of the time, Pallas kernels for 23%

profile of v2, /device:TPU:1, one launch (start us, length us, event | category | flops | bytes accessed | tf_op | source)
XLA Modules:
  0.0 124.5 jit_solution(10737855063625187950)
XLA Ops:
  0.6 2.1 %collective-permute-start = (bf16[400,256]{1,0:T(8,128)(2,1)}, bf16[400,256]{1,0:T(8,128)(2,1)S(1)}, u32[]{:S(2)}, u32[]{:S(2)}) collective-permute-start(bf16[400,256]{1,0:T(8,128)(2,1)} %bitcast.21), channel_id=1, source_target_pairs={{0,64},{64,128},{128,192},{192,0},{1,65},{65,129},{129,193},{193,1... | collective-permute-start | bytes 614408 | tf_op jit(solution)/shard_map/ppermute | solution.py:367
  2.8 2.5 %collective-permute-start.1 = (bf16[400,256]{1,0:T(8,128)(2,1)}, bf16[400,256]{1,0:T(8,128)(2,1)S(1)}, u32[]{:S(2)}, u32[]{:S(2)}) collective-permute-start(bf16[400,256]{1,0:T(8,128)(2,1)} %bitcast.22), channel_id=1, source_target_pairs={{0,128},{64,192},{128,0},{192,64},{1,129},{65,193},{129,1},{193,65... | collective-permute-start | bytes 614408 | tf_op jit(solution)/shard_map/ppermute | solution.py:367
  5.2 1.2 collective-permute-start.2
  6.4 7.9 %prep.1 = (f32[400,768]{1,0:T(8,128)}, bf16[400,768]{1,0:T(8,128)(2,1)}, bf16[400,768]{1,0:T(8,128)(2,1)}, f32[8,768]{1,0:T(8,128)}, s32[1,768]{1,0:T(1,128)}, /...) custom-call(bf16[400,768]{1,0:T(8,128)(2,1)} %bitcast.16, ...), custom_call_target="tpu_custom_call" | custom-call | flops 1000000 | bytes 100000 | tf_op jit(solution)/shard_map/prep/pallas_call | solution.py:142
  14.3 0.0 collective-permute-done.n1_ref
  14.3 0.0 collective-permute-done.1.n2_ref
  14.3 0.0 collective-permute-done.2.n3_ref
  14.3 0.6 copy-done.7
  15.0 0.1 copy-done.8
  15.0 0.1 copy-done.9
  15.1 12.5 %edge.1 = (bf16[1024,768]{1,0:T(8,128)(2,1)}, bf16[1024,768]{1,0:T(8,128)(2,1)}, f32[8,768]{1,0:T(8,128)}, f32[400,768]{1,0:T(8,128)}, f32[400,768]{1,0:T(8,128)...) custom-call(s32[1]{0:T(128)} %bitcast.core_ref, bf16[400,256]{1,0:T(8,128)(2,1)} %bitcast.24, bf16[400,256]{1,0:T(8,128)(2,1)} %copy-done.7, ...), custom_call_target="tpu_custom_call" | custom-call | flops 10000000000 | bytes 100000 | tf_op jit(solution)/shard_map/edge/pallas_call | solution.py:196
  27.6 1.5 %collective-permute-start.3 = (f32[400,768]{1,0:T(8,128)}, f32[400,768]{1,0:T(8,128)S(1)}, u32[]{:S(2)}, u32[]{:S(2)}) collective-permute-start(f32[400,768]{1,0:T(8,128)} %get-tuple-element.38), channel_id=1, source_target_pairs={{0,1},{1,0},{2,3},{3,2},{4,5},{5,4},{6,7},{7,6},{8,9},{9,8},{10,11... | collective-permute-start | bytes 3686408 | tf_op jit(solution)/shard_map/ppermute | solution.py:371
  29.1 4.6 %group.1 = (f32[400,256]{1,0:T(8,128)}, bf16[400,256]{1,0:T(8,128)(2,1)}, bf16[400,256]{1,0:T(8,128)(2,1)}, bf16[400,256]{1,0:T(8,128)(2,1)}) custom-call(bf16[400,768]{1,0:T(8,128)(2,1)} %get-tuple-element.33.q_ref, bf16[400,768]{1,0:T(8,128)(2,1)} %get-tuple-element.34.m_ref, bf16[1024,768]{1,0:T(8,128)(2,1)} %get-tuple-element.39.pt_ref, ...), custom_call_target="tpu_custom_call" | custom-call | flops 4000000000 | bytes 100000 | tf_op jit(solution)/shard_map/group/pallas_call | solution.py:215
  33.7 1.8 %collective-permute-start.4 = (bf16[400,256]{1,0:T(8,128)(2,1)}, bf16[400,256]{1,0:T(8,128)(2,1)S(1)}, u32[]{:S(2)}, u32[]{:S(2)}) collective-permute-start(bf16[400,256]{1,0:T(8,128)(2,1)} %get-tuple-element.50), channel_id=1, source_target_pairs={{0,192},{64,0},{128,64},{192,128},{1,193},{65,1},{129,65},{193,129... | collective-permute-start | bytes 614408 | tf_op jit(solution)/shard_map/ppermute | solution.py:367
  35.4 0.9 collective-permute-start.5
  36.3 0.5 collective-permute-start.6
  36.8 0.0 collective-permute-done.3.other_ref
  36.8 1.0 rel_chip.1
  37.8 6.3 %all-to-all-start = ((bf16[16,160,128]{2,1,0:T(8,128)(2,1)}), bf16[16,160,128]{2,1,0:T(8,128)(2,1)S(1)}, u32[]{:S(2)}, u32[]{:S(2)}) async-start(bf16[16,160,128]{2,1,0:T(8,128)(2,1)} %bitcast.5), calls=%async_computation | async-start | bytes 1310720 | tf_op jit(solution)/shard_map/all_to_all | solution.py:393
  44.1 8.0 %slot.1.part_ref = f32[4,1024,128]{2,1,0:T(8,128)} custom-call(s32[1,768]{1,0:T(1,128)} %get-tuple-element.44.target_h_ref, s32[1,768]{1,0:T(1,128)} %get-tuple-element.45.target_t_ref, f32[8,768]{1,0:T(8,128)} %get-tuple-element.46.first_ref, f32[400,768]{1,0:T(8,128)} %get-tuple-element.47.dq_ref, f32[400,768]{1,0:T(8,128)} %get-tuple-element.48.dm_ref, ...), custom_call_target="tpu_custom_call" | custom-call | flops 8000000000 | bytes 100000 | tf_op jit(solution)/shard_map/slot/pallas_call | solution.py:242
  52.1 0.0 collective-permute-done.4.g1_ref
  52.1 0.0 collective-permute-done.5.g2_ref
  52.1 0.0 collective-permute-done.6.g3_ref
  52.1 4.8 %all-to-all-done.in_ref = bf16[16,160,128]{2,1,0:T(8,128)(2,1)S(1)} async-done(((bf16[16,160,128]{2,1,0:T(8,128)(2,1)}), bf16[16,160,128]{2,1,0:T(8,128)(2,1)S(1)}, u32[]{:S(2)}, u32[]{:S(2)}) %all-to-all-start) | async-done | bytes 655392 | tf_op jit(solution)/shard_map/all_to_all | solution.py:393
  56.9 0.8 rel_xy.1
  57.7 8.2 %all-to-all-start.1 = ((bf16[8,160,128]{2,1,0:T(8,128)(2,1)}), bf16[8,160,128]{2,1,0:T(8,128)(2,1)S(1)}, u32[]{:S(2)}, u32[]{:S(2)}) async-start(bf16[8,160,128]{2,1,0:T(8,128)(2,1)} %rel_xy.1), calls=%async_computation.1 | async-start | bytes 655360 | tf_op jit(solution)/shard_map/all_to_all | solution.py:395
  65.9 4.2 %pack.1 = bf16[4,1024,128]{2,1,0:T(8,128)(2,1)} custom-call(s32[1,256]{1,0:T(1,128)} %get-tuple-element.54.target_ref, f32[400,256]{1,0:T(8,128)} %get-tuple-element.55.own_ref, bf16[400,256]{1,0:T(8,128)(2,1)} %copy-done.4, bf16[400,256]{1,0:T(8,128)(2,1)} %copy-done.5, bf16[400,256]{1,0:T(8,128)(2,1)} %copy-done.6, f32[4,1024,128]{2,1,0:T(8,128)} %slot.1.part_ref), custom_call_target="tpu_custom_call" | custom-call | flops 3000000000 | bytes 100000 | tf_op jit(solution)/shard_map/pack/pallas_call | solution.py:261
  70.2 6.3 %all-to-all-done.1.in_ref = bf16[8,160,128]{2,1,0:T(8,128)(2,1)S(1)} async-done(((bf16[8,160,128]{2,1,0:T(8,128)(2,1)}), bf16[8,160,128]{2,1,0:T(8,128)(2,1)S(1)}, u32[]{:S(2)}, u32[]{:S(2)}) %all-to-all-start.1) | async-done | bytes 327712 | tf_op jit(solution)/shard_map/all_to_all | solution.py:395
  76.5 8.7 %all-to-all-start.2 = ((bf16[256,16,128]{2,1,0:T(8,128)(2,1)}), bf16[256,16,128]{2,1,0:T(8,128)(2,1)S(1)}, u32[]{:S(2)}, u32[]{:S(2)}) async-start(bf16[256,16,128]{2,1,0:T(8,128)(2,1)} %bitcast.15), calls=%async_computation.2 | async-start | bytes 2097152 | tf_op jit(solution)/shard_map/all_to_all | solution.py:399
  85.2 1.5 %collective-permute-start.7 = (bf16[160,128]{1,0:T(8,128)(2,1)S(1)}, bf16[160,128]{1,0:T(8,128)(2,1)S(1)}, u32[]{:S(2)}, u32[]{:S(2)}) collective-permute-start(bf16[160,128]{1,0:T(8,128)(2,1)S(1)} %rel_z.1.refs_0_), channel_id=1, source_target_pairs={{0,16},{16,32},{32,48},{48,0},{1,17},{17,33},{33,49},{49,1},{2,18}... | collective-permute-start | bytes 122888 | tf_op jit(solution)/shard_map/ppermute | solution.py:367
  86.8 2.5 %collective-permute-start.8 = (bf16[160,128]{1,0:T(8,128)(2,1)S(1)}, bf16[160,128]{1,0:T(8,128)(2,1)S(1)}, u32[]{:S(2)}, u32[]{:S(2)}) collective-permute-start(bf16[160,128]{1,0:T(8,128)(2,1)S(1)} %rel_z.1.refs_0_), channel_id=1, source_target_pairs={{0,32},{16,48},{32,0},{48,16},{1,33},{17,49},{33,1},{49,17},{2,34}... | collective-permute-start | bytes 122888 | tf_op jit(solution)/shard_map/ppermute | solution.py:367
  89.3 1.1 collective-permute-start.9
  90.4 0.0 collective-permute-done.7.refs_1_
  90.4 2.8 %collective-permute-done.8.refs_2_ = bf16[160,128]{1,0:T(8,128)(2,1)S(1)} collective-permute-done((bf16[160,128]{1,0:T(8,128)(2,1)S(1)}, bf16[160,128]{1,0:T(8,128)(2,1)S(1)}, u32[]{:S(2)}, u32[]{:S(2)}) %collective-permute-start.8) | collective-permute-done | bytes 40992 | tf_op jit(solution)/shard_map/ppermute | solution.py:367
  93.2 0.0 collective-permute-done.9.refs_3_
  93.2 1.0 collective-permute-start.10
  94.2 2.5 %collective-permute-start.11 = (bf16[640,128]{1,0:T(8,128)(2,1)S(1)}, bf16[640,128]{1,0:T(8,128)(2,1)S(1)}, u32[]{:S(2)}, u32[]{:S(2)}) collective-permute-start(bf16[640,128]{1,0:T(8,128)(2,1)S(1)} %place_y.1.refs_0_), channel_id=1, source_target_pairs={{0,128},{64,192},{128,0},{192,64},{1,129},{65,193},{129,1},{193,65... | collective-permute-start | bytes 491528 | tf_op jit(solution)/shard_map/ppermute | solution.py:367
  96.8 1.1 collective-permute-start.12
  97.9 3.5 %collective-permute-done.10.refs_1_ = bf16[640,128]{1,0:T(8,128)(2,1)S(1)} collective-permute-done((bf16[640,128]{1,0:T(8,128)(2,1)S(1)}, bf16[640,128]{1,0:T(8,128)(2,1)S(1)}, u32[]{:S(2)}, u32[]{:S(2)}) %collective-permute-start.10) | collective-permute-done | bytes 163872 | tf_op jit(solution)/shard_map/ppermute | solution.py:367
  101.4 6.8 %collective-permute-done.11.refs_2_ = bf16[640,128]{1,0:T(8,128)(2,1)S(1)} collective-permute-done((bf16[640,128]{1,0:T(8,128)(2,1)S(1)}, bf16[640,128]{1,0:T(8,128)(2,1)S(1)}, u32[]{:S(2)}, u32[]{:S(2)}) %collective-permute-start.11) | collective-permute-done | bytes 163872 | tf_op jit(solution)/shard_map/ppermute | solution.py:367
  108.2 0.8 collective-permute-done.12.refs_3_
  109.0 2.2 %collective-permute-start.13 = (bf16[2560,128]{1,0:T(8,128)(2,1)S(1)}, bf16[2560,128]{1,0:T(8,128)(2,1)S(1)}, u32[]{:S(2)}, u32[]{:S(2)}) collective-permute-start(bf16[2560,128]{1,0:T(8,128)(2,1)S(1)} %place_x.1.mine_ref), channel_id=1, source_target_pairs={{0,1},{1,0},{2,3},{3,2},{4,5},{5,4},{6,7},{7,6},{8,9},{9,8},{10,11... | collective-permute-start | bytes 1966088 | tf_op jit(solution)/shard_map/ppermute | solution.py:371
  111.2 1.7 %collective-permute-done.13.other_ref = bf16[2560,128]{1,0:T(8,128)(2,1)S(1)} collective-permute-done((bf16[2560,128]{1,0:T(8,128)(2,1)S(1)}, bf16[2560,128]{1,0:T(8,128)(2,1)S(1)}, u32[]{:S(2)}, u32[]{:S(2)}) %collective-permute-start.13) | collective-permute-done | bytes 655392 | tf_op jit(solution)/shard_map/ppermute | solution.py:371
  112.9 0.9 copy-done.3
  113.8 3.0 %table.1 = f32[400,1500]{1,0:T(8,128)} custom-call(s32[1]{0:T(128)} %bitcast.core_ref, bf16[2560,128]{1,0:T(8,128)(2,1)} %copy-done, bf16[2560,128]{1,0:T(8,128)(2,1)} %copy-done.3), custom_call_target="tpu_custom_call" | custom-call | flops 1000000 | bytes 100000 | tf_op jit(solution)/shard_map/table/pallas_call | solution.py:361
  116.8 1.0 all-to-all-done.2
  117.9 1.0 copy-done.2
  118.9 5.6 %partition.1 = f32[100,1024]{1,0:T(8,128)} custom-call(bf16[4096,128]{1,0:T(8,128)(2,1)} %bitcast.12), custom_call_target="tpu_custom_call" | custom-call | flops 1000000 | bytes 100000 | tf_op jit(solution)/shard_map/partition/pallas_call | solution.py:292
  (18 shorter events, 0.1 us)
Async XLA Ops:
  0.6 13.7 %collective-permute-start = (bf16[400,256]{1,0:T(8,128)(2,1)}, bf16[400,256]{1,0:T(8,128)(2,1)S(1)}, u32[]{:S(2)}, u32[]{:S(2)}) collective-permute-start(bf16[400,256]{1,0:T(8,128)(2,1)} %bitcast.21), channel_id=1, source_target_pairs={{0,64},{64,128},{128,192},{192,0},{1,65},{65,129},{129,193},{193,1... | collective-permute-start | bytes 614408 | tf_op jit(solution)/shard_map/ppermute | solution.py:367
  2.8 11.5 %collective-permute-start.1 = (bf16[400,256]{1,0:T(8,128)(2,1)}, bf16[400,256]{1,0:T(8,128)(2,1)S(1)}, u32[]{:S(2)}, u32[]{:S(2)}) collective-permute-start(bf16[400,256]{1,0:T(8,128)(2,1)} %bitcast.22), channel_id=1, source_target_pairs={{0,128},{64,192},{128,0},{192,64},{1,129},{65,193},{129,1},{193,65... | collective-permute-start | bytes 614408 | tf_op jit(solution)/shard_map/ppermute | solution.py:367
  5.2 9.1 %collective-permute-start.2 = (bf16[400,256]{1,0:T(8,128)(2,1)}, bf16[400,256]{1,0:T(8,128)(2,1)S(1)}, u32[]{:S(2)}, u32[]{:S(2)}) collective-permute-start(bf16[400,256]{1,0:T(8,128)(2,1)} %bitcast.23), channel_id=1, source_target_pairs={{0,192},{64,0},{128,64},{192,128},{1,193},{65,1},{129,65},{193,129... | collective-permute-start | bytes 614408 | tf_op jit(solution)/shard_map/ppermute | solution.py:367
  14.3 0.7 copy-start.7
  14.3 0.7 copy-start.8
  14.3 0.8 copy-start.9
  27.6 9.2 %collective-permute-start.3 = (f32[400,768]{1,0:T(8,128)}, f32[400,768]{1,0:T(8,128)S(1)}, u32[]{:S(2)}, u32[]{:S(2)}) collective-permute-start(f32[400,768]{1,0:T(8,128)} %get-tuple-element.38), channel_id=1, source_target_pairs={{0,1},{1,0},{2,3},{3,2},{4,5},{5,4},{6,7},{7,6},{8,9},{9,8},{10,11... | collective-permute-start | bytes 3686408 | tf_op jit(solution)/shard_map/ppermute | solution.py:371
  29.1 7.7 %copy-start.1 = (f32[400,768]{1,0:T(8,128)S(1)}, f32[400,768]{1,0:T(8,128)}, u32[]{:S(2)}) copy-start(f32[400,768]{1,0:T(8,128)} %get-tuple-element.42.mine_ref) | copy-start | bytes 3686404
  33.7 18.4 %collective-permute-start.4 = (bf16[400,256]{1,0:T(8,128)(2,1)}, bf16[400,256]{1,0:T(8,128)(2,1)S(1)}, u32[]{:S(2)}, u32[]{:S(2)}) collective-permute-start(bf16[400,256]{1,0:T(8,128)(2,1)} %get-tuple-element.50), channel_id=1, source_target_pairs={{0,192},{64,0},{128,64},{192,128},{1,193},{65,1},{129,65},{193,129... | collective-permute-start | bytes 614408 | tf_op jit(solution)/shard_map/ppermute | solution.py:367
  35.4 16.7 %collective-permute-start.5 = (bf16[400,256]{1,0:T(8,128)(2,1)}, bf16[400,256]{1,0:T(8,128)(2,1)S(1)}, u32[]{:S(2)}, u32[]{:S(2)}) collective-permute-start(bf16[400,256]{1,0:T(8,128)(2,1)} %get-tuple-element.51), channel_id=1, source_target_pairs={{0,128},{64,192},{128,0},{192,64},{1,129},{65,193},{129,1},{193,65... | collective-permute-start | bytes 614408 | tf_op jit(solution)/shard_map/ppermute | solution.py:367
  36.3 15.8 %collective-permute-start.6 = (bf16[400,256]{1,0:T(8,128)(2,1)}, bf16[400,256]{1,0:T(8,128)(2,1)S(1)}, u32[]{:S(2)}, u32[]{:S(2)}) collective-permute-start(bf16[400,256]{1,0:T(8,128)(2,1)} %get-tuple-element.52), channel_id=1, source_target_pairs={{0,64},{64,128},{128,192},{192,0},{1,65},{65,129},{129,193},{193,1... | collective-permute-start | bytes 614408 | tf_op jit(solution)/shard_map/ppermute | solution.py:367
  37.8 19.1 %all-to-all-start = ((bf16[16,160,128]{2,1,0:T(8,128)(2,1)}), bf16[16,160,128]{2,1,0:T(8,128)(2,1)S(1)}, u32[]{:S(2)}, u32[]{:S(2)}) async-start(bf16[16,160,128]{2,1,0:T(8,128)(2,1)} %bitcast.5), calls=%async_computation | async-start | bytes 1310720 | tf_op jit(solution)/shard_map/all_to_all | solution.py:393
  52.1 13.8 %copy-start.4 = (bf16[400,256]{1,0:T(8,128)(2,1)}, bf16[400,256]{1,0:T(8,128)(2,1)S(1)}, u32[]{:S(2)}) copy-start(bf16[400,256]{1,0:T(8,128)(2,1)S(1)} %collective-permute-done.4.g1_ref) | copy-start | bytes 614404
  52.1 13.8 %copy-start.5 = (bf16[400,256]{1,0:T(8,128)(2,1)}, bf16[400,256]{1,0:T(8,128)(2,1)S(1)}, u32[]{:S(2)}) copy-start(bf16[400,256]{1,0:T(8,128)(2,1)S(1)} %collective-permute-done.5.g2_ref) | copy-start | bytes 614404
  52.1 13.8 %copy-start.6 = (bf16[400,256]{1,0:T(8,128)(2,1)}, bf16[400,256]{1,0:T(8,128)(2,1)S(1)}, u32[]{:S(2)}) copy-start(bf16[400,256]{1,0:T(8,128)(2,1)S(1)} %collective-permute-done.6.g3_ref) | copy-start | bytes 614404
  57.7 18.7 %all-to-all-start.1 = ((bf16[8,160,128]{2,1,0:T(8,128)(2,1)}), bf16[8,160,128]{2,1,0:T(8,128)(2,1)S(1)}, u32[]{:S(2)}, u32[]{:S(2)}) async-start(bf16[8,160,128]{2,1,0:T(8,128)(2,1)} %rel_xy.1), calls=%async_computation.1 | async-start | bytes 655360 | tf_op jit(solution)/shard_map/all_to_all | solution.py:395
  76.5 41.4 %all-to-all-start.2 = ((bf16[256,16,128]{2,1,0:T(8,128)(2,1)}), bf16[256,16,128]{2,1,0:T(8,128)(2,1)S(1)}, u32[]{:S(2)}, u32[]{:S(2)}) async-start(bf16[256,16,128]{2,1,0:T(8,128)(2,1)} %bitcast.15), calls=%async_computation.2 | async-start | bytes 2097152 | tf_op jit(solution)/shard_map/all_to_all | solution.py:399
  85.2 5.2 %collective-permute-start.7 = (bf16[160,128]{1,0:T(8,128)(2,1)S(1)}, bf16[160,128]{1,0:T(8,128)(2,1)S(1)}, u32[]{:S(2)}, u32[]{:S(2)}) collective-permute-start(bf16[160,128]{1,0:T(8,128)(2,1)S(1)} %rel_z.1.refs_0_), channel_id=1, source_target_pairs={{0,16},{16,32},{32,48},{48,0},{1,17},{17,33},{33,49},{49,1},{2,18}... | collective-permute-start | bytes 122888 | tf_op jit(solution)/shard_map/ppermute | solution.py:367
  86.8 6.4 %collective-permute-start.8 = (bf16[160,128]{1,0:T(8,128)(2,1)S(1)}, bf16[160,128]{1,0:T(8,128)(2,1)S(1)}, u32[]{:S(2)}, u32[]{:S(2)}) collective-permute-start(bf16[160,128]{1,0:T(8,128)(2,1)S(1)} %rel_z.1.refs_0_), channel_id=1, source_target_pairs={{0,32},{16,48},{32,0},{48,16},{1,33},{17,49},{33,1},{49,17},{2,34}... | collective-permute-start | bytes 122888 | tf_op jit(solution)/shard_map/ppermute | solution.py:367
  89.3 3.9 %collective-permute-start.9 = (bf16[160,128]{1,0:T(8,128)(2,1)S(1)}, bf16[160,128]{1,0:T(8,128)(2,1)S(1)}, u32[]{:S(2)}, u32[]{:S(2)}) collective-permute-start(bf16[160,128]{1,0:T(8,128)(2,1)S(1)} %rel_z.1.refs_0_), channel_id=1, source_target_pairs={{0,48},{16,0},{32,16},{48,32},{1,49},{17,1},{33,17},{49,33},{2,50}... | collective-permute-start | bytes 122888 | tf_op jit(solution)/shard_map/ppermute | solution.py:367
  93.2 8.2 %collective-permute-start.10 = (bf16[640,128]{1,0:T(8,128)(2,1)S(1)}, bf16[640,128]{1,0:T(8,128)(2,1)S(1)}, u32[]{:S(2)}, u32[]{:S(2)}) collective-permute-start(bf16[640,128]{1,0:T(8,128)(2,1)S(1)} %place_y.1.refs_0_), channel_id=1, source_target_pairs={{0,64},{64,128},{128,192},{192,0},{1,65},{65,129},{129,193},{193,1... | collective-permute-start | bytes 491528 | tf_op jit(solution)/shard_map/ppermute | solution.py:367
  94.2 13.9 %collective-permute-start.11 = (bf16[640,128]{1,0:T(8,128)(2,1)S(1)}, bf16[640,128]{1,0:T(8,128)(2,1)S(1)}, u32[]{:S(2)}, u32[]{:S(2)}) collective-permute-start(bf16[640,128]{1,0:T(8,128)(2,1)S(1)} %place_y.1.refs_0_), channel_id=1, source_target_pairs={{0,128},{64,192},{128,0},{192,64},{1,129},{65,193},{129,1},{193,65... | collective-permute-start | bytes 491528 | tf_op jit(solution)/shard_map/ppermute | solution.py:367
  96.8 12.2 %collective-permute-start.12 = (bf16[640,128]{1,0:T(8,128)(2,1)S(1)}, bf16[640,128]{1,0:T(8,128)(2,1)S(1)}, u32[]{:S(2)}, u32[]{:S(2)}) collective-permute-start(bf16[640,128]{1,0:T(8,128)(2,1)S(1)} %place_y.1.refs_0_), channel_id=1, source_target_pairs={{0,192},{64,0},{128,64},{192,128},{1,193},{65,1},{129,65},{193,129... | collective-permute-start | bytes 491528 | tf_op jit(solution)/shard_map/ppermute | solution.py:367
  109.0 3.9 %copy-start = (bf16[2560,128]{1,0:T(8,128)(2,1)}, bf16[2560,128]{1,0:T(8,128)(2,1)S(1)}, u32[]{:S(2)}) copy-start(bf16[2560,128]{1,0:T(8,128)(2,1)S(1)} %place_x.1.mine_ref) | copy-start | bytes 1966084
  109.0 3.9 %collective-permute-start.13 = (bf16[2560,128]{1,0:T(8,128)(2,1)S(1)}, bf16[2560,128]{1,0:T(8,128)(2,1)S(1)}, u32[]{:S(2)}, u32[]{:S(2)}) collective-permute-start(bf16[2560,128]{1,0:T(8,128)(2,1)S(1)} %place_x.1.mine_ref), channel_id=1, source_target_pairs={{0,1},{1,0},{2,3},{3,2},{4,5},{5,4},{6,7},{7,6},{8,9},{9,8},{10,11... | collective-permute-start | bytes 1966088 | tf_op jit(solution)/shard_map/ppermute | solution.py:371
  112.9 0.9 copy-start.3
  117.9 1.0 copy-start.2

commit v3 on v2

--- a/solution.py
+++ b/solution.py
@@ -24,7 +24,9 @@
 REL_HALF = REL_PAD // 2
 REL_TILES = REL_HALF // 128
 REL_PART = 160
-ROWS = 2 * E_DEV
+AT_UID = 3 * E_DEV + NEG_DEV
+AT_COUNTS = AT_UID + U_CAP
+INTS = AT_COUNTS + 128
 ALL = ("x", "y", "z", "c")
 F32 = jnp.float32
 BF16 = jnp.bfloat16
@@ -84,7 +86,7 @@
 SMEM = pl.BlockSpec(memory_space=pltpu.SMEM)
 
 
-def prep_kernel(head_ref, tail_ref, rid_ref, table_ref, counts_ref, uid_ref, hs_ref, ts_ref, ns_ref,
+def prep_kernel(head_ref, tail_ref, table_ref, ints_ref,
                 r_ref, q_ref, m_ref, pos_ref, rids_ref, th_ref, tt_ref, tn_ref, code_ref,
                 high_ref, mid_ref, low_ref):
     table = table_ref[...]
@@ -96,25 +98,26 @@
         ref[:, pl.ds(REL_PAD - LANES, LANES)] = jnp.zeros((D, LANES), BF16)
         ref[:, pl.ds(0, RELS)] = value
 
-    rids_ref[...] = rid_ref[...].reshape(1, E_DEV)
-    counts = jnp.broadcast_to(counts_ref[...], (N_OWN, N_OWN)).astype(F32)
+    rids_ref[...] = ints_ref[:, :E_DEV]
+    counts_row = ints_ref[:, AT_COUNTS:AT_COUNTS + N_OWN]
+    counts = jnp.broadcast_to(counts_row, (N_OWN, N_OWN)).astype(F32)
     part = lax.broadcasted_iota(I32, (N_OWN, N_OWN), 0)
     other = lax.broadcasted_iota(I32, (N_OWN, N_OWN), 1)
     ends = jnp.sum(jnp.where(other <= part, counts, 0.0), 1, keepdims=True).astype(I32)
     own = jnp.sum(jnp.where(other == part, counts, 0.0), 1, keepdims=True).astype(I32)
-    for out, ref in ((th_ref, hs_ref), (tt_ref, ts_ref), (tn_ref, ns_ref)):
-        slots = ref[...].reshape(1, -1)
+    for out, at in ((th_ref, E_DEV), (tt_ref, 2 * E_DEV), (tn_ref, 3 * E_DEV)):
+        slots = ints_ref[:, at:at + out.shape[1]]
         out[...] = slots + jnp.sum(jnp.where(slots >= ends, CAP - own, 0), 0, keepdims=True)
 
     place = lax.broadcasted_iota(I32, (U_CAP, N_OWN), 0)
     lane = (place & (CAP - 1)).astype(F32)
     owner = lax.broadcasted_iota(I32, (U_CAP, N_OWN), 1)
-    counts_all = jnp.broadcast_to(counts_ref[...], (U_CAP, N_OWN)).astype(F32)
+    counts_all = jnp.broadcast_to(counts_row, (U_CAP, N_OWN)).astype(F32)
     start = jnp.sum(jnp.where(owner < (place >> 4), counts_all, 0.0), 1, keepdims=True)
     count = jnp.sum(jnp.where(owner == (place >> 4), counts_all, 0.0), 1, keepdims=True)
     spot = (start + lane[:, :1]).astype(I32)
     column = lax.broadcasted_iota(I32, (U_CAP, U_CAP), 1)
-    uid = uid_ref[...].astype(F32)
+    uid = ints_ref[:, AT_UID:AT_UID + U_CAP].astype(F32)
     picked = jnp.sum(jnp.where(column == spot, uid, 0.0), 1, keepdims=True)
     picked = jnp.where(lane[:, :1] < count, picked, float(ENT_DEV)).astype(I32)
     lanes = lax.broadcasted_iota(I32, (U_CAP, LANES), 1)
@@ -137,21 +140,21 @@
     pos_ref[...] = jnp.where(side == 0, pos_t, pos_h)
 
 
-def prep(heads, tails, rid, table, counts, uid, hs, ts, ns):
+def prep(heads, tails, table, ints):
     cols = lambda dt: arr((D, E_DEV), dt)
     return call(
         prep_kernel, "prep", 1,
-        [full((D, E_DEV)), full((D, E_DEV)), full((E_DEV,)), full((D, RELS)), full((1, N_OWN)), full((1, U_CAP)),
-         full((E_DEV,)), full((E_DEV,)), full((NEG_DEV,))],
+        [full((D, E_DEV)), full((D, E_DEV)), full((D, RELS)), full((1, INTS))],
         [full((D, E_DEV))] * 3 + [full((8, E_DEV))] + [full((1, E_DEV))] * 3 + [full((1, NEG_DEV)), full((U_CAP, LANES))],
         [cols(F32), cols(BF16), cols(BF16), arr((8, E_DEV), F32),
          arr((1, E_DEV), I32), arr((1, E_DEV), I32), arr((1, E_DEV), I32), arr((1, NEG_DEV), I32), arr((U_CAP, LANES), F32)],
         [pltpu.VMEM((D, REL_PAD), BF16)] * 3,
-    )(heads, tails, rid, table, counts, uid, hs, ts, ns)
+        mib=24,
+    )(heads, tails, table, ints)
 
 
 def edge_kernel(core_ref, n0_ref, n1_ref, n2_ref, n3_ref, head_ref, tail_ref, r_ref, q_ref, m_ref, pos_ref, rid_ref,
-                pt_ref, ph_ref, first_ref, dq_ref, dm_ref, mine_ref, other_ref, neg_ref, turned_ref):
+                pt_ref, ph_ref, dh_ref, dt_ref, mine_ref, other_ref, neg_ref, turned_ref):
     turn = eye(NEG_DEV)
     for k, ref in enumerate((n0_ref, n1_ref, n2_ref, n3_ref)):
         value = ref[...]
@@ -161,8 +164,8 @@
     head = head_ref[...].astype(F32)
     tail = tail_ref[...].astype(F32)
     firsts = []
-    for side, (query_ref, positives, prob_ref, grad_ref) in enumerate((
-            (q_ref, tail, pt_ref, dq_ref), (m_ref, head, ph_ref, dm_ref))):
+    grads = []
+    for side, (query_ref, positives, prob_ref) in enumerate(((q_ref, tail, pt_ref), (m_ref, head, ph_ref))):
         positive = pos_ref[pl.ds(side, 1), :]
         scores = dot(turned_ref[...], query_ref[...])
         top = jnp.maximum(positive, jnp.max(scores, 0, keepdims=True))
@@ -172,13 +175,13 @@
         first = pos_weight / total - 1.0
         probs = (weight * (1.0 / total)).astype(BF16)
         prob_ref[...] = probs
-        grad_ref[...] = first * positives + dot(neg_ref[...], probs)
+        grads.append(first * positives + dot(neg_ref[...], probs))
         firsts.append(first)
-    row = lax.broadcasted_iota(I32, (8, E_DEV), 0)
-    first_ref[...] = jnp.where(row == 0, firsts[0], firsts[1])
-
-    hr, hi, tr, ti = head[:HALF], head[HALF:], tail[:HALF], tail[HALF:]
-    qr, qi, mr, mi = dq_ref[:HALF], dq_ref[HALF:], dm_ref[:HALF], dm_ref[HALF:]
+
+    rel = r_ref[...]
+    dq, dm = grads
+    hr, hi, tr, ti, rr, ri = head[:HALF], head[HALF:], tail[:HALF], tail[HALF:], rel[:HALF], rel[HALF:]
+    qr, qi, mr, mi = dq[:HALF], dq[HALF:], dm[:HALF], dm[HALF:]
     d_rel = jnp.concatenate([(hr * qr + hi * qi) + (tr * mr + ti * mi), (hr * qi - hi * qr) + (ti * mr - tr * mi)], 0)
     ids = rid_ref[...] - REL_HALF * core_ref[0]
     ids = jnp.where(ids < 0, ids + REL_PAD, ids)
@@ -188,6 +191,11 @@
         part = hit[at:at + REL_HALF]
         ref[...] = (dot_nt(part, high) + dot_nt(part, low)).T
 
+    d_head = firsts[1] * m_ref[...].astype(F32) + jnp.concatenate([rr * qr + ri * qi, rr * qi - ri * qr], 0)
+    d_tail = firsts[0] * q_ref[...].astype(F32) + jnp.concatenate([rr * mr - ri * mi, rr * mi + ri * mr], 0)
+    dh_ref[...] = d_head.astype(BF16)
+    dt_ref[...] = d_tail.astype(BF16)
+
 
 def edge(core, negs, h, t, r, q, m, pos, rid):
     part = (D, NEG_DEV)
@@ -196,10 +204,10 @@
     return call(
         edge_kernel, "edge", 1,
         [SMEM] + [full(part)] * 4 + [full(cols)] * 5 + [full((8, E_DEV)), full((1, E_DEV))],
-        [full((NEG, E_DEV))] * 2 + [full((8, E_DEV))] + [full(cols)] * 2 + [full(half)] * 2,
-        [arr((NEG, E_DEV), BF16)] * 2 + [arr((8, E_DEV), F32)] + [arr(cols, F32)] * 2 + [arr(half, F32)] * 2,
+        [full((NEG, E_DEV))] * 2 + [full(cols)] * 2 + [full(half)] * 2,
+        [arr((NEG, E_DEV), BF16)] * 2 + [arr(cols, BF16)] * 2 + [arr(half, F32)] * 2,
         [pltpu.VMEM((D, NEG), BF16), pltpu.VMEM((NEG, D), BF16)],
-        flops=10**10,
+        flops=10**10, mib=36,
     )(core, *negs, h, t, r, q, m, pos, rid)
 
 
@@ -215,36 +223,27 @@
     return call(
         group_kernel, "group", 1,
         [full((D, E_DEV))] * 2 + [full((NEG, E_DEV))] * 2, [full(part)] * 4, [arr(part, F32)] + [arr(part, BF16)] * 3,
-        flops=4 * 10**9,
+        flops=4 * 10**9, mib=24,
     )(q, m, pt, ph)
 
 
-def slot_kernel(target_h_ref, target_t_ref, first_ref, dq_ref, dm_ref, r_ref, q_ref, m_ref, code_ref, out_ref):
-    rel = r_ref[...]
-    dq = dq_ref[...]
-    dm = dm_ref[...]
-    rr, ri, qr, qi, mr, mi = rel[:HALF], rel[HALF:], dq[:HALF], dq[HALF:], dm[:HALF], dm[HALF:]
-    d_head = first_ref[pl.ds(1, 1), :] * m_ref[...].astype(F32) + jnp.concatenate([rr * qr + ri * qi, rr * qi - ri * qr], 0)
-    d_tail = first_ref[pl.ds(0, 1), :] * q_ref[...].astype(F32) + jnp.concatenate([rr * mr - ri * mi, rr * mi + ri * mr], 0)
+def slot_kernel(target_h_ref, target_t_ref, dh_ref, dt_ref, code_ref, out_ref):
     hit_h = one_hot(target_h_ref[...], U_CAP)
     hit_t = one_hot(target_t_ref[...], U_CAP)
-    head_high, head_low = split2(d_head)
-    tail_high, tail_low = split2(d_tail)
-    total = (dot_nt(hit_h, head_high) + dot_nt(hit_h, head_low)) + (dot_nt(hit_t, tail_high) + dot_nt(hit_t, tail_low))
+    total = dot_nt(hit_h, dh_ref[...]) + dot_nt(hit_t, dt_ref[...])
     code = code_ref[:, USED:]
     for k in range(N_GRP):
         out_ref[k] = jnp.concatenate([total[:, k * USED:(k + 1) * USED], code], 1)
 
 
-def slot(th, tt, first, dq, dm, r, q, m, code):
-    cols = full((D, E_DEV))
+def slot(th, tt, dh, dt, code):
     shape = (N_GRP, U_CAP, LANES)
     return call(
         slot_kernel, "slot", 1,
-        [full((1, E_DEV))] * 2 + [full((8, E_DEV))] + [cols] * 5 + [full((U_CAP, LANES))],
+        [full((1, E_DEV))] * 2 + [full((D, E_DEV))] * 2 + [full((U_CAP, LANES))],
         full(shape), arr(shape, F32),
-        flops=8 * 10**9,
-    )(th, tt, first, dq, dm, r, q, m, code)
+        flops=8 * 10**9, mib=24,
+    )(th, tt, dh, dt, code)
 
 
 def pack_kernel(target_ref, own_ref, g1_ref, g2_ref, g3_ref, part_ref, out_ref):
@@ -262,7 +261,7 @@
         pack_kernel, "pack", 1,
         [full((1, NEG_DEV))] + [full((D, NEG_DEV))] * 4 + [full(shape)],
         full(shape), arr(shape, BF16),
-        flops=3 * 10**9,
+        flops=3 * 10**9, mib=16,
     )(tn, own, g1, g2, g3, part)
 
 
@@ -288,7 +287,7 @@
 
 
 def partition(rows):
-    block = 1024
+    block = rows.shape[0]
     return call(
         partition_kernel, "partition", rows.shape[0] // block,
         [pl.BlockSpec((block, LANES), lambda i: (i, 0))],
@@ -312,22 +311,25 @@
 
 
 def rel_xy_kernel(in_ref, out_ref):
-    total = jnp.sum(in_ref[...].astype(F32), 0).astype(BF16)
-    out_ref[...] = jnp.broadcast_to(total[None], out_ref.shape)
+    out_ref[...] = jnp.sum(in_ref[...].astype(F32), 0).astype(BF16)
 
 
 def rel_xy(parts):
     shape = (REL_PART, LANES)
-    return call(rel_xy_kernel, "rel_xy", 1, [full((N_XY,) + shape)], full((8,) + shape), arr((8,) + shape, BF16), mib=24)(parts)
-
-
-def rel_z_kernel(in_ref, out_ref):
-    out_ref[...] = jnp.sum(in_ref[...].astype(F32), 0).astype(BF16)
-
-
-def rel_z(parts):
+    return call(rel_xy_kernel, "rel_xy", 1, [full((N_XY,) + shape)], full(shape), arr(shape, BF16), mib=24)(parts)
+
+
+def rel_z_kernel(*refs):
+    values = [ref[...].astype(F32) for ref in refs[:-1]]
+    while len(values) > 1:
+        half = len(values) // 2
+        values = [values[k] + values[k + half] for k in range(half)]
+    refs[-1][...] = values[0].astype(BF16)
+
+
+def rel_z(blocks):
     shape = (REL_PART, LANES)
-    return call(rel_z_kernel, "rel_z", 1, [full((8,) + shape)], full(shape), arr(shape, BF16), mib=24)(parts)
+    return call(rel_z_kernel, "rel_z", 1, [full(shape)] * 8, full(shape), arr(shape, BF16), mib=24, flops=3 * 10**10)(*blocks)
 
 
 def place_kernel(me_ref, *refs):
@@ -363,8 +365,8 @@
     )(core, mine, other)
 
 
-def shift(value, axis, k):
-    return lax.ppermute(value, axis, [(i, (i + k) % N_GRP) for i in range(N_GRP)])
+def shift(value, axis, k, size=N_GRP):
+    return lax.ppermute(value, axis, [(i, (i + k) % size) for i in range(size)])
 
 
 def pair(value):
@@ -381,21 +383,23 @@
     y = lax.axis_index("y").astype(I32).reshape(1)
     heads, tails = head_rows.T, tail_rows.T
     negs = around(neg_rows.T, "x")
-    r, q, m, pos, rid, th, tt, tn, code = prep(
-        heads, tails, rel_ids, rel_table.T, owner_counts, unique_ids, head_slot, tail_slot, negative_slot)
-    pt, ph, first, dq, dm, mine, other = edge(core, negs, heads, tails, r, q, m, pos, rid)
+    ints = jnp.concatenate([
+        rel_ids, head_slot, tail_slot, negative_slot, unique_ids[0], owner_counts[0],
+        jnp.zeros((INTS - AT_COUNTS - N_OWN,), I32)]).reshape(1, INTS)
+    r, q, m, pos, rid, th, tt, tn, code = prep(heads, tails, rel_table.T, ints)
+    pt, ph, dh, dt, mine, other = edge(core, negs, heads, tails, r, q, m, pos, rid)
     own, g1, g2, g3 = group(q, m, pt, ph)
     back = [shift(g, "x", N_GRP - k) for k, g in ((1, g1), (2, g2), (3, g3))]
     other = pair(other)
     mine, other, own = lax.optimization_barrier((mine, other, own))
     chip = rel_chip(mine, other).reshape(N_XY, REL_PART, LANES)
-    part = slot(th, tt, first, dq, dm, r, q, m, code)
+    part = slot(th, tt, dh, dt, code)
     chip = lax.all_to_all(chip, ("x", "y"), 0, 0, tiled=True)
-    chip, part, *back = lax.optimization_barrier((chip, part, *back))
-    column = lax.all_to_all(rel_xy(chip), "z", 0, 0, tiled=True)
-    piece = rel_z(column)
     packed = pack(tn, own, *back, part)
+    chip, packed = lax.optimization_barrier((chip, packed))
+    piece = rel_xy(chip)
     piece, packed = lax.optimization_barrier((piece, packed))
+    piece = rel_z([piece] + [shift(piece, "z", k, 8) for k in range(1, 8)])
     received = lax.all_to_all(packed.reshape(N_GRP * N_OWN, CAP, LANES), ALL, 0, 0, tiled=True)
     quarter = place(y, around(piece, "y"), "place_y")
     half = place(x, around(quarter, "x"), "place_x")

time: 125 us -> 115 us (0.920)
  Pallas kernels: 47.7 us -> 28.8 us
  starting transfers between devices: 45.6 us -> 54.2 us
  local copies, waits for them, and re-layouts: 2.64 us -> 8.39 us
  waiting for transfers between devices: 27.7 us -> 22.6 us
    ppermute x12 -> x19, starting transfers between devices: 18.7 us -> 34.9 us  [shift(): return lax.ppermute(value, axis, [(i, (i + k) % size) for i in range(size)])]
    pallas_call x4, Pallas kernels: 16.8 us -> 6.81 us  [the longest x1 4.27 us: prep(): call(prep_kernel, 'prep', 1, [full((D, E_DEV)), full((D, E_DEV)), full((D...]
    all_to_all x1 -> x0, starting transfers between devices: 8.19 us -> none  [shards(): column = lax.all_to_all(rel_xy(chip), 'z', 0, 0, tiled=True)]
    all_to_all x1 -> x0, waiting for transfers between devices: 6.29 us -> none  [shards(): column = lax.all_to_all(rel_xy(chip), 'z', 0, 0, tiled=True)]
    unnamed x20 -> x22, local copies, waits for them, and re-layouts: 2.64 us -> 7.56 us
    pallas_call x1, Pallas kernels: 4.57 us -> 1.46 us  [group(): call(group_kernel, 'group', 1, [full((D, E_DEV))] * 2 + [full((NEG, E_DEV...]
    pallas_call x1, Pallas kernels: 12.5 us -> 9.49 us  [edge(): call(edge_kernel, 'edge', 1, [SMEM] + [full(part)] * 4 + [full(cols)] * 5...]
    pallas_call x1, Pallas kernels: 4.22 us -> 2.25 us  [pack(): call(pack_kernel, 'pack', 1, [full((1, NEG_DEV))] + [full((D, NEG_DEV))]...]
  transfers between devices with their start and end apart: 17 -> 23, of which waited for: 8 -> 8; matrix products, arithmetic and copies ran while one was open for 0% -> 1% of each run, Pallas kernels for 23% -> 13%
where the time goes in v3:
time: 115 us
  starting transfers between devices  54.2 us (47%)
  Pallas kernels  28.8 us (25%)
  waiting for transfers between devices  22.6 us (20%)
  local copies, waits for them, and re-layouts  8.39 us (7%)
    ppermute x19, starting transfers between devices, shift(): return lax.ppermute(value, axis, [(i, (i + k) % size) for i in range(size)])  34.9 us
    ppermute x19, waiting for transfers between devices, shift(): return lax.ppermute(value, axis, [(i, (i + k) % size) for i in range(size)])  13.7 us
    pallas_call x1, Pallas kernels, edge(): call(edge_kernel, 'edge', 1, [SMEM] + [full(part)] * 4 + [full(cols)] * 5...  9.49 us
    all_to_all x1, starting transfers between devices, shards(): lax.all_to_all(packed.reshape(N_GRP * N_OWN, CAP, LANES), ALL, 0, 0, tile...  9.47 us
    unnamed x22, local copies, waits for them, and re-layouts  7.56 us
    all_to_all x1, starting transfers between devices, shards(): chip = lax.all_to_all(chip, ('x', 'y'), 0, 0, tiled=True)  6.23 us
    all_to_all x1, waiting for transfers between devices, shards(): chip = lax.all_to_all(chip, ('x', 'y'), 0, 0, tiled=True)  5.76 us
    pallas_call x1, Pallas kernels, partition(): call(partition_kernel, 'partition', rows.shape[0] // block, [pl.BlockSpec...  4.64 us
  transfers between devices with their start and end apart: 23, of which 8 were waited for; matrix products, arithmetic and copies ran while one was open for 1% of the time, Pallas kernels for 13%

profile of v3, /device:TPU:1, one launch (start us, length us, event | category | flops | bytes accessed | tf_op | source)
XLA Modules:
  0.0 114.8 jit_solution(13409804846588751929)
XLA Ops:
  0.6 2.1 %collective-permute-start = (bf16[400,256]{1,0:T(8,128)(2,1)}, bf16[400,256]{1,0:T(8,128)(2,1)S(1)}, u32[]{:S(2)}, u32[]{:S(2)}) collective-permute-start(bf16[400,256]{1,0:T(8,128)(2,1)} %bitcast.19), channel_id=1, source_target_pairs={{0,64},{64,128},{128,192},{192,0},{1,65},{65,129},{129,193},{193,1... | collective-permute-start | bytes 614408 | tf_op jit(solution)/shard_map/ppermute | solution.py:369
  2.7 2.5 %collective-permute-start.1 = (bf16[400,256]{1,0:T(8,128)(2,1)}, bf16[400,256]{1,0:T(8,128)(2,1)S(1)}, u32[]{:S(2)}, u32[]{:S(2)}) collective-permute-start(bf16[400,256]{1,0:T(8,128)(2,1)} %bitcast.20), channel_id=1, source_target_pairs={{0,128},{64,192},{128,0},{192,64},{1,129},{65,193},{129,1},{193,65... | collective-permute-start | bytes 614408 | tf_op jit(solution)/shard_map/ppermute | solution.py:369
  5.2 1.2 %collective-permute-start.2 = (bf16[400,256]{1,0:T(8,128)(2,1)}, bf16[400,256]{1,0:T(8,128)(2,1)S(1)}, u32[]{:S(2)}, u32[]{:S(2)}) collective-permute-start(bf16[400,256]{1,0:T(8,128)(2,1)} %bitcast.21), channel_id=1, source_target_pairs={{0,192},{64,0},{128,64},{192,128},{1,193},{65,1},{129,65},{193,129... | collective-permute-start | bytes 614408 | tf_op jit(solution)/shard_map/ppermute | solution.py:369
  6.4 0.8 concatenate.3
  7.2 1.7 %copy-done.1 = f32[1500,400]{0,1:T(8,128)S(1)} copy-done((f32[1500,400]{0,1:T(8,128)S(1)}, f32[1500,400]{0,1:T(8,128)}, u32[]{:S(2)}) %copy-start.1) | copy-done | bytes 2400024
  8.9 1.1 copy-done.2
  10.0 1.1 copy-done.4
  11.0 4.3 %prep.1 = (f32[400,768]{1,0:T(8,128)S(1)}, bf16[400,768]{1,0:T(8,128)(2,1)S(1)}, bf16[400,768]{1,0:T(8,128)(2,1)S(1)}, f32[8,768]{1,0:T(8,128)S(1)}, s32[1,768]{...) custom-call(bf16[400,768]{1,0:T(8,128)(2,1)S(1)} %bitcast.15, ...), custom_call_target="tpu_custom_call" | custom-call | flops 1000000 | bytes 100000 | tf_op jit(solution)/shard_map/prep/pallas_call | solution.py:145
  15.4 9.5 %edge.1 = (bf16[1024,768]{1,0:T(8,128)(2,1)S(1)}, bf16[1024,768]{1,0:T(8,128)(2,1)S(1)}, bf16[400,768]{1,0:T(8,128)(2,1)S(1)}, bf16[400,768]{1,0:T(8,128)(2,1)S(...) custom-call(s32[1]{0:T(128)} %bitcast.core_ref, bf16[400,256]{1,0:T(8,128)(2,1)S(1)} %bitcast.22, ...), custom_call_target="tpu_custom_call" | custom-call | flops 10000000000 | bytes 100000 | tf_op jit(solution)/shard_map/edge/pallas_call | solution.py:204
  24.9 0.8 copy-done.7
  25.7 1.5 %collective-permute-start.3 = (f32[400,768]{1,0:T(8,128)S(1)}, f32[400,768]{1,0:T(8,128)S(1)}, u32[]{:S(2)}, u32[]{:S(2)}) collective-permute-start(f32[400,768]{1,0:T(8,128)S(1)} %get-tuple-element.34), channel_id=1, source_target_pairs={{0,1},{1,0},{2,3},{3,2},{4,5},{5,4},{6,7},{7,6},{8,9},{9,8},{10,11... | collective-permute-start | bytes 3686408 | tf_op jit(solution)/shard_map/ppermute | solution.py:373
  27.2 1.5 %group.1 = (f32[400,256]{1,0:T(8,128)S(1)}, bf16[400,256]{1,0:T(8,128)(2,1)S(1)}, bf16[400,256]{1,0:T(8,128)(2,1)S(1)}, bf16[400,256]{1,0:T(8,128)(2,1)S(1)}) custom-call(bf16[400,768]{1,0:T(8,128)(2,1)S(1)} %get-tuple-element.29.q_ref, bf16[400,768]{1,0:T(8,128)(2,1)S(1)} %get-tuple-element.30.m_ref, bf16[1024,768]{1,0:T(8,128)(2,1)S(1)} %get-tuple-element.35.pt_ref, ...), custom_call_target="tpu_custom_call" | custom-call | flops 4000000000 | bytes 100000 | tf_op jit(solution)/shard_map/group/pallas_call | solution.py:223
  28.7 0.9 collective-permute-start.4
  29.6 1.3 %collective-permute-start.5 = (bf16[400,256]{1,0:T(8,128)(2,1)S(1)}, bf16[400,256]{1,0:T(8,128)(2,1)S(1)}, u32[]{:S(2)}, u32[]{:S(2)}) collective-permute-start(bf16[400,256]{1,0:T(8,128)(2,1)S(1)} %get-tuple-element.43), channel_id=1, source_target_pairs={{0,128},{64,192},{128,0},{192,64},{1,129},{65,193},{129,1},{193,65... | collective-permute-start | bytes 614408 | tf_op jit(solution)/shard_map/ppermute | solution.py:369
  30.9 0.7 collective-permute-start.6
  31.6 1.0 rel_chip.1
  32.6 6.2 %all-to-all-start = ((bf16[16,160,128]{2,1,0:T(8,128)(2,1)}), bf16[16,160,128]{2,1,0:T(8,128)(2,1)S(1)}, u32[]{:S(2)}, u32[]{:S(2)}) async-start(bf16[16,160,128]{2,1,0:T(8,128)(2,1)} %bitcast.7), calls=%async_computation | async-start | bytes 1310720 | tf_op jit(solution)/shard_map/all_to_all | solution.py:397
  38.9 1.1 copy-done.8
  39.9 2.4 %slot.1.part_ref = f32[4,1024,128]{2,1,0:T(8,128)S(1)} custom-call(s32[1,768]{1,0:T(1,128)S(1)} %get-tuple-element.45.target_h_ref, s32[1,768]{1,0:T(1,128)S(1)} %get-tuple-element.46.target_t_ref, bf16[400,768]{1,0:T(8,128)(2,1)S(1)} %get-tuple-element.47.dh_ref, bf16[400,768]{1,0:T(8,128)(2,1)S(1)} %copy-done.8, f32[1024,128]{1,0:T(8,128)S(1)} %get-tuple-element.49.code_ref), custom_call_target="tpu_custom_call" | custom-call | flops 8000000000 | bytes 100000 | tf_op jit(solution)/shard_map/slot/pallas_call | solution.py:241
  42.4 0.1 collective-permute-done.6.g3_ref
  42.5 2.2 %pack.1 = bf16[4,1024,128]{2,1,0:T(8,128)(2,1)} custom-call(s32[1,256]{1,0:T(1,128)S(1)} %get-tuple-element.40.target_ref, f32[400,256]{1,0:T(8,128)S(1)} %get-tuple-element.41.own_ref, bf16[400,256]{1,0:T(8,128)(2,1)S(1)} %collective-permute-done.4.g1_ref, bf16[400,256]{1,0:T(8,128)(2,1)S(1)} %collective-permute-done.5.g2_ref, ...), custom_call_target="tpu_custom_call" | custom-call | flops 3000000000 | bytes 100000 | tf_op jit(solution)/shard_map/pack/pallas_call | solution.py:260
  44.8 5.8 %all-to-all-done.in_ref = bf16[16,160,128]{2,1,0:T(8,128)(2,1)S(1)} async-done(((bf16[16,160,128]{2,1,0:T(8,128)(2,1)}), bf16[16,160,128]{2,1,0:T(8,128)(2,1)S(1)}, u32[]{:S(2)}, u32[]{:S(2)}) %all-to-all-start) | async-done | bytes 655392 | tf_op jit(solution)/shard_map/all_to_all | solution.py:397
  50.5 0.1 rel_xy.1.refs_0_
  50.6 1.7 %collective-permute-start.7 = (bf16[160,128]{1,0:T(8,128)(2,1)S(1)}, bf16[160,128]{1,0:T(8,128)(2,1)S(1)}, u32[]{:S(2)}, u32[]{:S(2)}) collective-permute-start(bf16[160,128]{1,0:T(8,128)(2,1)S(1)} %rel_xy.1.refs_0_), channel_id=1, source_target_pairs={{0,2},{2,4},{4,6},{6,8},{8,10},{10,12},{12,14},{14,0},{1,3},{3,5},... | collective-permute-start | bytes 122888 | tf_op jit(solution)/shard_map/ppermute | solution.py:369
  52.3 3.0 %collective-permute-start.8 = (bf16[160,128]{1,0:T(8,128)(2,1)S(1)}, bf16[160,128]{1,0:T(8,128)(2,1)S(1)}, u32[]{:S(2)}, u32[]{:S(2)}) collective-permute-start(bf16[160,128]{1,0:T(8,128)(2,1)S(1)} %rel_xy.1.refs_0_), channel_id=1, source_target_pairs={{0,4},{2,6},{4,8},{6,10},{8,12},{10,14},{12,0},{14,2},{1,5},{3,7},... | collective-permute-start | bytes 122888 | tf_op jit(solution)/shard_map/ppermute | solution.py:369
  55.3 3.8 %collective-permute-start.9 = (bf16[160,128]{1,0:T(8,128)(2,1)S(1)}, bf16[160,128]{1,0:T(8,128)(2,1)S(1)}, u32[]{:S(2)}, u32[]{:S(2)}) collective-permute-start(bf16[160,128]{1,0:T(8,128)(2,1)S(1)} %rel_xy.1.refs_0_), channel_id=1, source_target_pairs={{0,6},{2,8},{4,10},{6,12},{8,14},{10,0},{12,2},{14,4},{1,7},{3,9},... | collective-permute-start | bytes 122888 | tf_op jit(solution)/shard_map/ppermute | solution.py:369
  59.1 0.5 collective-permute-start.10
  59.5 4.5 %collective-permute-start.11 = (bf16[160,128]{1,0:T(8,128)(2,1)S(1)}, bf16[160,128]{1,0:T(8,128)(2,1)S(1)}, u32[]{:S(2)}, u32[]{:S(2)}) collective-permute-start(bf16[160,128]{1,0:T(8,128)(2,1)S(1)} %rel_xy.1.refs_0_), channel_id=1, source_target_pairs={{0,10},{2,12},{4,14},{6,0},{8,2},{10,4},{12,6},{14,8},{1,11},{3,13... | collective-permute-start | bytes 122888 | tf_op jit(solution)/shard_map/ppermute | solution.py:369
  64.0 2.4 %collective-permute-start.12 = (bf16[160,128]{1,0:T(8,128)(2,1)S(1)}, bf16[160,128]{1,0:T(8,128)(2,1)S(1)}, u32[]{:S(2)}, u32[]{:S(2)}) collective-permute-start(bf16[160,128]{1,0:T(8,128)(2,1)S(1)} %rel_xy.1.refs_0_), channel_id=1, source_target_pairs={{0,12},{2,14},{4,0},{6,2},{8,4},{10,6},{12,8},{14,10},{1,13},{3,15... | collective-permute-start | bytes 122888 | tf_op jit(solution)/shard_map/ppermute | solution.py:369
  66.4 0.7 collective-permute-start.13
  67.1 9.5 %all-to-all-start.1 = ((bf16[256,16,128]{2,1,0:T(8,128)(2,1)}), bf16[256,16,128]{2,1,0:T(8,128)(2,1)S(1)}, u32[]{:S(2)}, u32[]{:S(2)}) async-start(bf16[256,16,128]{2,1,0:T(8,128)(2,1)} %bitcast.8), calls=%async_computation.1 | async-start | bytes 2097152 | tf_op jit(solution)/shard_map/all_to_all | solution.py:403
  76.7 1.5 %collective-permute-start.14 = (bf16[160,128]{1,0:T(8,128)(2,1)S(1)}, bf16[160,128]{1,0:T(8,128)(2,1)S(1)}, u32[]{:S(2)}, u32[]{:S(2)}) collective-permute-start(bf16[160,128]{1,0:T(8,128)(2,1)S(1)} %rel_z.1.refs_0_), channel_id=1, source_target_pairs={{0,16},{16,32},{32,48},{48,0},{1,17},{17,33},{33,49},{49,1},{2,18}... | collective-permute-start | bytes 122888 | tf_op jit(solution)/shard_map/ppermute | solution.py:369
  78.2 2.5 %collective-permute-start.15 = (bf16[160,128]{1,0:T(8,128)(2,1)S(1)}, bf16[160,128]{1,0:T(8,128)(2,1)S(1)}, u32[]{:S(2)}, u32[]{:S(2)}) collective-permute-start(bf16[160,128]{1,0:T(8,128)(2,1)S(1)} %rel_z.1.refs_0_), channel_id=1, source_target_pairs={{0,32},{16,48},{32,0},{48,16},{1,33},{17,49},{33,1},{49,17},{2,34}... | collective-permute-start | bytes 122888 | tf_op jit(solution)/shard_map/ppermute | solution.py:369
  80.7 1.1 collective-permute-start.16
  81.8 2.5 %collective-permute-done.15.refs_2_ = bf16[160,128]{1,0:T(8,128)(2,1)S(1)} collective-permute-done((bf16[160,128]{1,0:T(8,128)(2,1)S(1)}, bf16[160,128]{1,0:T(8,128)(2,1)S(1)}, u32[]{:S(2)}, u32[]{:S(2)}) %collective-permute-start.15) | collective-permute-done | bytes 40992 | tf_op jit(solution)/shard_map/ppermute | solution.py:369
  84.4 1.2 %collective-permute-start.17 = (bf16[640,128]{1,0:T(8,128)(2,1)S(1)}, bf16[640,128]{1,0:T(8,128)(2,1)S(1)}, u32[]{:S(2)}, u32[]{:S(2)}) collective-permute-start(bf16[640,128]{1,0:T(8,128)(2,1)S(1)} %place_y.1.refs_0_), channel_id=1, source_target_pairs={{0,64},{64,128},{128,192},{192,0},{1,65},{65,129},{129,193},{193,1... | collective-permute-start | bytes 491528 | tf_op jit(solution)/shard_map/ppermute | solution.py:369
  85.6 2.4 %collective-permute-start.18 = (bf16[640,128]{1,0:T(8,128)(2,1)S(1)}, bf16[640,128]{1,0:T(8,128)(2,1)S(1)}, u32[]{:S(2)}, u32[]{:S(2)}) collective-permute-start(bf16[640,128]{1,0:T(8,128)(2,1)S(1)} %place_y.1.refs_0_), channel_id=1, source_target_pairs={{0,128},{64,192},{128,0},{192,64},{1,129},{65,193},{129,1},{193,65... | collective-permute-start | bytes 491528 | tf_op jit(solution)/shard_map/ppermute | solution.py:369
  87.9 1.1 collective-permute-start.19
  89.0 3.4 %collective-permute-done.17.refs_1_ = bf16[640,128]{1,0:T(8,128)(2,1)S(1)} collective-permute-done((bf16[640,128]{1,0:T(8,128)(2,1)S(1)}, bf16[640,128]{1,0:T(8,128)(2,1)S(1)}, u32[]{:S(2)}, u32[]{:S(2)}) %collective-permute-start.17) | collective-permute-done | bytes 163872 | tf_op jit(solution)/shard_map/ppermute | solution.py:369
  92.4 6.9 %collective-permute-done.18.refs_2_ = bf16[640,128]{1,0:T(8,128)(2,1)S(1)} collective-permute-done((bf16[640,128]{1,0:T(8,128)(2,1)S(1)}, bf16[640,128]{1,0:T(8,128)(2,1)S(1)}, u32[]{:S(2)}, u32[]{:S(2)}) %collective-permute-start.18) | collective-permute-done | bytes 163872 | tf_op jit(solution)/shard_map/ppermute | solution.py:369
  99.4 0.6 collective-permute-done.19.refs_3_
  100.0 2.1 %collective-permute-start.20 = (bf16[2560,128]{1,0:T(8,128)(2,1)S(1)}, bf16[2560,128]{1,0:T(8,128)(2,1)S(1)}, u32[]{:S(2)}, u32[]{:S(2)}) collective-permute-start(bf16[2560,128]{1,0:T(8,128)(2,1)S(1)} %place_x.1.mine_ref), channel_id=1, source_target_pairs={{0,1},{1,0},{2,3},{3,2},{4,5},{5,4},{6,7},{7,6},{8,9},{9,8},{10,11... | collective-permute-start | bytes 1966088 | tf_op jit(solution)/shard_map/ppermute | solution.py:373
  102.2 1.7 %collective-permute-done.20.other_ref = bf16[2560,128]{1,0:T(8,128)(2,1)S(1)} collective-permute-done((bf16[2560,128]{1,0:T(8,128)(2,1)S(1)}, bf16[2560,128]{1,0:T(8,128)(2,1)S(1)}, u32[]{:S(2)}, u32[]{:S(2)}) %collective-permute-start.20) | collective-permute-done | bytes 655392 | tf_op jit(solution)/shard_map/ppermute | solution.py:373
  103.9 0.8 copy-done.10
  104.7 3.0 %table.1 = f32[400,1500]{1,0:T(8,128)} custom-call(s32[1]{0:T(128)} %bitcast.core_ref, bf16[2560,128]{1,0:T(8,128)(2,1)} %copy-done, bf16[2560,128]{1,0:T(8,128)(2,1)} %copy-done.10), custom_call_target="tpu_custom_call" | custom-call | flops 1000000 | bytes 100000 | tf_op jit(solution)/shard_map/table/pallas_call | solution.py:363
  107.8 1.4 %all-to-all-done.1 = bf16[256,16,128]{2,1,0:T(8,128)(2,1)S(1)} async-done(((bf16[256,16,128]{2,1,0:T(8,128)(2,1)}), bf16[256,16,128]{2,1,0:T(8,128)(2,1)S(1)}, u32[]{:S(2)}, u32[]{:S(2)}) %all-to-all-start.1) | async-done | bytes 1048608 | tf_op jit(solution)/shard_map/all_to_all | solution.py:403
  109.2 1.0 copy-done.9
  110.2 4.6 %partition.1 = f32[100,1024]{1,0:T(8,128)} custom-call(bf16[4096,128]{1,0:T(8,128)(2,1)} %bitcast.23), custom_call_target="tpu_custom_call" | custom-call | flops 1000000 | bytes 100000 | tf_op jit(solution)/shard_map/partition/pallas_call | solution.py:291
  (35 shorter events, 0.2 us)
Async XLA Ops:
  0.6 14.7 %collective-permute-start = (bf16[400,256]{1,0:T(8,128)(2,1)}, bf16[400,256]{1,0:T(8,128)(2,1)S(1)}, u32[]{:S(2)}, u32[]{:S(2)}) collective-permute-start(bf16[400,256]{1,0:T(8,128)(2,1)} %bitcast.19), channel_id=1, source_target_pairs={{0,64},{64,128},{128,192},{192,0},{1,65},{65,129},{129,193},{193,1... | collective-permute-start | bytes 614408 | tf_op jit(solution)/shard_map/ppermute | solution.py:369
  2.7 12.6 %collective-permute-start.1 = (bf16[400,256]{1,0:T(8,128)(2,1)}, bf16[400,256]{1,0:T(8,128)(2,1)S(1)}, u32[]{:S(2)}, u32[]{:S(2)}) collective-permute-start(bf16[400,256]{1,0:T(8,128)(2,1)} %bitcast.20), channel_id=1, source_target_pairs={{0,128},{64,192},{128,0},{192,64},{1,129},{65,193},{129,1},{193,65... | collective-permute-start | bytes 614408 | tf_op jit(solution)/shard_map/ppermute | solution.py:369
  5.2 10.1 %collective-permute-start.2 = (bf16[400,256]{1,0:T(8,128)(2,1)}, bf16[400,256]{1,0:T(8,128)(2,1)S(1)}, u32[]{:S(2)}, u32[]{:S(2)}) collective-permute-start(bf16[400,256]{1,0:T(8,128)(2,1)} %bitcast.21), channel_id=1, source_target_pairs={{0,192},{64,0},{128,64},{192,128},{1,193},{65,1},{129,65},{193,129... | collective-permute-start | bytes 614408 | tf_op jit(solution)/shard_map/ppermute | solution.py:369
  7.2 1.7 %copy-start.1 = (f32[1500,400]{0,1:T(8,128)S(1)}, f32[1500,400]{0,1:T(8,128)}, u32[]{:S(2)}) copy-start(f32[1500,400]{0,1:T(8,128)} %param.14) | copy-start | bytes 7200004
  8.9 1.1 copy-start.2
  10.0 1.1 copy-start.4
  11.0 4.3 %copy-start.3 = (bf16[768,400]{0,1:T(8,128)(2,1)S(1)}, bf16[768,400]{0,1:T(8,128)(2,1)}, u32[]{:S(2)}) copy-start(bf16[768,400]{0,1:T(8,128)(2,1)} %param.10) | copy-start | bytes 1843204
  11.0 4.3 %copy-start.5 = (bf16[768,400]{0,1:T(8,128)(2,1)S(1)}, bf16[768,400]{0,1:T(8,128)(2,1)}, u32[]{:S(2)}) copy-start(bf16[768,400]{0,1:T(8,128)(2,1)} %param.11) | copy-start | bytes 1843204
  11.0 4.3 %copy-start.6 = (bf16[256,400]{0,1:T(8,128)(2,1)S(1)}, bf16[256,400]{0,1:T(8,128)(2,1)}, u32[]{:S(2)}) copy-start(bf16[256,400]{0,1:T(8,128)(2,1)} %param.13) | copy-start | bytes 614404
  24.9 0.8 copy-start.7
  25.7 5.9 %collective-permute-start.3 = (f32[400,768]{1,0:T(8,128)S(1)}, f32[400,768]{1,0:T(8,128)S(1)}, u32[]{:S(2)}, u32[]{:S(2)}) collective-permute-start(f32[400,768]{1,0:T(8,128)S(1)} %get-tuple-element.34), channel_id=1, source_target_pairs={{0,1},{1,0},{2,3},{3,2},{4,5},{5,4},{6,7},{7,6},{8,9},{9,8},{10,11... | collective-permute-start | bytes 3686408 | tf_op jit(solution)/shard_map/ppermute | solution.py:373
  28.7 13.6 %collective-permute-start.4 = (bf16[400,256]{1,0:T(8,128)(2,1)S(1)}, bf16[400,256]{1,0:T(8,128)(2,1)S(1)}, u32[]{:S(2)}, u32[]{:S(2)}) collective-permute-start(bf16[400,256]{1,0:T(8,128)(2,1)S(1)} %get-tuple-element.42), channel_id=1, source_target_pairs={{0,192},{64,0},{128,64},{192,128},{1,193},{65,1},{129,65},{193,129... | collective-permute-start | bytes 614408 | tf_op jit(solution)/shard_map/ppermute | solution.py:369
  29.6 12.8 %collective-permute-start.5 = (bf16[400,256]{1,0:T(8,128)(2,1)S(1)}, bf16[400,256]{1,0:T(8,128)(2,1)S(1)}, u32[]{:S(2)}, u32[]{:S(2)}) collective-permute-start(bf16[400,256]{1,0:T(8,128)(2,1)S(1)} %get-tuple-element.43), channel_id=1, source_target_pairs={{0,128},{64,192},{128,0},{192,64},{1,129},{65,193},{129,1},{193,65... | collective-permute-start | bytes 614408 | tf_op jit(solution)/shard_map/ppermute | solution.py:369
  30.9 11.6 %collective-permute-start.6 = (bf16[400,256]{1,0:T(8,128)(2,1)S(1)}, bf16[400,256]{1,0:T(8,128)(2,1)S(1)}, u32[]{:S(2)}, u32[]{:S(2)}) collective-permute-start(bf16[400,256]{1,0:T(8,128)(2,1)S(1)} %get-tuple-element.44), channel_id=1, source_target_pairs={{0,64},{64,128},{128,192},{192,0},{1,65},{65,129},{129,193},{193,1... | collective-permute-start | bytes 614408 | tf_op jit(solution)/shard_map/ppermute | solution.py:369
  32.6 17.9 %all-to-all-start = ((bf16[16,160,128]{2,1,0:T(8,128)(2,1)}), bf16[16,160,128]{2,1,0:T(8,128)(2,1)S(1)}, u32[]{:S(2)}, u32[]{:S(2)}) async-start(bf16[16,160,128]{2,1,0:T(8,128)(2,1)} %bitcast.7), calls=%async_computation | async-start | bytes 1310720 | tf_op jit(solution)/shard_map/all_to_all | solution.py:397
  38.9 1.1 copy-start.8
  50.6 13.4 %collective-permute-start.7 = (bf16[160,128]{1,0:T(8,128)(2,1)S(1)}, bf16[160,128]{1,0:T(8,128)(2,1)S(1)}, u32[]{:S(2)}, u32[]{:S(2)}) collective-permute-start(bf16[160,128]{1,0:T(8,128)(2,1)S(1)} %rel_xy.1.refs_0_), channel_id=1, source_target_pairs={{0,2},{2,4},{4,6},{6,8},{8,10},{10,12},{12,14},{14,0},{1,3},{3,5},... | collective-permute-start | bytes 122888 | tf_op jit(solution)/shard_map/ppermute | solution.py:369
  52.3 14.1 %collective-permute-start.8 = (bf16[160,128]{1,0:T(8,128)(2,1)S(1)}, bf16[160,128]{1,0:T(8,128)(2,1)S(1)}, u32[]{:S(2)}, u32[]{:S(2)}) collective-permute-start(bf16[160,128]{1,0:T(8,128)(2,1)S(1)} %rel_xy.1.refs_0_), channel_id=1, source_target_pairs={{0,4},{2,6},{4,8},{6,10},{8,12},{10,14},{12,0},{14,2},{1,5},{3,7},... | collective-permute-start | bytes 122888 | tf_op jit(solution)/shard_map/ppermute | solution.py:369
  55.3 21.3 %collective-permute-start.9 = (bf16[160,128]{1,0:T(8,128)(2,1)S(1)}, bf16[160,128]{1,0:T(8,128)(2,1)S(1)}, u32[]{:S(2)}, u32[]{:S(2)}) collective-permute-start(bf16[160,128]{1,0:T(8,128)(2,1)S(1)} %rel_xy.1.refs_0_), channel_id=1, source_target_pairs={{0,6},{2,8},{4,10},{6,12},{8,14},{10,0},{12,2},{14,4},{1,7},{3,9},... | collective-permute-start | bytes 122888 | tf_op jit(solution)/shard_map/ppermute | solution.py:369
  59.1 17.5 %collective-permute-start.10 = (bf16[160,128]{1,0:T(8,128)(2,1)S(1)}, bf16[160,128]{1,0:T(8,128)(2,1)S(1)}, u32[]{:S(2)}, u32[]{:S(2)}) collective-permute-start(bf16[160,128]{1,0:T(8,128)(2,1)S(1)} %rel_xy.1.refs_0_), channel_id=1, source_target_pairs={{0,8},{2,10},{4,12},{6,14},{8,0},{10,2},{12,4},{14,6},{1,9},{3,11}... | collective-permute-start | bytes 122888 | tf_op jit(solution)/shard_map/ppermute | solution.py:369
  59.5 17.1 %collective-permute-start.11 = (bf16[160,128]{1,0:T(8,128)(2,1)S(1)}, bf16[160,128]{1,0:T(8,128)(2,1)S(1)}, u32[]{:S(2)}, u32[]{:S(2)}) collective-permute-start(bf16[160,128]{1,0:T(8,128)(2,1)S(1)} %rel_xy.1.refs_0_), channel_id=1, source_target_pairs={{0,10},{2,12},{4,14},{6,0},{8,2},{10,4},{12,6},{14,8},{1,11},{3,13... | collective-permute-start | bytes 122888 | tf_op jit(solution)/shard_map/ppermute | solution.py:369
  64.0 12.6 %collective-permute-start.12 = (bf16[160,128]{1,0:T(8,128)(2,1)S(1)}, bf16[160,128]{1,0:T(8,128)(2,1)S(1)}, u32[]{:S(2)}, u32[]{:S(2)}) collective-permute-start(bf16[160,128]{1,0:T(8,128)(2,1)S(1)} %rel_xy.1.refs_0_), channel_id=1, source_target_pairs={{0,12},{2,14},{4,0},{6,2},{8,4},{10,6},{12,8},{14,10},{1,13},{3,15... | collective-permute-start | bytes 122888 | tf_op jit(solution)/shard_map/ppermute | solution.py:369
  66.4 10.2 %collective-permute-start.13 = (bf16[160,128]{1,0:T(8,128)(2,1)S(1)}, bf16[160,128]{1,0:T(8,128)(2,1)S(1)}, u32[]{:S(2)}, u32[]{:S(2)}) collective-permute-start(bf16[160,128]{1,0:T(8,128)(2,1)S(1)} %rel_xy.1.refs_0_), channel_id=1, source_target_pairs={{0,14},{2,0},{4,2},{6,4},{8,6},{10,8},{12,10},{14,12},{1,15},{3,1}... | collective-permute-start | bytes 122888 | tf_op jit(solution)/shard_map/ppermute | solution.py:369
  67.1 42.1 %all-to-all-start.1 = ((bf16[256,16,128]{2,1,0:T(8,128)(2,1)}), bf16[256,16,128]{2,1,0:T(8,128)(2,1)S(1)}, u32[]{:S(2)}, u32[]{:S(2)}) async-start(bf16[256,16,128]{2,1,0:T(8,128)(2,1)} %bitcast.8), calls=%async_computation.1 | async-start | bytes 2097152 | tf_op jit(solution)/shard_map/all_to_all | solution.py:403
  76.7 5.1 %collective-permute-start.14 = (bf16[160,128]{1,0:T(8,128)(2,1)S(1)}, bf16[160,128]{1,0:T(8,128)(2,1)S(1)}, u32[]{:S(2)}, u32[]{:S(2)}) collective-permute-start(bf16[160,128]{1,0:T(8,128)(2,1)S(1)} %rel_z.1.refs_0_), channel_id=1, source_target_pairs={{0,16},{16,32},{32,48},{48,0},{1,17},{17,33},{33,49},{49,1},{2,18}... | collective-permute-start | bytes 122888 | tf_op jit(solution)/shard_map/ppermute | solution.py:369
  78.2 6.2 %collective-permute-start.15 = (bf16[160,128]{1,0:T(8,128)(2,1)S(1)}, bf16[160,128]{1,0:T(8,128)(2,1)S(1)}, u32[]{:S(2)}, u32[]{:S(2)}) collective-permute-start(bf16[160,128]{1,0:T(8,128)(2,1)S(1)} %rel_z.1.refs_0_), channel_id=1, source_target_pairs={{0,32},{16,48},{32,0},{48,16},{1,33},{17,49},{33,1},{49,17},{2,34}... | collective-permute-start | bytes 122888 | tf_op jit(solution)/shard_map/ppermute | solution.py:369
  80.7 3.6 %collective-permute-start.16 = (bf16[160,128]{1,0:T(8,128)(2,1)S(1)}, bf16[160,128]{1,0:T(8,128)(2,1)S(1)}, u32[]{:S(2)}, u32[]{:S(2)}) collective-permute-start(bf16[160,128]{1,0:T(8,128)(2,1)S(1)} %rel_z.1.refs_0_), channel_id=1, source_target_pairs={{0,48},{16,0},{32,16},{48,32},{1,49},{17,1},{33,17},{49,33},{2,50}... | collective-permute-start | bytes 122888 | tf_op jit(solution)/shard_map/ppermute | solution.py:369
  84.4 8.0 %collective-permute-start.17 = (bf16[640,128]{1,0:T(8,128)(2,1)S(1)}, bf16[640,128]{1,0:T(8,128)(2,1)S(1)}, u32[]{:S(2)}, u32[]{:S(2)}) collective-permute-start(bf16[640,128]{1,0:T(8,128)(2,1)S(1)} %place_y.1.refs_0_), channel_id=1, source_target_pairs={{0,64},{64,128},{128,192},{192,0},{1,65},{65,129},{129,193},{193,1... | collective-permute-start | bytes 491528 | tf_op jit(solution)/shard_map/ppermute | solution.py:369
  85.6 13.8 %collective-permute-start.18 = (bf16[640,128]{1,0:T(8,128)(2,1)S(1)}, bf16[640,128]{1,0:T(8,128)(2,1)S(1)}, u32[]{:S(2)}, u32[]{:S(2)}) collective-permute-start(bf16[640,128]{1,0:T(8,128)(2,1)S(1)} %place_y.1.refs_0_), channel_id=1, source_target_pairs={{0,128},{64,192},{128,0},{192,64},{1,129},{65,193},{129,1},{193,65... | collective-permute-start | bytes 491528 | tf_op jit(solution)/shard_map/ppermute | solution.py:369
  87.9 12.1 %collective-permute-start.19 = (bf16[640,128]{1,0:T(8,128)(2,1)S(1)}, bf16[640,128]{1,0:T(8,128)(2,1)S(1)}, u32[]{:S(2)}, u32[]{:S(2)}) collective-permute-start(bf16[640,128]{1,0:T(8,128)(2,1)S(1)} %place_y.1.refs_0_), channel_id=1, source_target_pairs={{0,192},{64,0},{128,64},{192,128},{1,193},{65,1},{129,65},{193,129... | collective-permute-start | bytes 491528 | tf_op jit(solution)/shard_map/ppermute | solution.py:369
  100.0 3.9 %copy-start = (bf16[2560,128]{1,0:T(8,128)(2,1)}, bf16[2560,128]{1,0:T(8,128)(2,1)S(1)}, u32[]{:S(2)}) copy-start(bf16[2560,128]{1,0:T(8,128)(2,1)S(1)} %place_x.1.mine_ref) | copy-start | bytes 1966084
  100.0 3.9 %collective-permute-start.20 = (bf16[2560,128]{1,0:T(8,128)(2,1)S(1)}, bf16[2560,128]{1,0:T(8,128)(2,1)S(1)}, u32[]{:S(2)}, u32[]{:S(2)}) collective-permute-start(bf16[2560,128]{1,0:T(8,128)(2,1)S(1)} %place_x.1.mine_ref), channel_id=1, source_target_pairs={{0,1},{1,0},{2,3},{3,2},{4,5},{5,4},{6,7},{7,6},{8,9},{9,8},{10,11... | collective-permute-start | bytes 1966088 | tf_op jit(solution)/shard_map/ppermute | solution.py:373
  103.9 0.8 copy-start.10
  109.2 1.0 copy-start.9

commit v4 on v3

--- a/solution.py
+++ b/solution.py
@@ -154,7 +154,7 @@
 
 
 def edge_kernel(core_ref, n0_ref, n1_ref, n2_ref, n3_ref, head_ref, tail_ref, r_ref, q_ref, m_ref, pos_ref, rid_ref,
-                pt_ref, ph_ref, dh_ref, dt_ref, mine_ref, other_ref, neg_ref, turned_ref):
+                own_ref, g1_ref, g2_ref, g3_ref, rows_ref, mine_ref, other_ref, neg_ref, turned_ref):
     turn = eye(NEG_DEV)
     for k, ref in enumerate((n0_ref, n1_ref, n2_ref, n3_ref)):
         value = ref[...]
@@ -165,7 +165,8 @@
     tail = tail_ref[...].astype(F32)
     firsts = []
     grads = []
-    for side, (query_ref, positives, prob_ref) in enumerate(((q_ref, tail, pt_ref), (m_ref, head, ph_ref))):
+    term = jnp.zeros((D, NEG), F32)
+    for side, (query_ref, positives) in enumerate(((q_ref, tail), (m_ref, head))):
         positive = pos_ref[pl.ds(side, 1), :]
         scores = dot(turned_ref[...], query_ref[...])
         top = jnp.maximum(positive, jnp.max(scores, 0, keepdims=True))
@@ -174,9 +175,12 @@
         total = pos_weight + jnp.sum(weight, 0, keepdims=True)
         first = pos_weight / total - 1.0
         probs = (weight * (1.0 / total)).astype(BF16)
-        prob_ref[...] = probs
+        term = term + dot_nt(query_ref[...], probs)
         grads.append(first * positives + dot(neg_ref[...], probs))
         firsts.append(first)
+    own_ref[...] = term[:, :NEG_DEV]
+    for k, ref in enumerate((g1_ref, g2_ref, g3_ref)):
+        ref[...] = term[:, (k + 1) * NEG_DEV:(k + 2) * NEG_DEV].astype(BF16)
 
     rel = r_ref[...]
     dq, dm = grads
@@ -187,14 +191,15 @@
     ids = jnp.where(ids < 0, ids + REL_PAD, ids)
     hit = one_hot(ids, REL_PAD)
     high, low = split2(d_rel)
+    both = jnp.concatenate([high, low], 0)
     for ref, at in ((other_ref, REL_HALF), (mine_ref, 0)):
-        part = hit[at:at + REL_HALF]
-        ref[...] = (dot_nt(part, high) + dot_nt(part, low)).T
+        term = dot_nt(both, hit[at:at + REL_HALF])
+        ref[...] = term[:D] + term[D:]
 
     d_head = firsts[1] * m_ref[...].astype(F32) + jnp.concatenate([rr * qr + ri * qi, rr * qi - ri * qr], 0)
     d_tail = firsts[0] * q_ref[...].astype(F32) + jnp.concatenate([rr * mr - ri * mi, rr * mi + ri * mr], 0)
-    dh_ref[...] = d_head.astype(BF16)
-    dt_ref[...] = d_tail.astype(BF16)
+    rows_ref[:, pl.ds(0, E_DEV)] = d_head.astype(BF16)
+    rows_ref[:, pl.ds(E_DEV, E_DEV)] = d_tail.astype(BF16)
 
 
 def edge(core, negs, h, t, r, q, m, pos, rid):
@@ -204,46 +209,30 @@
     return call(
         edge_kernel, "edge", 1,
         [SMEM] + [full(part)] * 4 + [full(cols)] * 5 + [full((8, E_DEV)), full((1, E_DEV))],
-        [full((NEG, E_DEV))] * 2 + [full(cols)] * 2 + [full(half)] * 2,
-        [arr((NEG, E_DEV), BF16)] * 2 + [arr(cols, BF16)] * 2 + [arr(half, F32)] * 2,
+        [full(part)] * 4 + [full((D, 2 * E_DEV))] + [full(half)] * 2,
+        [arr(part, F32)] + [arr(part, BF16)] * 3 + [arr((D, 2 * E_DEV), BF16)] + [arr(half, F32)] * 2,
         [pltpu.VMEM((D, NEG), BF16), pltpu.VMEM((NEG, D), BF16)],
         flops=10**10, mib=36,
     )(core, *negs, h, t, r, q, m, pos, rid)
 
 
-def group_kernel(q_ref, m_ref, pt_ref, ph_ref, own_ref, g1_ref, g2_ref, g3_ref):
-    term = dot_nt(q_ref[...], pt_ref[...]) + dot_nt(m_ref[...], ph_ref[...])
-    own_ref[...] = term[:, :NEG_DEV]
-    for k, ref in enumerate((g1_ref, g2_ref, g3_ref)):
-        ref[...] = term[:, (k + 1) * NEG_DEV:(k + 2) * NEG_DEV].astype(BF16)
-
-
-def group(q, m, pt, ph):
-    part = (D, NEG_DEV)
-    return call(
-        group_kernel, "group", 1,
-        [full((D, E_DEV))] * 2 + [full((NEG, E_DEV))] * 2, [full(part)] * 4, [arr(part, F32)] + [arr(part, BF16)] * 3,
-        flops=4 * 10**9, mib=24,
-    )(q, m, pt, ph)
-
-
-def slot_kernel(target_h_ref, target_t_ref, dh_ref, dt_ref, code_ref, out_ref):
+def slot_kernel(target_h_ref, target_t_ref, rows_ref, code_ref, out_ref):
     hit_h = one_hot(target_h_ref[...], U_CAP)
     hit_t = one_hot(target_t_ref[...], U_CAP)
-    total = dot_nt(hit_h, dh_ref[...]) + dot_nt(hit_t, dt_ref[...])
+    total = dot_nt(hit_h, rows_ref[:, pl.ds(0, E_DEV)]) + dot_nt(hit_t, rows_ref[:, pl.ds(E_DEV, E_DEV)])
     code = code_ref[:, USED:]
     for k in range(N_GRP):
         out_ref[k] = jnp.concatenate([total[:, k * USED:(k + 1) * USED], code], 1)
 
 
-def slot(th, tt, dh, dt, code):
+def slot(th, tt, rows, code):
     shape = (N_GRP, U_CAP, LANES)
     return call(
         slot_kernel, "slot", 1,
-        [full((1, E_DEV))] * 2 + [full((D, E_DEV))] * 2 + [full((U_CAP, LANES))],
+        [full((1, E_DEV))] * 2 + [full((D, 2 * E_DEV)), full((U_CAP, LANES))],
         full(shape), arr(shape, F32),
         flops=8 * 10**9, mib=24,
-    )(th, tt, dh, dt, code)
+    )(th, tt, rows, code)
 
 
 def pack_kernel(target_ref, own_ref, g1_ref, g2_ref, g3_ref, part_ref, out_ref):
@@ -294,6 +283,7 @@
         full((USED, ENT_DEV)),
         arr((USED, ENT_DEV), F32),
         [pltpu.VMEM((ENT_DEV, LANES), F32)],
+        mib=32,
     )(rows)
 
 
@@ -307,7 +297,7 @@
 
 def rel_chip(mine, other):
     shape = (N_XY * REL_PART, LANES)
-    return call(rel_chip_kernel, "rel_chip", 1, [full((D, REL_HALF))] * 2, full(shape), arr(shape, BF16), mib=24)(mine, other)
+    return call(rel_chip_kernel, "rel_chip", 1, [full((D, REL_HALF))] * 2, full(shape), arr(shape, BF16), mib=12)(mine, other)
 
 
 def rel_xy_kernel(in_ref, out_ref):
@@ -316,20 +306,57 @@
 
 def rel_xy(parts):
     shape = (REL_PART, LANES)
-    return call(rel_xy_kernel, "rel_xy", 1, [full((N_XY,) + shape)], full(shape), arr(shape, BF16), mib=24)(parts)
-
-
-def rel_z_kernel(*refs):
-    values = [ref[...].astype(F32) for ref in refs[:-1]]
+    return call(rel_xy_kernel, "rel_xy", 1, [full((N_XY,) + shape)], full(shape), arr(shape, BF16), mib=12)(parts)
+
+
+def chip_pair_kernel(core_ref, mine_ref, other_ref, out_ref):
+    at = pl.multiple_of(core_ref[0] * REL_PART, REL_PART)
+    out_ref[pl.ds(at, REL_PART), :] = mine_ref[...]
+    out_ref[pl.ds(REL_PART - at, REL_PART), :] = other_ref[...]
+
+
+def chip_pair(core, mine, other):
+    shape = (REL_PART, LANES)
+    out = (2 * REL_PART, LANES)
+    return call(chip_pair_kernel, "chip_pair", 1, [SMEM] + [full(shape)] * 2, full(out), arr(out, BF16), mib=12)(core, mine, other)
+
+
+def split_pair_kernel(core_ref, b1_ref, b2_ref, b3_ref, far_ref, mine_ref, other_ref):
+    at = pl.multiple_of(core_ref[0] * REL_PART, REL_PART)
+    for k, ref in enumerate((b1_ref, b2_ref, b3_ref)):
+        mine_ref[pl.ds(k * REL_PART, REL_PART), :] = ref[pl.ds(at, REL_PART), :]
+        other_ref[pl.ds(k * REL_PART, REL_PART), :] = ref[pl.ds(REL_PART - at, REL_PART), :]
+    mine_ref[pl.ds(3 * REL_PART, REL_PART), :] = far_ref[...]
+
+
+def split_pair(core, blocks, far):
+    rows = (4 * REL_PART, LANES), (3 * REL_PART, LANES)
+    return call(
+        split_pair_kernel, "split_pair", 1, [SMEM] + [full((2 * REL_PART, LANES))] * 3 + [full((REL_PART, LANES))],
+        [full(shape) for shape in rows], [arr(shape, BF16) for shape in rows], mib=12, flops=3 * 10**10
+    )(core, *blocks, far)
+
+
+def rel_z_kernel(core_ref, own_ref, mine_ref, other_ref, out_ref):
+    value = lambda ref, k: ref[pl.ds(k * REL_PART, REL_PART), :].astype(F32)
+    ahead = [value(mine_ref, k) for k in range(3)]
+    behind = [value(other_ref, k) for k in range(3)]
+    first = core_ref[0] == 0
+    back = [own_ref[...].astype(F32)] + [jnp.where(first, a, b) for a, b in zip(ahead, behind)]
+    back += [value(mine_ref, 3)] + [jnp.where(first, b, a) for a, b in zip(ahead[::-1], behind[::-1])]
+    values = back
     while len(values) > 1:
         half = len(values) // 2
         values = [values[k] + values[k + half] for k in range(half)]
-    refs[-1][...] = values[0].astype(BF16)
-
-
-def rel_z(blocks):
+    out_ref[...] = values[0].astype(BF16)
+
+
+def rel_z(core, own, mine, other):
     shape = (REL_PART, LANES)
-    return call(rel_z_kernel, "rel_z", 1, [full(shape)] * 8, full(shape), arr(shape, BF16), mib=24, flops=3 * 10**10)(*blocks)
+    return call(
+        rel_z_kernel, "rel_z", 1, [SMEM, full(shape), full((4 * REL_PART, LANES)), full((3 * REL_PART, LANES))], full(shape),
+        arr(shape, BF16), mib=12,
+    )(core, own, mine, other)
 
 
 def place_kernel(me_ref, *refs):
@@ -344,7 +371,7 @@
     rows = blocks[0].shape[0]
     shape = (rows * N_GRP, LANES)
     return call(
-        place_kernel, name, 1, [SMEM] + [full((rows, LANES))] * N_GRP, full(shape), arr(shape, BF16), mib=24
+        place_kernel, name, 1, [SMEM] + [full((rows, LANES))] * N_GRP, full(shape), arr(shape, BF16), mib=12
     )(me, *blocks)
 
 
@@ -361,7 +388,7 @@
 
 def table(core, mine, other):
     return call(
-        table_kernel, "table", 1, [SMEM] + [full((N_XY * REL_PART, LANES))] * 2, full((D, RELS)), arr((D, RELS), F32)
+        table_kernel, "table", 1, [SMEM] + [full((N_XY * REL_PART, LANES))] * 2, full((D, RELS)), arr((D, RELS), F32), mib=20
     )(core, mine, other)
 
 
@@ -371,6 +398,11 @@
 
 def pair(value):
     return lax.ppermute(value, "c", [(0, 1), (1, 0)])
+
+
+def shift_zc(value, ahead):
+    pairs = [(2 * z + c, 2 * ((z + ahead[c]) % 8) + c) for z in range(8) for c in range(2)]
+    return lax.ppermute(value, ("z", "c"), pairs)
 
 
 def around(value, axis):
@@ -387,19 +419,19 @@
         rel_ids, head_slot, tail_slot, negative_slot, unique_ids[0], owner_counts[0],
         jnp.zeros((INTS - AT_COUNTS - N_OWN,), I32)]).reshape(1, INTS)
     r, q, m, pos, rid, th, tt, tn, code = prep(heads, tails, rel_table.T, ints)
-    pt, ph, dh, dt, mine, other = edge(core, negs, heads, tails, r, q, m, pos, rid)
-    own, g1, g2, g3 = group(q, m, pt, ph)
+    own, g1, g2, g3, rows, mine, other = edge(core, negs, heads, tails, r, q, m, pos, rid)
     back = [shift(g, "x", N_GRP - k) for k, g in ((1, g1), (2, g2), (3, g3))]
     other = pair(other)
-    mine, other, own = lax.optimization_barrier((mine, other, own))
     chip = rel_chip(mine, other).reshape(N_XY, REL_PART, LANES)
-    part = slot(th, tt, dh, dt, code)
+    part = slot(th, tt, rows, code)
     chip = lax.all_to_all(chip, ("x", "y"), 0, 0, tiled=True)
     packed = pack(tn, own, *back, part)
     chip, packed = lax.optimization_barrier((chip, packed))
     piece = rel_xy(chip)
     piece, packed = lax.optimization_barrier((piece, packed))
-    piece = rel_z([piece] + [shift(piece, "z", k, 8) for k in range(1, 8)])
+    both = chip_pair(core, piece, pair(piece))
+    mine, other = split_pair(core, [shift_zc(both, ahead) for ahead in ((1, 7), (2, 6), (3, 5))], shift(piece, "z", 4, 8))
+    piece = rel_z(core, piece, mine, pair(other))
     received = lax.all_to_all(packed.reshape(N_GRP * N_OWN, CAP, LANES), ALL, 0, 0, tiled=True)
     quarter = place(y, around(piece, "y"), "place_y")
     half = place(x, around(quarter, "x"), "place_x")

time: 115 us -> 108 us (0.939)
  starting transfers between devices: 54.2 us -> 50.4 us
  Pallas kernels: 28.8 us -> 25.7 us
  local copies, waits for them, and re-layouts: 8.39 us -> 5.97 us
  waiting for transfers between devices: 22.6 us -> 24.8 us
    ppermute x19 -> x13, starting transfers between devices: 34.9 us -> 20.9 us  [shift(): return lax.ppermute(value, axis, [(i, (i + k) % size) for i in range(size)])]
    ppermute x0 -> x3, starting transfers between devices: none -> 7.27 us  [shift_zc(): return lax.ppermute(value, ('z', 'c'), pairs)]
    ppermute x2 -> x4, starting transfers between devices: 3.64 us -> 8.32 us  [pair(): return lax.ppermute(value, 'c', [(0, 1), (1, 0)])]
    unnamed x22 -> x16, local copies, waits for them, and re-layouts: 7.56 us -> 5.13 us
    ppermute x2 -> x4, waiting for transfers between devices: 1.73 us -> 3.57 us  [pair(): return lax.ppermute(value, 'c', [(0, 1), (1, 0)])]
    all_to_all x1, starting transfers between devices: 9.47 us -> 7.69 us  [shards(): lax.all_to_all(packed.reshape(N_GRP * N_OWN, CAP, LANES), ALL, 0, 0, tile...]
    pallas_call x3 -> x4, Pallas kernels: 3.9 us -> 2.48 us  [the longest x1 2.38 us: slot(): call(slot_kernel, 'slot', 1, [full((1, E_DEV))] * 2 + [full((D, 2 * E_DEV...]
    pallas_call x1, Pallas kernels: 3.03 us -> 1.74 us  [table(): call(table_kernel, 'table', 1, [SMEM] + [full((N_XY * REL_PART, LANES))]...]
  transfers between devices with their start and end apart: 23 -> 22, of which waited for: 8 -> 10; matrix products, arithmetic and copies ran while one was open for 1% -> 1% of each run, Pallas kernels for 13% -> 11%
where the time goes in v4:
time: 108 us
  starting transfers between devices  50.4 us (47%)
  Pallas kernels  25.7 us (24%)
  waiting for transfers between devices  24.8 us (23%)
  local copies, waits for them, and re-layouts  5.97 us (6%)
    ppermute x13, starting transfers between devices, shift(): return lax.ppermute(value, axis, [(i, (i + k) % size) for i in range(size)])  20.9 us
    ppermute x13, waiting for transfers between devices, shift(): return lax.ppermute(value, axis, [(i, (i + k) % size) for i in range(size)])  13.8 us
    pallas_call x1, Pallas kernels, edge(): call(edge_kernel, 'edge', 1, [SMEM] + [full(part)] * 4 + [full(cols)] * 5...  10.3 us
    ppermute x4, starting transfers between devices, pair(): return lax.ppermute(value, 'c', [(0, 1), (1, 0)])  8.32 us
    all_to_all x1, starting transfers between devices, shards(): lax.all_to_all(packed.reshape(N_GRP * N_OWN, CAP, LANES), ALL, 0, 0, tile...  7.69 us
    ppermute x3, starting transfers between devices, shift_zc(): return lax.ppermute(value, ('z', 'c'), pairs)  7.27 us
    all_to_all x1, starting transfers between devices, shards(): chip = lax.all_to_all(chip, ('x', 'y'), 0, 0, tiled=True)  6.23 us
    all_to_all x1, waiting for transfers between devices, shards(): chip = lax.all_to_all(chip, ('x', 'y'), 0, 0, tiled=True)  5.63 us
  transfers between devices with their start and end apart: 22, of which 10 were waited for; matrix products, arithmetic and copies ran while one was open for 1% of the time, Pallas kernels for 11%

profile of v4, /device:TPU:1, one launch (start us, length us, event | category | flops | bytes accessed | tf_op | source)
XLA Modules:
  0.0 107.7 jit_solution(18296186892118320017)
XLA Ops:
  0.6 2.1 %collective-permute-start = (bf16[400,256]{1,0:T(8,128)(2,1)}, bf16[400,256]{1,0:T(8,128)(2,1)S(1)}, u32[]{:S(2)}, u32[]{:S(2)}) collective-permute-start(bf16[400,256]{1,0:T(8,128)(2,1)} %bitcast.20), channel_id=1, source_target_pairs={{0,64},{64,128},{128,192},{192,0},{1,65},{65,129},{129,193},{193,1... | collective-permute-start | bytes 614408 | tf_op jit(solution)/shard_map/ppermute | solution.py:396
  2.7 2.5 %collective-permute-start.1 = (bf16[400,256]{1,0:T(8,128)(2,1)}, bf16[400,256]{1,0:T(8,128)(2,1)S(1)}, u32[]{:S(2)}, u32[]{:S(2)}) collective-permute-start(bf16[400,256]{1,0:T(8,128)(2,1)} %bitcast.21), channel_id=1, source_target_pairs={{0,128},{64,192},{128,0},{192,64},{1,129},{65,193},{129,1},{193,65... | collective-permute-start | bytes 614408 | tf_op jit(solution)/shard_map/ppermute | solution.py:396
  5.2 1.2 %collective-permute-start.2 = (bf16[400,256]{1,0:T(8,128)(2,1)}, bf16[400,256]{1,0:T(8,128)(2,1)S(1)}, u32[]{:S(2)}, u32[]{:S(2)}) collective-permute-start(bf16[400,256]{1,0:T(8,128)(2,1)} %bitcast.22), channel_id=1, source_target_pairs={{0,192},{64,0},{128,64},{192,128},{1,193},{65,1},{129,65},{193,129... | collective-permute-start | bytes 614408 | tf_op jit(solution)/shard_map/ppermute | solution.py:396
  6.4 0.8 concatenate.3
  7.2 0.0 copy-start
  7.2 1.7 %copy-done = f32[1500,400]{0,1:T(8,128)S(1)} copy-done((f32[1500,400]{0,1:T(8,128)S(1)}, f32[1500,400]{0,1:T(8,128)}, u32[]{:S(2)}) %copy-start) | copy-done | bytes 2400024
  8.9 1.1 copy-done.1
  10.0 1.1 copy-done.3
  11.0 4.3 %prep.1 = (f32[400,768]{1,0:T(8,128)S(1)}, bf16[400,768]{1,0:T(8,128)(2,1)S(1)}, bf16[400,768]{1,0:T(8,128)(2,1)S(1)}, f32[8,768]{1,0:T(8,128)S(1)}, s32[1,768]{...) custom-call(bf16[400,768]{1,0:T(8,128)(2,1)S(1)} %bitcast.16, ...), custom_call_target="tpu_custom_call" | custom-call | flops 1000000 | bytes 100000 | tf_op jit(solution)/shard_map/prep/pallas_call | solution.py:145
  15.4 10.3 %edge.1 = (f32[400,256]{1,0:T(8,128)S(1)}, bf16[400,256]{1,0:T(8,128)(2,1)S(1)}, bf16[400,256]{1,0:T(8,128)(2,1)S(1)}, bf16[400,256]{1,0:T(8,128)(2,1)S(1)}, bf1...) custom-call(s32[1]{0:T(128)} %bitcast.core_ref, bf16[400,256]{1,0:T(8,128)(2,1)S(1)} %bitcast.23, ...), custom_call_target="tpu_custom_call" | custom-call | flops 10000000000 | bytes 100000 | tf_op jit(solution)/shard_map/edge/pallas_call | solution.py:209
  25.7 0.0 copy-start.6
  25.7 1.6 %collective-permute-start.3 = (f32[400,768]{1,0:T(8,128)S(1)}, f32[400,768]{1,0:T(8,128)S(1)}, u32[]{:S(2)}, u32[]{:S(2)}) collective-permute-start(f32[400,768]{1,0:T(8,128)S(1)} %get-tuple-element.30), channel_id=1, source_target_pairs={{0,1},{1,0},{2,3},{3,2},{4,5},{5,4},{6,7},{7,6},{8,9},{9,8},{10,11... | collective-permute-start | bytes 3686408 | tf_op jit(solution)/shard_map/ppermute | solution.py:400
  27.3 0.8 collective-permute-start.4
  28.2 1.3 %collective-permute-start.5 = (bf16[400,256]{1,0:T(8,128)(2,1)S(1)}, bf16[400,256]{1,0:T(8,128)(2,1)S(1)}, u32[]{:S(2)}, u32[]{:S(2)}) collective-permute-start(bf16[400,256]{1,0:T(8,128)(2,1)S(1)} %get-tuple-element.34), channel_id=1, source_target_pairs={{0,128},{64,192},{128,0},{192,64},{1,129},{65,193},{129,1},{193,65... | collective-permute-start | bytes 614408 | tf_op jit(solution)/shard_map/ppermute | solution.py:396
  29.4 0.7 collective-permute-start.6
  30.2 1.0 rel_chip.1
  31.2 6.2 %all-to-all-start = ((bf16[16,160,128]{2,1,0:T(8,128)(2,1)}), bf16[16,160,128]{2,1,0:T(8,128)(2,1)S(1)}, u32[]{:S(2)}, u32[]{:S(2)}) async-start(bf16[16,160,128]{2,1,0:T(8,128)(2,1)} %bitcast.7), calls=%async_computation | async-start | bytes 1310720 | tf_op jit(solution)/shard_map/all_to_all | solution.py:427
  37.4 0.0 copy-start.7
  37.5 1.3 %copy-done.7 = bf16[400,1536]{1,0:T(8,128)(2,1)S(1)} copy-done((bf16[400,1536]{1,0:T(8,128)(2,1)S(1)}, bf16[400,1536]{1,0:T(8,128)(2,1)}, u32[]{:S(2)}) %copy-start.7) | copy-done | bytes 1228824
  38.7 2.4 %slot.1.part_ref = f32[4,1024,128]{2,1,0:T(8,128)S(1)} custom-call(s32[1,768]{1,0:T(1,128)S(1)} %get-tuple-element.36.target_h_ref, s32[1,768]{1,0:T(1,128)S(1)} %get-tuple-element.37.target_t_ref, bf16[400,1536]{1,0:T(8,128)(2,1)S(1)} %copy-done.7, f32[1024,128]{1,0:T(8,128)S(1)} %get-tuple-element.39.code_ref), custom_call_target="tpu_custom_call" | custom-call | flops 8000000000 | bytes 100000 | tf_op jit(solution)/shard_map/slot/pallas_call | solution.py:230
  41.2 2.3 %pack.1 = bf16[4,1024,128]{2,1,0:T(8,128)(2,1)} custom-call(s32[1,256]{1,0:T(1,128)S(1)} %get-tuple-element.31.target_ref, f32[400,256]{1,0:T(8,128)S(1)} %get-tuple-element.32.own_ref, bf16[400,256]{1,0:T(8,128)(2,1)S(1)} %collective-permute-done.4.g1_ref, bf16[400,256]{1,0:T(8,128)(2,1)S(1)} %collective-permute-done.5.g2_ref, ...), custom_call_target="tpu_custom_call" | custom-call | flops 3000000000 | bytes 100000 | tf_op jit(solution)/shard_map/pack/pallas_call | solution.py:249
  43.4 5.6 %all-to-all-done.in_ref = bf16[16,160,128]{2,1,0:T(8,128)(2,1)S(1)} async-done(((bf16[16,160,128]{2,1,0:T(8,128)(2,1)}), bf16[16,160,128]{2,1,0:T(8,128)(2,1)S(1)}, u32[]{:S(2)}, u32[]{:S(2)}) %all-to-all-start) | async-done | bytes 655392 | tf_op jit(solution)/shard_map/all_to_all | solution.py:427
  49.1 0.1 rel_xy.1.mine_ref.own_ref
  49.2 2.3 %collective-permute-start.7 = (bf16[160,128]{1,0:T(8,128)(2,1)S(1)}, bf16[160,128]{1,0:T(8,128)(2,1)S(1)}, u32[]{:S(2)}, u32[]{:S(2)}) collective-permute-start(bf16[160,128]{1,0:T(8,128)(2,1)S(1)} %rel_xy.1.mine_ref.own_ref), channel_id=1, source_target_pairs={{0,1},{1,0},{2,3},{3,2},{4,5},{5,4},{6,7},{7,6},{8,9},{9,8},{10,11... | collective-permute-start | bytes 122888 | tf_op jit(solution)/shard_map/ppermute | solution.py:400
  51.5 0.9 collective-permute-done.7.other_ref
  52.4 6.5 %collective-permute-start.10 = (bf16[320,128]{1,0:T(8,128)(2,1)S(1)}, bf16[320,128]{1,0:T(8,128)(2,1)S(1)}, u32[]{:S(2)}, u32[]{:S(2)}) collective-permute-start(bf16[320,128]{1,0:T(8,128)(2,1)S(1)} %chip_pair.1), channel_id=1, source_target_pairs={{0,6},{1,11},{2,8},{3,13},{4,10},{5,15},{6,12},{7,1},{8,14},{9,3},... | collective-permute-start | bytes 245768 | tf_op jit(solution)/shard_map/ppermute | solution.py:405
  58.9 0.7 collective-permute-start.8
  59.6 4.5 %collective-permute-start.11 = (bf16[160,128]{1,0:T(8,128)(2,1)S(1)}, bf16[160,128]{1,0:T(8,128)(2,1)S(1)}, u32[]{:S(2)}, u32[]{:S(2)}) collective-permute-start(bf16[160,128]{1,0:T(8,128)(2,1)S(1)} %rel_xy.1.mine_ref.own_ref), channel_id=1, source_target_pairs={{0,8},{2,10},{4,12},{6,14},{8,0},{10,2},{12,4},{14,6},{1,9},{3,11}... | collective-permute-start | bytes 122888 | tf_op jit(solution)/shard_map/ppermute | solution.py:396
  64.1 7.7 %all-to-all-start.1 = ((bf16[256,16,128]{2,1,0:T(8,128)(2,1)}), bf16[256,16,128]{2,1,0:T(8,128)(2,1)S(1)}, u32[]{:S(2)}, u32[]{:S(2)}) async-start(bf16[256,16,128]{2,1,0:T(8,128)(2,1)} %bitcast.8), calls=%async_computation.1 | async-start | bytes 2097152 | tf_op jit(solution)/shard_map/all_to_all | solution.py:435
  71.9 2.2 %collective-permute-start.12 = (bf16[480,128]{1,0:T(8,128)(2,1)S(1)}, bf16[480,128]{1,0:T(8,128)(2,1)S(1)}, u32[]{:S(2)}, u32[]{:S(2)}) collective-permute-start(bf16[480,128]{1,0:T(8,128)(2,1)S(1)} %get-tuple-element.45), channel_id=1, source_target_pairs={{0,1},{1,0},{2,3},{3,2},{4,5},{5,4},{6,7},{7,6},{8,9},{9,8},{10,11... | collective-permute-start | bytes 368648 | tf_op jit(solution)/shard_map/ppermute | solution.py:400
  74.1 1.0 collective-permute-done.12.other_ref
  75.1 0.1 rel_z.1.refs_0_
  75.1 0.3 collective-permute-start.13
  75.5 2.0 %collective-permute-start.14 = (bf16[160,128]{1,0:T(8,128)(2,1)S(1)}, bf16[160,128]{1,0:T(8,128)(2,1)S(1)}, u32[]{:S(2)}, u32[]{:S(2)}) collective-permute-start(bf16[160,128]{1,0:T(8,128)(2,1)S(1)} %rel_z.1.refs_0_), channel_id=1, source_target_pairs={{0,32},{16,48},{32,0},{48,16},{1,33},{17,49},{33,1},{49,17},{2,34}... | collective-permute-start | bytes 122888 | tf_op jit(solution)/shard_map/ppermute | solution.py:396
  77.5 1.1 %collective-permute-start.15 = (bf16[160,128]{1,0:T(8,128)(2,1)S(1)}, bf16[160,128]{1,0:T(8,128)(2,1)S(1)}, u32[]{:S(2)}, u32[]{:S(2)}) collective-permute-start(bf16[160,128]{1,0:T(8,128)(2,1)S(1)} %rel_z.1.refs_0_), channel_id=1, source_target_pairs={{0,48},{16,0},{32,16},{48,32},{1,49},{17,1},{33,17},{49,33},{2,50}... | collective-permute-start | bytes 122888 | tf_op jit(solution)/shard_map/ppermute | solution.py:396
  78.6 3.0 %collective-permute-done.13.refs_1_ = bf16[160,128]{1,0:T(8,128)(2,1)S(1)} collective-permute-done((bf16[160,128]{1,0:T(8,128)(2,1)S(1)}, bf16[160,128]{1,0:T(8,128)(2,1)S(1)}, u32[]{:S(2)}, u32[]{:S(2)}) %collective-permute-start.13) | collective-permute-done | bytes 40992 | tf_op jit(solution)/shard_map/ppermute | solution.py:396
  81.6 0.2 collective-permute-done.15.refs_3_
  81.9 0.6 collective-permute-start.16
  82.5 2.7 %collective-permute-start.17 = (bf16[640,128]{1,0:T(8,128)(2,1)S(1)}, bf16[640,128]{1,0:T(8,128)(2,1)S(1)}, u32[]{:S(2)}, u32[]{:S(2)}) collective-permute-start(bf16[640,128]{1,0:T(8,128)(2,1)S(1)} %place_y.1.refs_0_), channel_id=1, source_target_pairs={{0,128},{64,192},{128,0},{192,64},{1,129},{65,193},{129,1},{193,65... | collective-permute-start | bytes 491528 | tf_op jit(solution)/shard_map/ppermute | solution.py:396
  85.1 1.2 %collective-permute-start.18 = (bf16[640,128]{1,0:T(8,128)(2,1)S(1)}, bf16[640,128]{1,0:T(8,128)(2,1)S(1)}, u32[]{:S(2)}, u32[]{:S(2)}) collective-permute-start(bf16[640,128]{1,0:T(8,128)(2,1)S(1)} %place_y.1.refs_0_), channel_id=1, source_target_pairs={{0,192},{64,0},{128,64},{192,128},{1,193},{65,1},{129,65},{193,129... | collective-permute-start | bytes 491528 | tf_op jit(solution)/shard_map/ppermute | solution.py:396
  86.3 3.8 %collective-permute-done.16.refs_1_ = bf16[640,128]{1,0:T(8,128)(2,1)S(1)} collective-permute-done((bf16[640,128]{1,0:T(8,128)(2,1)S(1)}, bf16[640,128]{1,0:T(8,128)(2,1)S(1)}, u32[]{:S(2)}, u32[]{:S(2)}) %collective-permute-start.16) | collective-permute-done | bytes 163872 | tf_op jit(solution)/shard_map/ppermute | solution.py:396
  90.1 6.5 %collective-permute-done.17.refs_2_ = bf16[640,128]{1,0:T(8,128)(2,1)S(1)} collective-permute-done((bf16[640,128]{1,0:T(8,128)(2,1)S(1)}, bf16[640,128]{1,0:T(8,128)(2,1)S(1)}, u32[]{:S(2)}, u32[]{:S(2)}) %collective-permute-start.17) | collective-permute-done | bytes 163872 | tf_op jit(solution)/shard_map/ppermute | solution.py:396
  96.6 0.2 collective-permute-done.18.refs_3_
  96.9 2.2 %collective-permute-start.19 = (bf16[2560,128]{1,0:T(8,128)(2,1)S(1)}, bf16[2560,128]{1,0:T(8,128)(2,1)S(1)}, u32[]{:S(2)}, u32[]{:S(2)}) collective-permute-start(bf16[2560,128]{1,0:T(8,128)(2,1)S(1)} %place_x.1.mine_ref), channel_id=1, source_target_pairs={{0,1},{1,0},{2,3},{3,2},{4,5},{5,4},{6,7},{7,6},{8,9},{9,8},{10,11... | collective-permute-start | bytes 1966088 | tf_op jit(solution)/shard_map/ppermute | solution.py:400
  99.1 1.7 %collective-permute-done.19.other_ref = bf16[2560,128]{1,0:T(8,128)(2,1)S(1)} collective-permute-done((bf16[2560,128]{1,0:T(8,128)(2,1)S(1)}, bf16[2560,128]{1,0:T(8,128)(2,1)S(1)}, u32[]{:S(2)}, u32[]{:S(2)}) %collective-permute-start.19) | collective-permute-done | bytes 655392 | tf_op jit(solution)/shard_map/ppermute | solution.py:400
  100.8 1.7 %table.1 = f32[400,1500]{1,0:T(8,128)} custom-call(s32[1]{0:T(128)} %bitcast.core_ref, bf16[2560,128]{1,0:T(8,128)(2,1)S(1)} %place_x.1.mine_ref, bf16[2560,128]{1,0:T(8,128)(2,1)S(1)} %collective-permute-done.19.other_ref), custom_call_target="tpu_custom_call" | custom-call | flops 1000000 | bytes 100000 | tf_op jit(solution)/shard_map/table/pallas_call | solution.py:390
  102.5 1.8 %all-to-all-done.1 = bf16[256,16,128]{2,1,0:T(8,128)(2,1)S(1)} async-done(((bf16[256,16,128]{2,1,0:T(8,128)(2,1)}), bf16[256,16,128]{2,1,0:T(8,128)(2,1)S(1)}, u32[]{:S(2)}, u32[]{:S(2)}) %all-to-all-start.1) | async-done | bytes 1048608 | tf_op jit(solution)/shard_map/all_to_all | solution.py:435
  104.3 3.4 %partition.1 = f32[100,1024]{1,0:T(8,128)} custom-call(bf16[4096,128]{1,0:T(8,128)(2,1)S(1)} %bitcast.14), custom_call_target="tpu_custom_call" | custom-call | flops 1000000 | bytes 100000 | tf_op jit(solution)/shard_map/partition/pallas_call | solution.py:280
  (28 shorter events, 0.2 us)
Async XLA Ops:
  0.6 14.7 %collective-permute-start = (bf16[400,256]{1,0:T(8,128)(2,1)}, bf16[400,256]{1,0:T(8,128)(2,1)S(1)}, u32[]{:S(2)}, u32[]{:S(2)}) collective-permute-start(bf16[400,256]{1,0:T(8,128)(2,1)} %bitcast.20), channel_id=1, source_target_pairs={{0,64},{64,128},{128,192},{192,0},{1,65},{65,129},{129,193},{193,1... | collective-permute-start | bytes 614408 | tf_op jit(solution)/shard_map/ppermute | solution.py:396
  2.7 12.6 %collective-permute-start.1 = (bf16[400,256]{1,0:T(8,128)(2,1)}, bf16[400,256]{1,0:T(8,128)(2,1)S(1)}, u32[]{:S(2)}, u32[]{:S(2)}) collective-permute-start(bf16[400,256]{1,0:T(8,128)(2,1)} %bitcast.21), channel_id=1, source_target_pairs={{0,128},{64,192},{128,0},{192,64},{1,129},{65,193},{129,1},{193,65... | collective-permute-start | bytes 614408 | tf_op jit(solution)/shard_map/ppermute | solution.py:396
  5.2 10.2 %collective-permute-start.2 = (bf16[400,256]{1,0:T(8,128)(2,1)}, bf16[400,256]{1,0:T(8,128)(2,1)S(1)}, u32[]{:S(2)}, u32[]{:S(2)}) collective-permute-start(bf16[400,256]{1,0:T(8,128)(2,1)} %bitcast.22), channel_id=1, source_target_pairs={{0,192},{64,0},{128,64},{192,128},{1,193},{65,1},{129,65},{193,129... | collective-permute-start | bytes 614408 | tf_op jit(solution)/shard_map/ppermute | solution.py:396
  7.2 1.7 %copy-start = (f32[1500,400]{0,1:T(8,128)S(1)}, f32[1500,400]{0,1:T(8,128)}, u32[]{:S(2)}) copy-start(f32[1500,400]{0,1:T(8,128)} %param.14) | copy-start | bytes 7200004
  8.9 1.1 copy-start.1
  10.0 1.1 copy-start.3
  11.0 4.3 %copy-start.2 = (bf16[768,400]{0,1:T(8,128)(2,1)S(1)}, bf16[768,400]{0,1:T(8,128)(2,1)}, u32[]{:S(2)}) copy-start(bf16[768,400]{0,1:T(8,128)(2,1)} %param.10) | copy-start | bytes 1843204
  11.0 4.3 %copy-start.4 = (bf16[768,400]{0,1:T(8,128)(2,1)S(1)}, bf16[768,400]{0,1:T(8,128)(2,1)}, u32[]{:S(2)}) copy-start(bf16[768,400]{0,1:T(8,128)(2,1)} %param.11) | copy-start | bytes 1843204
  11.0 4.3 %copy-start.5 = (bf16[256,400]{0,1:T(8,128)(2,1)S(1)}, bf16[256,400]{0,1:T(8,128)(2,1)}, u32[]{:S(2)}) copy-start(bf16[256,400]{0,1:T(8,128)(2,1)} %param.13) | copy-start | bytes 614404
  25.7 5.5 %copy-start.6 = (bf16[400,1536]{1,0:T(8,128)(2,1)}, bf16[400,1536]{1,0:T(8,128)(2,1)S(1)}, u32[]{:S(2)}) copy-start(bf16[400,1536]{1,0:T(8,128)(2,1)S(1)} %get-tuple-element.38.rows_ref) | copy-start | bytes 3686404
  25.7 4.4 %collective-permute-start.3 = (f32[400,768]{1,0:T(8,128)S(1)}, f32[400,768]{1,0:T(8,128)S(1)}, u32[]{:S(2)}, u32[]{:S(2)}) collective-permute-start(f32[400,768]{1,0:T(8,128)S(1)} %get-tuple-element.30), channel_id=1, source_target_pairs={{0,1},{1,0},{2,3},{3,2},{4,5},{5,4},{6,7},{7,6},{8,9},{9,8},{10,11... | collective-permute-start | bytes 3686408 | tf_op jit(solution)/shard_map/ppermute | solution.py:400
  27.3 13.8 %collective-permute-start.4 = (bf16[400,256]{1,0:T(8,128)(2,1)S(1)}, bf16[400,256]{1,0:T(8,128)(2,1)S(1)}, u32[]{:S(2)}, u32[]{:S(2)}) collective-permute-start(bf16[400,256]{1,0:T(8,128)(2,1)S(1)} %get-tuple-element.33), channel_id=1, source_target_pairs={{0,192},{64,0},{128,64},{192,128},{1,193},{65,1},{129,65},{193,129... | collective-permute-start | bytes 614408 | tf_op jit(solution)/shard_map/ppermute | solution.py:396
  28.2 13.0 %collective-permute-start.5 = (bf16[400,256]{1,0:T(8,128)(2,1)S(1)}, bf16[400,256]{1,0:T(8,128)(2,1)S(1)}, u32[]{:S(2)}, u32[]{:S(2)}) collective-permute-start(bf16[400,256]{1,0:T(8,128)(2,1)S(1)} %get-tuple-element.34), channel_id=1, source_target_pairs={{0,128},{64,192},{128,0},{192,64},{1,129},{65,193},{129,1},{193,65... | collective-permute-start | bytes 614408 | tf_op jit(solution)/shard_map/ppermute | solution.py:396
  29.4 11.7 %collective-permute-start.6 = (bf16[400,256]{1,0:T(8,128)(2,1)S(1)}, bf16[400,256]{1,0:T(8,128)(2,1)S(1)}, u32[]{:S(2)}, u32[]{:S(2)}) collective-permute-start(bf16[400,256]{1,0:T(8,128)(2,1)S(1)} %get-tuple-element.35), channel_id=1, source_target_pairs={{0,64},{64,128},{128,192},{192,0},{1,65},{65,129},{129,193},{193,1... | collective-permute-start | bytes 614408 | tf_op jit(solution)/shard_map/ppermute | solution.py:396
  31.2 17.9 %all-to-all-start = ((bf16[16,160,128]{2,1,0:T(8,128)(2,1)}), bf16[16,160,128]{2,1,0:T(8,128)(2,1)S(1)}, u32[]{:S(2)}, u32[]{:S(2)}) async-start(bf16[16,160,128]{2,1,0:T(8,128)(2,1)} %bitcast.7), calls=%async_computation | async-start | bytes 1310720 | tf_op jit(solution)/shard_map/all_to_all | solution.py:427
  37.4 1.3 %copy-start.7 = (bf16[400,1536]{1,0:T(8,128)(2,1)S(1)}, bf16[400,1536]{1,0:T(8,128)(2,1)}, u32[]{:S(2)}) copy-start(bf16[400,1536]{1,0:T(8,128)(2,1)} %copy-done.6) | copy-start | bytes 3686404
  49.2 3.2 %collective-permute-start.7 = (bf16[160,128]{1,0:T(8,128)(2,1)S(1)}, bf16[160,128]{1,0:T(8,128)(2,1)S(1)}, u32[]{:S(2)}, u32[]{:S(2)}) collective-permute-start(bf16[160,128]{1,0:T(8,128)(2,1)S(1)} %rel_xy.1.mine_ref.own_ref), channel_id=1, source_target_pairs={{0,1},{1,0},{2,3},{3,2},{4,5},{5,4},{6,7},{7,6},{8,9},{9,8},{10,11... | collective-permute-start | bytes 122888 | tf_op jit(solution)/shard_map/ppermute | solution.py:400
  52.4 19.5 %collective-permute-start.10 = (bf16[320,128]{1,0:T(8,128)(2,1)S(1)}, bf16[320,128]{1,0:T(8,128)(2,1)S(1)}, u32[]{:S(2)}, u32[]{:S(2)}) collective-permute-start(bf16[320,128]{1,0:T(8,128)(2,1)S(1)} %chip_pair.1), channel_id=1, source_target_pairs={{0,6},{1,11},{2,8},{3,13},{4,10},{5,15},{6,12},{7,1},{8,14},{9,3},... | collective-permute-start | bytes 245768 | tf_op jit(solution)/shard_map/ppermute | solution.py:405
  58.9 12.9 %collective-permute-start.8 = (bf16[320,128]{1,0:T(8,128)(2,1)S(1)}, bf16[320,128]{1,0:T(8,128)(2,1)S(1)}, u32[]{:S(2)}, u32[]{:S(2)}) collective-permute-start(bf16[320,128]{1,0:T(8,128)(2,1)S(1)} %chip_pair.1), channel_id=1, source_target_pairs={{0,2},{1,15},{2,4},{3,1},{4,6},{5,3},{6,8},{7,5},{8,10},{9,7},{10,... | collective-permute-start | bytes 245768 | tf_op jit(solution)/shard_map/ppermute | solution.py:405
  59.6 12.2 %collective-permute-start.9 = (bf16[320,128]{1,0:T(8,128)(2,1)S(1)}, bf16[320,128]{1,0:T(8,128)(2,1)S(1)}, u32[]{:S(2)}, u32[]{:S(2)}) collective-permute-start(bf16[320,128]{1,0:T(8,128)(2,1)S(1)} %chip_pair.1), channel_id=1, source_target_pairs={{0,4},{1,13},{2,6},{3,15},{4,8},{5,1},{6,10},{7,3},{8,12},{9,5},{1... | collective-permute-start | bytes 245768 | tf_op jit(solution)/shard_map/ppermute | solution.py:405
  59.6 12.2 %collective-permute-start.11 = (bf16[160,128]{1,0:T(8,128)(2,1)S(1)}, bf16[160,128]{1,0:T(8,128)(2,1)S(1)}, u32[]{:S(2)}, u32[]{:S(2)}) collective-permute-start(bf16[160,128]{1,0:T(8,128)(2,1)S(1)} %rel_xy.1.mine_ref.own_ref), channel_id=1, source_target_pairs={{0,8},{2,10},{4,12},{6,14},{8,0},{10,2},{12,4},{14,6},{1,9},{3,11}... | collective-permute-start | bytes 122888 | tf_op jit(solution)/shard_map/ppermute | solution.py:396
  64.1 40.2 %all-to-all-start.1 = ((bf16[256,16,128]{2,1,0:T(8,128)(2,1)}), bf16[256,16,128]{2,1,0:T(8,128)(2,1)S(1)}, u32[]{:S(2)}, u32[]{:S(2)}) async-start(bf16[256,16,128]{2,1,0:T(8,128)(2,1)} %bitcast.8), calls=%async_computation.1 | async-start | bytes 2097152 | tf_op jit(solution)/shard_map/all_to_all | solution.py:435
  71.9 3.2 %collective-permute-start.12 = (bf16[480,128]{1,0:T(8,128)(2,1)S(1)}, bf16[480,128]{1,0:T(8,128)(2,1)S(1)}, u32[]{:S(2)}, u32[]{:S(2)}) collective-permute-start(bf16[480,128]{1,0:T(8,128)(2,1)S(1)} %get-tuple-element.45), channel_id=1, source_target_pairs={{0,1},{1,0},{2,3},{3,2},{4,5},{5,4},{6,7},{7,6},{8,9},{9,8},{10,11... | collective-permute-start | bytes 368648 | tf_op jit(solution)/shard_map/ppermute | solution.py:400
  75.1 6.5 %collective-permute-start.13 = (bf16[160,128]{1,0:T(8,128)(2,1)S(1)}, bf16[160,128]{1,0:T(8,128)(2,1)S(1)}, u32[]{:S(2)}, u32[]{:S(2)}) collective-permute-start(bf16[160,128]{1,0:T(8,128)(2,1)S(1)} %rel_z.1.refs_0_), channel_id=1, source_target_pairs={{0,16},{16,32},{32,48},{48,0},{1,17},{17,33},{33,49},{49,1},{2,18}... | collective-permute-start | bytes 122888 | tf_op jit(solution)/shard_map/ppermute | solution.py:396
  75.5 6.2 %collective-permute-start.14 = (bf16[160,128]{1,0:T(8,128)(2,1)S(1)}, bf16[160,128]{1,0:T(8,128)(2,1)S(1)}, u32[]{:S(2)}, u32[]{:S(2)}) collective-permute-start(bf16[160,128]{1,0:T(8,128)(2,1)S(1)} %rel_z.1.refs_0_), channel_id=1, source_target_pairs={{0,32},{16,48},{32,0},{48,16},{1,33},{17,49},{33,1},{49,17},{2,34}... | collective-permute-start | bytes 122888 | tf_op jit(solution)/shard_map/ppermute | solution.py:396
  77.5 4.4 %collective-permute-start.15 = (bf16[160,128]{1,0:T(8,128)(2,1)S(1)}, bf16[160,128]{1,0:T(8,128)(2,1)S(1)}, u32[]{:S(2)}, u32[]{:S(2)}) collective-permute-start(bf16[160,128]{1,0:T(8,128)(2,1)S(1)} %rel_z.1.refs_0_), channel_id=1, source_target_pairs={{0,48},{16,0},{32,16},{48,32},{1,49},{17,1},{33,17},{49,33},{2,50}... | collective-permute-start | bytes 122888 | tf_op jit(solution)/shard_map/ppermute | solution.py:396
  81.9 8.2 %collective-permute-start.16 = (bf16[640,128]{1,0:T(8,128)(2,1)S(1)}, bf16[640,128]{1,0:T(8,128)(2,1)S(1)}, u32[]{:S(2)}, u32[]{:S(2)}) collective-permute-start(bf16[640,128]{1,0:T(8,128)(2,1)S(1)} %place_y.1.refs_0_), channel_id=1, source_target_pairs={{0,64},{64,128},{128,192},{192,0},{1,65},{65,129},{129,193},{193,1... | collective-permute-start | bytes 491528 | tf_op jit(solution)/shard_map/ppermute | solution.py:396
  82.5 14.1 %collective-permute-start.17 = (bf16[640,128]{1,0:T(8,128)(2,1)S(1)}, bf16[640,128]{1,0:T(8,128)(2,1)S(1)}, u32[]{:S(2)}, u32[]{:S(2)}) collective-permute-start(bf16[640,128]{1,0:T(8,128)(2,1)S(1)} %place_y.1.refs_0_), channel_id=1, source_target_pairs={{0,128},{64,192},{128,0},{192,64},{1,129},{65,193},{129,1},{193,65... | collective-permute-start | bytes 491528 | tf_op jit(solution)/shard_map/ppermute | solution.py:396
  85.1 11.7 %collective-permute-start.18 = (bf16[640,128]{1,0:T(8,128)(2,1)S(1)}, bf16[640,128]{1,0:T(8,128)(2,1)S(1)}, u32[]{:S(2)}, u32[]{:S(2)}) collective-permute-start(bf16[640,128]{1,0:T(8,128)(2,1)S(1)} %place_y.1.refs_0_), channel_id=1, source_target_pairs={{0,192},{64,0},{128,64},{192,128},{1,193},{65,1},{129,65},{193,129... | collective-permute-start | bytes 491528 | tf_op jit(solution)/shard_map/ppermute | solution.py:396
  96.9 3.9 %collective-permute-start.19 = (bf16[2560,128]{1,0:T(8,128)(2,1)S(1)}, bf16[2560,128]{1,0:T(8,128)(2,1)S(1)}, u32[]{:S(2)}, u32[]{:S(2)}) collective-permute-start(bf16[2560,128]{1,0:T(8,128)(2,1)S(1)} %place_x.1.mine_ref), channel_id=1, source_target_pairs={{0,1},{1,0},{2,3},{3,2},{4,5},{5,4},{6,7},{7,6},{8,9},{9,8},{10,11... | collective-permute-start | bytes 1966088 | tf_op jit(solution)/shard_map/ppermute | solution.py:400

commit v5 on v4

--- a/solution.py
+++ b/solution.py
@@ -198,8 +198,10 @@
 
     d_head = firsts[1] * m_ref[...].astype(F32) + jnp.concatenate([rr * qr + ri * qi, rr * qi - ri * qr], 0)
     d_tail = firsts[0] * q_ref[...].astype(F32) + jnp.concatenate([rr * mr - ri * mi, rr * mi + ri * mr], 0)
-    rows_ref[:, pl.ds(0, E_DEV)] = d_head.astype(BF16)
-    rows_ref[:, pl.ds(E_DEV, E_DEV)] = d_tail.astype(BF16)
+    for k, value in enumerate((d_head, d_tail)):
+        high, low = split2(value)
+        rows_ref[:, pl.ds(k * E_DEV, E_DEV)] = high
+        rows_ref[:, pl.ds((k + 2) * E_DEV, E_DEV)] = low
 
 
 def edge(core, negs, h, t, r, q, m, pos, rid):
@@ -209,8 +211,8 @@
     return call(
         edge_kernel, "edge", 1,
         [SMEM] + [full(part)] * 4 + [full(cols)] * 5 + [full((8, E_DEV)), full((1, E_DEV))],
-        [full(part)] * 4 + [full((D, 2 * E_DEV))] + [full(half)] * 2,
-        [arr(part, F32)] + [arr(part, BF16)] * 3 + [arr((D, 2 * E_DEV), BF16)] + [arr(half, F32)] * 2,
+        [full(part)] * 4 + [full((D, 4 * E_DEV))] + [full(half)] * 2,
+        [arr(part, F32)] + [arr(part, BF16)] * 3 + [arr((D, 4 * E_DEV), BF16)] + [arr(half, F32)] * 2,
         [pltpu.VMEM((D, NEG), BF16), pltpu.VMEM((NEG, D), BF16)],
         flops=10**10, mib=36,
     )(core, *negs, h, t, r, q, m, pos, rid)
@@ -219,7 +221,8 @@
 def slot_kernel(target_h_ref, target_t_ref, rows_ref, code_ref, out_ref):
     hit_h = one_hot(target_h_ref[...], U_CAP)
     hit_t = one_hot(target_t_ref[...], U_CAP)
-    total = dot_nt(hit_h, rows_ref[:, pl.ds(0, E_DEV)]) + dot_nt(hit_t, rows_ref[:, pl.ds(E_DEV, E_DEV)])
+    parts = [rows_ref[:, pl.ds(k * E_DEV, E_DEV)] for k in range(4)]
+    total = (dot_nt(hit_h, parts[0]) + dot_nt(hit_h, parts[2])) + (dot_nt(hit_t, parts[1]) + dot_nt(hit_t, parts[3]))
     code = code_ref[:, USED:]
     for k in range(N_GRP):
         out_ref[k] = jnp.concatenate([total[:, k * USED:(k + 1) * USED], code], 1)
@@ -229,7 +232,7 @@
     shape = (N_GRP, U_CAP, LANES)
     return call(
         slot_kernel, "slot", 1,
-        [full((1, E_DEV))] * 2 + [full((D, 2 * E_DEV)), full((U_CAP, LANES))],
+        [full((1, E_DEV))] * 2 + [full((D, 4 * E_DEV)), full((U_CAP, LANES))],
         full(shape), arr(shape, F32),
         flops=8 * 10**9, mib=24,
     )(th, tt, rows, code)

time: 108 us -> 108 us (level)
  Pallas kernels: 25.7 us -> 27.5 us
    all_to_all x1, waiting for transfers between devices: 5.63 us -> 3.61 us  [shards(): chip = lax.all_to_all(chip, ('x', 'y'), 0, 0, tiled=True)]
    pallas_call x1, Pallas kernels: 2.38 us -> 4 us  [slot(): call(slot_kernel, 'slot', 1, [full((1, E_DEV))] * 2 + [full((D, 4 * E_DEV...]
  transfers between devices with their start and end apart: 22 -> 22, of which waited for: 10 -> 10; matrix products, arithmetic and copies ran while one was open for 1% -> 1% of each run, Pallas kernels for 11% -> 12%
where the time goes in v5:
time: 108 us
  starting transfers between devices  49.4 us (46%)
  Pallas kernels  27.5 us (25%)
  waiting for transfers between devices  23.8 us (22%)
  local copies, waits for them, and re-layouts  6.38 us (6%)
    ppermute x13, starting transfers between devices, shift(): return lax.ppermute(value, axis, [(i, (i + k) % size) for i in range(size)])  20.1 us
    ppermute x13, waiting for transfers between devices, shift(): return lax.ppermute(value, axis, [(i, (i + k) % size) for i in range(size)])  14.8 us
    pallas_call x1, Pallas kernels, edge(): call(edge_kernel, 'edge', 1, [SMEM] + [full(part)] * 4 + [full(cols)] * 5...  10.5 us
    ppermute x4, starting transfers between devices, pair(): return lax.ppermute(value, 'c', [(0, 1), (1, 0)])  8.06 us
    all_to_all x1, starting transfers between devices, shards(): lax.all_to_all(packed.reshape(N_GRP * N_OWN, CAP, LANES), ALL, 0, 0, tile...  7.69 us
    ppermute x3, starting transfers between devices, shift_zc(): return lax.ppermute(value, ('z', 'c'), pairs)  7.27 us
    all_to_all x1, starting transfers between devices, shards(): chip = lax.all_to_all(chip, ('x', 'y'), 0, 0, tiled=True)  6.23 us
    unnamed x16, local copies, waits for them, and re-layouts  5.54 us
  transfers between devices with their start and end apart: 22, of which 10 were waited for; matrix products, arithmetic and copies ran while one was open for 1% of the time, Pallas kernels for 12%

profile of v5, /device:TPU:1, one launch (start us, length us, event | category | flops | bytes accessed | tf_op | source)
XLA Modules:
  0.0 107.9 jit_solution(990818574204713276)
XLA Ops:
  0.6 2.1 %collective-permute-start = (bf16[400,256]{1,0:T(8,128)(2,1)}, bf16[400,256]{1,0:T(8,128)(2,1)S(1)}, u32[]{:S(2)}, u32[]{:S(2)}) collective-permute-start(bf16[400,256]{1,0:T(8,128)(2,1)} %bitcast.20), channel_id=1, source_target_pairs={{0,64},{64,128},{128,192},{192,0},{1,65},{65,129},{129,193},{193,1... | collective-permute-start | bytes 614408 | tf_op jit(solution)/shard_map/ppermute | solution.py:399
  2.7 2.5 %collective-permute-start.1 = (bf16[400,256]{1,0:T(8,128)(2,1)}, bf16[400,256]{1,0:T(8,128)(2,1)S(1)}, u32[]{:S(2)}, u32[]{:S(2)}) collective-permute-start(bf16[400,256]{1,0:T(8,128)(2,1)} %bitcast.21), channel_id=1, source_target_pairs={{0,128},{64,192},{128,0},{192,64},{1,129},{65,193},{129,1},{193,65... | collective-permute-start | bytes 614408 | tf_op jit(solution)/shard_map/ppermute | solution.py:399
  5.2 1.2 %collective-permute-start.2 = (bf16[400,256]{1,0:T(8,128)(2,1)}, bf16[400,256]{1,0:T(8,128)(2,1)S(1)}, u32[]{:S(2)}, u32[]{:S(2)}) collective-permute-start(bf16[400,256]{1,0:T(8,128)(2,1)} %bitcast.22), channel_id=1, source_target_pairs={{0,192},{64,0},{128,64},{192,128},{1,193},{65,1},{129,65},{193,129... | collective-permute-start | bytes 614408 | tf_op jit(solution)/shard_map/ppermute | solution.py:399
  6.4 0.8 concatenate.3
  7.2 0.0 copy-start
  7.2 1.7 %copy-done = f32[1500,400]{0,1:T(8,128)S(1)} copy-done((f32[1500,400]{0,1:T(8,128)S(1)}, f32[1500,400]{0,1:T(8,128)}, u32[]{:S(2)}) %copy-start) | copy-done | bytes 2400024
  8.9 1.1 copy-done.1
  10.0 1.1 copy-done.3
  11.0 4.3 %prep.1 = (f32[400,768]{1,0:T(8,128)S(1)}, bf16[400,768]{1,0:T(8,128)(2,1)S(1)}, bf16[400,768]{1,0:T(8,128)(2,1)S(1)}, f32[8,768]{1,0:T(8,128)S(1)}, s32[1,768]{...) custom-call(bf16[400,768]{1,0:T(8,128)(2,1)S(1)} %bitcast.16, ...), custom_call_target="tpu_custom_call" | custom-call | flops 1000000 | bytes 100000 | tf_op jit(solution)/shard_map/prep/pallas_call | solution.py:145
  15.4 10.5 %edge.1 = (f32[400,256]{1,0:T(8,128)S(1)}, bf16[400,256]{1,0:T(8,128)(2,1)S(1)}, bf16[400,256]{1,0:T(8,128)(2,1)S(1)}, bf16[400,256]{1,0:T(8,128)(2,1)S(1)}, bf1...) custom-call(s32[1]{0:T(128)} %bitcast.core_ref, bf16[400,256]{1,0:T(8,128)(2,1)S(1)} %bitcast.23, ...), custom_call_target="tpu_custom_call" | custom-call | flops 10000000000 | bytes 100000 | tf_op jit(solution)/shard_map/edge/pallas_call | solution.py:211
  25.9 0.0 copy-start.6
  25.9 1.6 %collective-permute-start.3 = (f32[400,768]{1,0:T(8,128)S(1)}, f32[400,768]{1,0:T(8,128)S(1)}, u32[]{:S(2)}, u32[]{:S(2)}) collective-permute-start(f32[400,768]{1,0:T(8,128)S(1)} %get-tuple-element.30), channel_id=1, source_target_pairs={{0,1},{1,0},{2,3},{3,2},{4,5},{5,4},{6,7},{7,6},{8,9},{9,8},{10,11... | collective-permute-start | bytes 3686408 | tf_op jit(solution)/shard_map/ppermute | solution.py:403
  27.5 0.8 collective-permute-start.4
  28.4 1.3 %collective-permute-start.5 = (bf16[400,256]{1,0:T(8,128)(2,1)S(1)}, bf16[400,256]{1,0:T(8,128)(2,1)S(1)}, u32[]{:S(2)}, u32[]{:S(2)}) collective-permute-start(bf16[400,256]{1,0:T(8,128)(2,1)S(1)} %get-tuple-element.34), channel_id=1, source_target_pairs={{0,128},{64,192},{128,0},{192,64},{1,129},{65,193},{129,1},{193,65... | collective-permute-start | bytes 614408 | tf_op jit(solution)/shard_map/ppermute | solution.py:399
  29.6 0.7 collective-permute-start.6
  30.4 1.0 rel_chip.1
  31.4 6.2 %all-to-all-start = ((bf16[16,160,128]{2,1,0:T(8,128)(2,1)}), bf16[16,160,128]{2,1,0:T(8,128)(2,1)S(1)}, u32[]{:S(2)}, u32[]{:S(2)}) async-start(bf16[16,160,128]{2,1,0:T(8,128)(2,1)} %bitcast.7), calls=%async_computation | async-start | bytes 1310720 | tf_op jit(solution)/shard_map/all_to_all | solution.py:430
  37.7 0.0 copy-start.7
  37.7 1.7 %copy-done.7 = bf16[400,3072]{1,0:T(8,128)(2,1)S(1)} copy-done((bf16[400,3072]{1,0:T(8,128)(2,1)S(1)}, bf16[400,3072]{1,0:T(8,128)(2,1)}, u32[]{:S(2)}) %copy-start.7) | copy-done | bytes 2457624
  39.4 4.0 %slot.1.part_ref = f32[4,1024,128]{2,1,0:T(8,128)S(1)} custom-call(s32[1,768]{1,0:T(1,128)S(1)} %get-tuple-element.36.target_h_ref, s32[1,768]{1,0:T(1,128)S(1)} %get-tuple-element.37.target_t_ref, bf16[400,3072]{1,0:T(8,128)(2,1)S(1)} %copy-done.7, f32[1024,128]{1,0:T(8,128)S(1)} %get-tuple-element.39.code_ref), custom_call_target="tpu_custom_call" | custom-call | flops 8000000000 | bytes 100000 | tf_op jit(solution)/shard_map/slot/pallas_call | solution.py:233
  43.4 2.3 %pack.1 = bf16[4,1024,128]{2,1,0:T(8,128)(2,1)} custom-call(s32[1,256]{1,0:T(1,128)S(1)} %get-tuple-element.31.target_ref, f32[400,256]{1,0:T(8,128)S(1)} %get-tuple-element.32.own_ref, bf16[400,256]{1,0:T(8,128)(2,1)S(1)} %collective-permute-done.4.g1_ref, bf16[400,256]{1,0:T(8,128)(2,1)S(1)} %collective-permute-done.5.g2_ref, ...), custom_call_target="tpu_custom_call" | custom-call | flops 3000000000 | bytes 100000 | tf_op jit(solution)/shard_map/pack/pallas_call | solution.py:252
  45.7 3.6 %all-to-all-done.in_ref = bf16[16,160,128]{2,1,0:T(8,128)(2,1)S(1)} async-done(((bf16[16,160,128]{2,1,0:T(8,128)(2,1)}), bf16[16,160,128]{2,1,0:T(8,128)(2,1)S(1)}, u32[]{:S(2)}, u32[]{:S(2)}) %all-to-all-start) | async-done | bytes 655392 | tf_op jit(solution)/shard_map/all_to_all | solution.py:430
  49.3 0.1 rel_xy.1.mine_ref.own_ref
  49.4 2.3 %collective-permute-start.7 = (bf16[160,128]{1,0:T(8,128)(2,1)S(1)}, bf16[160,128]{1,0:T(8,128)(2,1)S(1)}, u32[]{:S(2)}, u32[]{:S(2)}) collective-permute-start(bf16[160,128]{1,0:T(8,128)(2,1)S(1)} %rel_xy.1.mine_ref.own_ref), channel_id=1, source_target_pairs={{0,1},{1,0},{2,3},{3,2},{4,5},{5,4},{6,7},{7,6},{8,9},{9,8},{10,11... | collective-permute-start | bytes 122888 | tf_op jit(solution)/shard_map/ppermute | solution.py:403
  51.7 0.9 collective-permute-done.7.other_ref
  52.6 6.5 %collective-permute-start.10 = (bf16[320,128]{1,0:T(8,128)(2,1)S(1)}, bf16[320,128]{1,0:T(8,128)(2,1)S(1)}, u32[]{:S(2)}, u32[]{:S(2)}) collective-permute-start(bf16[320,128]{1,0:T(8,128)(2,1)S(1)} %chip_pair.1), channel_id=1, source_target_pairs={{0,6},{1,11},{2,8},{3,13},{4,10},{5,15},{6,12},{7,1},{8,14},{9,3},... | collective-permute-start | bytes 245768 | tf_op jit(solution)/shard_map/ppermute | solution.py:408
  59.1 0.7 collective-permute-start.8
  59.8 4.5 %collective-permute-start.11 = (bf16[160,128]{1,0:T(8,128)(2,1)S(1)}, bf16[160,128]{1,0:T(8,128)(2,1)S(1)}, u32[]{:S(2)}, u32[]{:S(2)}) collective-permute-start(bf16[160,128]{1,0:T(8,128)(2,1)S(1)} %rel_xy.1.mine_ref.own_ref), channel_id=1, source_target_pairs={{0,8},{2,10},{4,12},{6,14},{8,0},{10,2},{12,4},{14,6},{1,9},{3,11}... | collective-permute-start | bytes 122888 | tf_op jit(solution)/shard_map/ppermute | solution.py:399
  64.3 7.7 %all-to-all-start.1 = ((bf16[256,16,128]{2,1,0:T(8,128)(2,1)}), bf16[256,16,128]{2,1,0:T(8,128)(2,1)S(1)}, u32[]{:S(2)}, u32[]{:S(2)}) async-start(bf16[256,16,128]{2,1,0:T(8,128)(2,1)} %bitcast.8), calls=%async_computation.1 | async-start | bytes 2097152 | tf_op jit(solution)/shard_map/all_to_all | solution.py:438
  72.1 2.2 %collective-permute-start.12 = (bf16[480,128]{1,0:T(8,128)(2,1)S(1)}, bf16[480,128]{1,0:T(8,128)(2,1)S(1)}, u32[]{:S(2)}, u32[]{:S(2)}) collective-permute-start(bf16[480,128]{1,0:T(8,128)(2,1)S(1)} %get-tuple-element.45), channel_id=1, source_target_pairs={{0,1},{1,0},{2,3},{3,2},{4,5},{5,4},{6,7},{7,6},{8,9},{9,8},{10,11... | collective-permute-start | bytes 368648 | tf_op jit(solution)/shard_map/ppermute | solution.py:403
  74.3 1.0 collective-permute-done.12.other_ref
  75.3 0.1 rel_z.1.refs_0_
  75.4 0.1 collective-permute-start.13
  75.5 2.0 %collective-permute-start.14 = (bf16[160,128]{1,0:T(8,128)(2,1)S(1)}, bf16[160,128]{1,0:T(8,128)(2,1)S(1)}, u32[]{:S(2)}, u32[]{:S(2)}) collective-permute-start(bf16[160,128]{1,0:T(8,128)(2,1)S(1)} %rel_z.1.refs_0_), channel_id=1, source_target_pairs={{0,32},{16,48},{32,0},{48,16},{1,33},{17,49},{33,1},{49,17},{2,34}... | collective-permute-start | bytes 122888 | tf_op jit(solution)/shard_map/ppermute | solution.py:399
  77.5 1.1 %collective-permute-start.15 = (bf16[160,128]{1,0:T(8,128)(2,1)S(1)}, bf16[160,128]{1,0:T(8,128)(2,1)S(1)}, u32[]{:S(2)}, u32[]{:S(2)}) collective-permute-start(bf16[160,128]{1,0:T(8,128)(2,1)S(1)} %rel_z.1.refs_0_), channel_id=1, source_target_pairs={{0,48},{16,0},{32,16},{48,32},{1,49},{17,1},{33,17},{49,33},{2,50}... | collective-permute-start | bytes 122888 | tf_op jit(solution)/shard_map/ppermute | solution.py:399
  78.6 3.1 %collective-permute-done.13.refs_1_ = bf16[160,128]{1,0:T(8,128)(2,1)S(1)} collective-permute-done((bf16[160,128]{1,0:T(8,128)(2,1)S(1)}, bf16[160,128]{1,0:T(8,128)(2,1)S(1)}, u32[]{:S(2)}, u32[]{:S(2)}) %collective-permute-start.13) | collective-permute-done | bytes 40992 | tf_op jit(solution)/shard_map/ppermute | solution.py:399
  81.7 0.7 collective-permute-done.15.refs_3_
  82.4 0.1 collective-permute-start.16
  82.5 2.3 %collective-permute-start.17 = (bf16[640,128]{1,0:T(8,128)(2,1)S(1)}, bf16[640,128]{1,0:T(8,128)(2,1)S(1)}, u32[]{:S(2)}, u32[]{:S(2)}) collective-permute-start(bf16[640,128]{1,0:T(8,128)(2,1)S(1)} %place_y.1.refs_0_), channel_id=1, source_target_pairs={{0,128},{64,192},{128,0},{192,64},{1,129},{65,193},{129,1},{193,65... | collective-permute-start | bytes 491528 | tf_op jit(solution)/shard_map/ppermute | solution.py:399
  84.9 1.4 %collective-permute-start.18 = (bf16[640,128]{1,0:T(8,128)(2,1)S(1)}, bf16[640,128]{1,0:T(8,128)(2,1)S(1)}, u32[]{:S(2)}, u32[]{:S(2)}) collective-permute-start(bf16[640,128]{1,0:T(8,128)(2,1)S(1)} %place_y.1.refs_0_), channel_id=1, source_target_pairs={{0,192},{64,0},{128,64},{192,128},{1,193},{65,1},{129,65},{193,129... | collective-permute-start | bytes 491528 | tf_op jit(solution)/shard_map/ppermute | solution.py:399
  86.3 6.2 %collective-permute-done.16.refs_1_ = bf16[640,128]{1,0:T(8,128)(2,1)S(1)} collective-permute-done((bf16[640,128]{1,0:T(8,128)(2,1)S(1)}, bf16[640,128]{1,0:T(8,128)(2,1)S(1)}, u32[]{:S(2)}, u32[]{:S(2)}) %collective-permute-start.16) | collective-permute-done | bytes 163872 | tf_op jit(solution)/shard_map/ppermute | solution.py:399
  92.5 3.8 %collective-permute-done.17.refs_2_ = bf16[640,128]{1,0:T(8,128)(2,1)S(1)} collective-permute-done((bf16[640,128]{1,0:T(8,128)(2,1)S(1)}, bf16[640,128]{1,0:T(8,128)(2,1)S(1)}, u32[]{:S(2)}, u32[]{:S(2)}) %collective-permute-start.17) | collective-permute-done | bytes 163872 | tf_op jit(solution)/shard_map/ppermute | solution.py:399
  96.3 1.0 collective-permute-done.18.refs_3_
  97.3 1.9 %collective-permute-start.19 = (bf16[2560,128]{1,0:T(8,128)(2,1)S(1)}, bf16[2560,128]{1,0:T(8,128)(2,1)S(1)}, u32[]{:S(2)}, u32[]{:S(2)}) collective-permute-start(bf16[2560,128]{1,0:T(8,128)(2,1)S(1)} %place_x.1.mine_ref), channel_id=1, source_target_pairs={{0,1},{1,0},{2,3},{3,2},{4,5},{5,4},{6,7},{7,6},{8,9},{9,8},{10,11... | collective-permute-start | bytes 1966088 | tf_op jit(solution)/shard_map/ppermute | solution.py:403
  99.3 1.7 %collective-permute-done.19.other_ref = bf16[2560,128]{1,0:T(8,128)(2,1)S(1)} collective-permute-done((bf16[2560,128]{1,0:T(8,128)(2,1)S(1)}, bf16[2560,128]{1,0:T(8,128)(2,1)S(1)}, u32[]{:S(2)}, u32[]{:S(2)}) %collective-permute-start.19) | collective-permute-done | bytes 655392 | tf_op jit(solution)/shard_map/ppermute | solution.py:403
  101.0 1.7 %table.1 = f32[400,1500]{1,0:T(8,128)} custom-call(s32[1]{0:T(128)} %bitcast.core_ref, bf16[2560,128]{1,0:T(8,128)(2,1)S(1)} %place_x.1.mine_ref, bf16[2560,128]{1,0:T(8,128)(2,1)S(1)} %collective-permute-done.19.other_ref), custom_call_target="tpu_custom_call" | custom-call | flops 1000000 | bytes 100000 | tf_op jit(solution)/shard_map/table/pallas_call | solution.py:393
  102.7 1.8 %all-to-all-done.1 = bf16[256,16,128]{2,1,0:T(8,128)(2,1)S(1)} async-done(((bf16[256,16,128]{2,1,0:T(8,128)(2,1)}), bf16[256,16,128]{2,1,0:T(8,128)(2,1)S(1)}, u32[]{:S(2)}, u32[]{:S(2)}) %all-to-all-start.1) | async-done | bytes 1048608 | tf_op jit(solution)/shard_map/all_to_all | solution.py:438
  104.5 3.4 %partition.1 = f32[100,1024]{1,0:T(8,128)} custom-call(bf16[4096,128]{1,0:T(8,128)(2,1)S(1)} %bitcast.14), custom_call_target="tpu_custom_call" | custom-call | flops 1000000 | bytes 100000 | tf_op jit(solution)/shard_map/partition/pallas_call | solution.py:283
  (28 shorter events, 0.2 us)
Async XLA Ops:
  0.6 14.7 %collective-permute-start = (bf16[400,256]{1,0:T(8,128)(2,1)}, bf16[400,256]{1,0:T(8,128)(2,1)S(1)}, u32[]{:S(2)}, u32[]{:S(2)}) collective-permute-start(bf16[400,256]{1,0:T(8,128)(2,1)} %bitcast.20), channel_id=1, source_target_pairs={{0,64},{64,128},{128,192},{192,0},{1,65},{65,129},{129,193},{193,1... | collective-permute-start | bytes 614408 | tf_op jit(solution)/shard_map/ppermute | solution.py:399
  2.7 12.6 %collective-permute-start.1 = (bf16[400,256]{1,0:T(8,128)(2,1)}, bf16[400,256]{1,0:T(8,128)(2,1)S(1)}, u32[]{:S(2)}, u32[]{:S(2)}) collective-permute-start(bf16[400,256]{1,0:T(8,128)(2,1)} %bitcast.21), channel_id=1, source_target_pairs={{0,128},{64,192},{128,0},{192,64},{1,129},{65,193},{129,1},{193,65... | collective-permute-start | bytes 614408 | tf_op jit(solution)/shard_map/ppermute | solution.py:399
  5.2 10.2 %collective-permute-start.2 = (bf16[400,256]{1,0:T(8,128)(2,1)}, bf16[400,256]{1,0:T(8,128)(2,1)S(1)}, u32[]{:S(2)}, u32[]{:S(2)}) collective-permute-start(bf16[400,256]{1,0:T(8,128)(2,1)} %bitcast.22), channel_id=1, source_target_pairs={{0,192},{64,0},{128,64},{192,128},{1,193},{65,1},{129,65},{193,129... | collective-permute-start | bytes 614408 | tf_op jit(solution)/shard_map/ppermute | solution.py:399
  7.2 1.7 %copy-start = (f32[1500,400]{0,1:T(8,128)S(1)}, f32[1500,400]{0,1:T(8,128)}, u32[]{:S(2)}) copy-start(f32[1500,400]{0,1:T(8,128)} %param.14) | copy-start | bytes 7200004
  8.9 1.1 copy-start.1
  10.0 1.1 copy-start.3
  11.0 4.3 %copy-start.2 = (bf16[768,400]{0,1:T(8,128)(2,1)S(1)}, bf16[768,400]{0,1:T(8,128)(2,1)}, u32[]{:S(2)}) copy-start(bf16[768,400]{0,1:T(8,128)(2,1)} %param.10) | copy-start | bytes 1843204
  11.0 4.3 %copy-start.4 = (bf16[768,400]{0,1:T(8,128)(2,1)S(1)}, bf16[768,400]{0,1:T(8,128)(2,1)}, u32[]{:S(2)}) copy-start(bf16[768,400]{0,1:T(8,128)(2,1)} %param.11) | copy-start | bytes 1843204
  11.0 4.3 %copy-start.5 = (bf16[256,400]{0,1:T(8,128)(2,1)S(1)}, bf16[256,400]{0,1:T(8,128)(2,1)}, u32[]{:S(2)}) copy-start(bf16[256,400]{0,1:T(8,128)(2,1)} %param.13) | copy-start | bytes 614404
  25.9 5.5 %copy-start.6 = (bf16[400,3072]{1,0:T(8,128)(2,1)}, bf16[400,3072]{1,0:T(8,128)(2,1)S(1)}, u32[]{:S(2)}) copy-start(bf16[400,3072]{1,0:T(8,128)(2,1)S(1)} %get-tuple-element.38.rows_ref) | copy-start | bytes 7372804
  25.9 4.4 %collective-permute-start.3 = (f32[400,768]{1,0:T(8,128)S(1)}, f32[400,768]{1,0:T(8,128)S(1)}, u32[]{:S(2)}, u32[]{:S(2)}) collective-permute-start(f32[400,768]{1,0:T(8,128)S(1)} %get-tuple-element.30), channel_id=1, source_target_pairs={{0,1},{1,0},{2,3},{3,2},{4,5},{5,4},{6,7},{7,6},{8,9},{9,8},{10,11... | collective-permute-start | bytes 3686408 | tf_op jit(solution)/shard_map/ppermute | solution.py:403
  27.5 15.8 %collective-permute-start.4 = (bf16[400,256]{1,0:T(8,128)(2,1)S(1)}, bf16[400,256]{1,0:T(8,128)(2,1)S(1)}, u32[]{:S(2)}, u32[]{:S(2)}) collective-permute-start(bf16[400,256]{1,0:T(8,128)(2,1)S(1)} %get-tuple-element.33), channel_id=1, source_target_pairs={{0,192},{64,0},{128,64},{192,128},{1,193},{65,1},{129,65},{193,129... | collective-permute-start | bytes 614408 | tf_op jit(solution)/shard_map/ppermute | solution.py:399
  28.4 15.0 %collective-permute-start.5 = (bf16[400,256]{1,0:T(8,128)(2,1)S(1)}, bf16[400,256]{1,0:T(8,128)(2,1)S(1)}, u32[]{:S(2)}, u32[]{:S(2)}) collective-permute-start(bf16[400,256]{1,0:T(8,128)(2,1)S(1)} %get-tuple-element.34), channel_id=1, source_target_pairs={{0,128},{64,192},{128,0},{192,64},{1,129},{65,193},{129,1},{193,65... | collective-permute-start | bytes 614408 | tf_op jit(solution)/shard_map/ppermute | solution.py:399
  29.6 13.7 %collective-permute-start.6 = (bf16[400,256]{1,0:T(8,128)(2,1)S(1)}, bf16[400,256]{1,0:T(8,128)(2,1)S(1)}, u32[]{:S(2)}, u32[]{:S(2)}) collective-permute-start(bf16[400,256]{1,0:T(8,128)(2,1)S(1)} %get-tuple-element.35), channel_id=1, source_target_pairs={{0,64},{64,128},{128,192},{192,0},{1,65},{65,129},{129,193},{193,1... | collective-permute-start | bytes 614408 | tf_op jit(solution)/shard_map/ppermute | solution.py:399
  31.4 17.9 %all-to-all-start = ((bf16[16,160,128]{2,1,0:T(8,128)(2,1)}), bf16[16,160,128]{2,1,0:T(8,128)(2,1)S(1)}, u32[]{:S(2)}, u32[]{:S(2)}) async-start(bf16[16,160,128]{2,1,0:T(8,128)(2,1)} %bitcast.7), calls=%async_computation | async-start | bytes 1310720 | tf_op jit(solution)/shard_map/all_to_all | solution.py:430
  37.7 1.7 %copy-start.7 = (bf16[400,3072]{1,0:T(8,128)(2,1)S(1)}, bf16[400,3072]{1,0:T(8,128)(2,1)}, u32[]{:S(2)}) copy-start(bf16[400,3072]{1,0:T(8,128)(2,1)} %copy-done.6) | copy-start | bytes 7372804
  49.4 3.2 %collective-permute-start.7 = (bf16[160,128]{1,0:T(8,128)(2,1)S(1)}, bf16[160,128]{1,0:T(8,128)(2,1)S(1)}, u32[]{:S(2)}, u32[]{:S(2)}) collective-permute-start(bf16[160,128]{1,0:T(8,128)(2,1)S(1)} %rel_xy.1.mine_ref.own_ref), channel_id=1, source_target_pairs={{0,1},{1,0},{2,3},{3,2},{4,5},{5,4},{6,7},{7,6},{8,9},{9,8},{10,11... | collective-permute-start | bytes 122888 | tf_op jit(solution)/shard_map/ppermute | solution.py:403
  52.6 19.5 %collective-permute-start.10 = (bf16[320,128]{1,0:T(8,128)(2,1)S(1)}, bf16[320,128]{1,0:T(8,128)(2,1)S(1)}, u32[]{:S(2)}, u32[]{:S(2)}) collective-permute-start(bf16[320,128]{1,0:T(8,128)(2,1)S(1)} %chip_pair.1), channel_id=1, source_target_pairs={{0,6},{1,11},{2,8},{3,13},{4,10},{5,15},{6,12},{7,1},{8,14},{9,3},... | collective-permute-start | bytes 245768 | tf_op jit(solution)/shard_map/ppermute | solution.py:408
  59.1 12.9 %collective-permute-start.8 = (bf16[320,128]{1,0:T(8,128)(2,1)S(1)}, bf16[320,128]{1,0:T(8,128)(2,1)S(1)}, u32[]{:S(2)}, u32[]{:S(2)}) collective-permute-start(bf16[320,128]{1,0:T(8,128)(2,1)S(1)} %chip_pair.1), channel_id=1, source_target_pairs={{0,2},{1,15},{2,4},{3,1},{4,6},{5,3},{6,8},{7,5},{8,10},{9,7},{10,... | collective-permute-start | bytes 245768 | tf_op jit(solution)/shard_map/ppermute | solution.py:408
  59.8 12.2 %collective-permute-start.9 = (bf16[320,128]{1,0:T(8,128)(2,1)S(1)}, bf16[320,128]{1,0:T(8,128)(2,1)S(1)}, u32[]{:S(2)}, u32[]{:S(2)}) collective-permute-start(bf16[320,128]{1,0:T(8,128)(2,1)S(1)} %chip_pair.1), channel_id=1, source_target_pairs={{0,4},{1,13},{2,6},{3,15},{4,8},{5,1},{6,10},{7,3},{8,12},{9,5},{1... | collective-permute-start | bytes 245768 | tf_op jit(solution)/shard_map/ppermute | solution.py:408
  59.8 12.2 %collective-permute-start.11 = (bf16[160,128]{1,0:T(8,128)(2,1)S(1)}, bf16[160,128]{1,0:T(8,128)(2,1)S(1)}, u32[]{:S(2)}, u32[]{:S(2)}) collective-permute-start(bf16[160,128]{1,0:T(8,128)(2,1)S(1)} %rel_xy.1.mine_ref.own_ref), channel_id=1, source_target_pairs={{0,8},{2,10},{4,12},{6,14},{8,0},{10,2},{12,4},{14,6},{1,9},{3,11}... | collective-permute-start | bytes 122888 | tf_op jit(solution)/shard_map/ppermute | solution.py:399
  64.3 40.2 %all-to-all-start.1 = ((bf16[256,16,128]{2,1,0:T(8,128)(2,1)}), bf16[256,16,128]{2,1,0:T(8,128)(2,1)S(1)}, u32[]{:S(2)}, u32[]{:S(2)}) async-start(bf16[256,16,128]{2,1,0:T(8,128)(2,1)} %bitcast.8), calls=%async_computation.1 | async-start | bytes 2097152 | tf_op jit(solution)/shard_map/all_to_all | solution.py:438
  72.1 3.2 %collective-permute-start.12 = (bf16[480,128]{1,0:T(8,128)(2,1)S(1)}, bf16[480,128]{1,0:T(8,128)(2,1)S(1)}, u32[]{:S(2)}, u32[]{:S(2)}) collective-permute-start(bf16[480,128]{1,0:T(8,128)(2,1)S(1)} %get-tuple-element.45), channel_id=1, source_target_pairs={{0,1},{1,0},{2,3},{3,2},{4,5},{5,4},{6,7},{7,6},{8,9},{9,8},{10,11... | collective-permute-start | bytes 368648 | tf_op jit(solution)/shard_map/ppermute | solution.py:403
  75.4 6.3 %collective-permute-start.13 = (bf16[160,128]{1,0:T(8,128)(2,1)S(1)}, bf16[160,128]{1,0:T(8,128)(2,1)S(1)}, u32[]{:S(2)}, u32[]{:S(2)}) collective-permute-start(bf16[160,128]{1,0:T(8,128)(2,1)S(1)} %rel_z.1.refs_0_), channel_id=1, source_target_pairs={{0,16},{16,32},{32,48},{48,0},{1,17},{17,33},{33,49},{49,1},{2,18}... | collective-permute-start | bytes 122888 | tf_op jit(solution)/shard_map/ppermute | solution.py:399
  75.5 6.3 %collective-permute-start.14 = (bf16[160,128]{1,0:T(8,128)(2,1)S(1)}, bf16[160,128]{1,0:T(8,128)(2,1)S(1)}, u32[]{:S(2)}, u32[]{:S(2)}) collective-permute-start(bf16[160,128]{1,0:T(8,128)(2,1)S(1)} %rel_z.1.refs_0_), channel_id=1, source_target_pairs={{0,32},{16,48},{32,0},{48,16},{1,33},{17,49},{33,1},{49,17},{2,34}... | collective-permute-start | bytes 122888 | tf_op jit(solution)/shard_map/ppermute | solution.py:399
  77.5 4.9 %collective-permute-start.15 = (bf16[160,128]{1,0:T(8,128)(2,1)S(1)}, bf16[160,128]{1,0:T(8,128)(2,1)S(1)}, u32[]{:S(2)}, u32[]{:S(2)}) collective-permute-start(bf16[160,128]{1,0:T(8,128)(2,1)S(1)} %rel_z.1.refs_0_), channel_id=1, source_target_pairs={{0,48},{16,0},{32,16},{48,32},{1,49},{17,1},{33,17},{49,33},{2,50}... | collective-permute-start | bytes 122888 | tf_op jit(solution)/shard_map/ppermute | solution.py:399
  82.4 10.1 %collective-permute-start.16 = (bf16[640,128]{1,0:T(8,128)(2,1)S(1)}, bf16[640,128]{1,0:T(8,128)(2,1)S(1)}, u32[]{:S(2)}, u32[]{:S(2)}) collective-permute-start(bf16[640,128]{1,0:T(8,128)(2,1)S(1)} %place_y.1.refs_0_), channel_id=1, source_target_pairs={{0,64},{64,128},{128,192},{192,0},{1,65},{65,129},{129,193},{193,1... | collective-permute-start | bytes 491528 | tf_op jit(solution)/shard_map/ppermute | solution.py:399
  82.5 13.7 %collective-permute-start.17 = (bf16[640,128]{1,0:T(8,128)(2,1)S(1)}, bf16[640,128]{1,0:T(8,128)(2,1)S(1)}, u32[]{:S(2)}, u32[]{:S(2)}) collective-permute-start(bf16[640,128]{1,0:T(8,128)(2,1)S(1)} %place_y.1.refs_0_), channel_id=1, source_target_pairs={{0,128},{64,192},{128,0},{192,64},{1,129},{65,193},{129,1},{193,65... | collective-permute-start | bytes 491528 | tf_op jit(solution)/shard_map/ppermute | solution.py:399
  84.9 12.4 %collective-permute-start.18 = (bf16[640,128]{1,0:T(8,128)(2,1)S(1)}, bf16[640,128]{1,0:T(8,128)(2,1)S(1)}, u32[]{:S(2)}, u32[]{:S(2)}) collective-permute-start(bf16[640,128]{1,0:T(8,128)(2,1)S(1)} %place_y.1.refs_0_), channel_id=1, source_target_pairs={{0,192},{64,0},{128,64},{192,128},{1,193},{65,1},{129,65},{193,129... | collective-permute-start | bytes 491528 | tf_op jit(solution)/shard_map/ppermute | solution.py:399
  97.3 3.6 %collective-permute-start.19 = (bf16[2560,128]{1,0:T(8,128)(2,1)S(1)}, bf16[2560,128]{1,0:T(8,128)(2,1)S(1)}, u32[]{:S(2)}, u32[]{:S(2)}) collective-permute-start(bf16[2560,128]{1,0:T(8,128)(2,1)S(1)} %place_x.1.mine_ref), channel_id=1, source_target_pairs={{0,1},{1,0},{2,3},{3,2},{4,5},{5,4},{6,7},{7,6},{8,9},{9,8},{10,11... | collective-permute-start | bytes 1966088 | tf_op jit(solution)/shard_map/ppermute | solution.py:403

commit v6 on v5

--- a/solution.py
+++ b/solution.py
@@ -263,7 +263,12 @@
     lane = lax.broadcasted_iota(I32, (8, LANES), 1)
     weight = jnp.where(lane == USED, 32.0, jnp.where(lane == USED + 1, 1.0, 0.0)).astype(BF16)
     ids = dot_nt(weight, rows)[:1].astype(I32)
-    term = dot(one_hot(ids, ENT_DEV), rows)
+    group = jnp.broadcast_to(rows[:, USED:USED + 1], rows.shape)
+    none = jnp.zeros((), BF16)
+    lower = jnp.where(group < 16, rows, none)
+    upper = jnp.where(group < 32, rows, none) - lower
+    both = dot(one_hot(ids & (ENT_DEV // 2 - 1), ENT_DEV // 2), jnp.concatenate([lower, upper], 1))
+    term = jnp.concatenate([both[:, :LANES], both[:, LANES:]], 0)
 
     @pl.when(step == 0)
     def _():

time: 108 us -> 108 us (level)
  transfers between devices with their start and end apart: 22 -> 22, of which waited for: 10 -> 10; matrix products, arithmetic and copies ran while one was open for 1% -> 1% of each run, Pallas kernels for 12% -> 13%
where the time goes in v6:
time: 108 us; the launch traced here: 107 us
  starting transfers between devices  49.4 us (46%)
  Pallas kernels  26.7 us (25%)
  waiting for transfers between devices  23.8 us (22%)
  local copies, waits for them, and re-layouts  6.38 us (6%)
    ppermute x13, starting transfers between devices, shift(): return lax.ppermute(value, axis, [(i, (i + k) % size) for i in range(size)])  20.1 us
    ppermute x13, waiting for transfers between devices, shift(): return lax.ppermute(value, axis, [(i, (i + k) % size) for i in range(size)])  14.8 us
    pallas_call x1, Pallas kernels, edge(): call(edge_kernel, 'edge', 1, [SMEM] + [full(part)] * 4 + [full(cols)] * 5...  10.5 us
    ppermute x4, starting transfers between devices, pair(): return lax.ppermute(value, 'c', [(0, 1), (1, 0)])  8.06 us
    all_to_all x1, starting transfers between devices, shards(): lax.all_to_all(packed.reshape(N_GRP * N_OWN, CAP, LANES), ALL, 0, 0, tile...  7.69 us
    ppermute x3, starting transfers between devices, shift_zc(): return lax.ppermute(value, ('z', 'c'), pairs)  7.27 us
    all_to_all x1, starting transfers between devices, shards(): chip = lax.all_to_all(chip, ('x', 'y'), 0, 0, tiled=True)  6.23 us
    unnamed x16, local copies, waits for them, and re-layouts  5.54 us
  transfers between devices with their start and end apart: 22, of which 10 were waited for; matrix products, arithmetic and copies ran while one was open for 1% of the time, Pallas kernels for 13%

profile of v6, /device:TPU:1, one launch (start us, length us, event | category | flops | bytes accessed | tf_op | source)
XLA Modules:
  0.0 107.2 jit_solution(18000697194136306822)
XLA Ops:
  0.6 2.1 %collective-permute-start = (bf16[400,256]{1,0:T(8,128)(2,1)}, bf16[400,256]{1,0:T(8,128)(2,1)S(1)}, u32[]{:S(2)}, u32[]{:S(2)}) collective-permute-start(bf16[400,256]{1,0:T(8,128)(2,1)} %bitcast.20), channel_id=1, source_target_pairs={{0,64},{64,128},{128,192},{192,0},{1,65},{65,129},{129,193},{193,1... | collective-permute-start | bytes 614408 | tf_op jit(solution)/shard_map/ppermute | solution.py:404
  2.7 2.5 %collective-permute-start.1 = (bf16[400,256]{1,0:T(8,128)(2,1)}, bf16[400,256]{1,0:T(8,128)(2,1)S(1)}, u32[]{:S(2)}, u32[]{:S(2)}) collective-permute-start(bf16[400,256]{1,0:T(8,128)(2,1)} %bitcast.21), channel_id=1, source_target_pairs={{0,128},{64,192},{128,0},{192,64},{1,129},{65,193},{129,1},{193,65... | collective-permute-start | bytes 614408 | tf_op jit(solution)/shard_map/ppermute | solution.py:404
  5.2 1.2 %collective-permute-start.2 = (bf16[400,256]{1,0:T(8,128)(2,1)}, bf16[400,256]{1,0:T(8,128)(2,1)S(1)}, u32[]{:S(2)}, u32[]{:S(2)}) collective-permute-start(bf16[400,256]{1,0:T(8,128)(2,1)} %bitcast.22), channel_id=1, source_target_pairs={{0,192},{64,0},{128,64},{192,128},{1,193},{65,1},{129,65},{193,129... | collective-permute-start | bytes 614408 | tf_op jit(solution)/shard_map/ppermute | solution.py:404
  6.4 0.8 concatenate.3
  7.2 0.0 copy-start
  7.2 1.7 %copy-done = f32[1500,400]{0,1:T(8,128)S(1)} copy-done((f32[1500,400]{0,1:T(8,128)S(1)}, f32[1500,400]{0,1:T(8,128)}, u32[]{:S(2)}) %copy-start) | copy-done | bytes 2400024
  8.9 1.1 copy-done.1
  10.0 1.1 copy-done.3
  11.0 4.3 %prep.1 = (f32[400,768]{1,0:T(8,128)S(1)}, bf16[400,768]{1,0:T(8,128)(2,1)S(1)}, bf16[400,768]{1,0:T(8,128)(2,1)S(1)}, f32[8,768]{1,0:T(8,128)S(1)}, s32[1,768]{...) custom-call(bf16[400,768]{1,0:T(8,128)(2,1)S(1)} %bitcast.16, ...), custom_call_target="tpu_custom_call" | custom-call | flops 1000000 | bytes 100000 | tf_op jit(solution)/shard_map/prep/pallas_call | solution.py:145
  15.4 10.5 %edge.1 = (f32[400,256]{1,0:T(8,128)S(1)}, bf16[400,256]{1,0:T(8,128)(2,1)S(1)}, bf16[400,256]{1,0:T(8,128)(2,1)S(1)}, bf16[400,256]{1,0:T(8,128)(2,1)S(1)}, bf1...) custom-call(s32[1]{0:T(128)} %bitcast.core_ref, bf16[400,256]{1,0:T(8,128)(2,1)S(1)} %bitcast.23, ...), custom_call_target="tpu_custom_call" | custom-call | flops 10000000000 | bytes 100000 | tf_op jit(solution)/shard_map/edge/pallas_call | solution.py:211
  25.9 0.0 copy-start.6
  25.9 1.6 %collective-permute-start.3 = (f32[400,768]{1,0:T(8,128)S(1)}, f32[400,768]{1,0:T(8,128)S(1)}, u32[]{:S(2)}, u32[]{:S(2)}) collective-permute-start(f32[400,768]{1,0:T(8,128)S(1)} %get-tuple-element.30), channel_id=1, source_target_pairs={{0,1},{1,0},{2,3},{3,2},{4,5},{5,4},{6,7},{7,6},{8,9},{9,8},{10,11... | collective-permute-start | bytes 3686408 | tf_op jit(solution)/shard_map/ppermute | solution.py:408
  27.5 0.8 collective-permute-start.4
  28.4 1.3 %collective-permute-start.5 = (bf16[400,256]{1,0:T(8,128)(2,1)S(1)}, bf16[400,256]{1,0:T(8,128)(2,1)S(1)}, u32[]{:S(2)}, u32[]{:S(2)}) collective-permute-start(bf16[400,256]{1,0:T(8,128)(2,1)S(1)} %get-tuple-element.34), channel_id=1, source_target_pairs={{0,128},{64,192},{128,0},{192,64},{1,129},{65,193},{129,1},{193,65... | collective-permute-start | bytes 614408 | tf_op jit(solution)/shard_map/ppermute | solution.py:404
  29.6 0.7 collective-permute-start.6
  30.4 1.0 rel_chip.1
  31.4 6.2 %all-to-all-start = ((bf16[16,160,128]{2,1,0:T(8,128)(2,1)}), bf16[16,160,128]{2,1,0:T(8,128)(2,1)S(1)}, u32[]{:S(2)}, u32[]{:S(2)}) async-start(bf16[16,160,128]{2,1,0:T(8,128)(2,1)} %bitcast.7), calls=%async_computation | async-start | bytes 1310720 | tf_op jit(solution)/shard_map/all_to_all | solution.py:435
  37.7 0.0 copy-start.7
  37.7 1.7 %copy-done.7 = bf16[400,3072]{1,0:T(8,128)(2,1)S(1)} copy-done((bf16[400,3072]{1,0:T(8,128)(2,1)S(1)}, bf16[400,3072]{1,0:T(8,128)(2,1)}, u32[]{:S(2)}) %copy-start.7) | copy-done | bytes 2457624
  39.4 4.0 %slot.1.part_ref = f32[4,1024,128]{2,1,0:T(8,128)S(1)} custom-call(s32[1,768]{1,0:T(1,128)S(1)} %get-tuple-element.36.target_h_ref, s32[1,768]{1,0:T(1,128)S(1)} %get-tuple-element.37.target_t_ref, bf16[400,3072]{1,0:T(8,128)(2,1)S(1)} %copy-done.7, f32[1024,128]{1,0:T(8,128)S(1)} %get-tuple-element.39.code_ref), custom_call_target="tpu_custom_call" | custom-call | flops 8000000000 | bytes 100000 | tf_op jit(solution)/shard_map/slot/pallas_call | solution.py:233
  43.4 2.3 %pack.1 = bf16[4,1024,128]{2,1,0:T(8,128)(2,1)} custom-call(s32[1,256]{1,0:T(1,128)S(1)} %get-tuple-element.31.target_ref, f32[400,256]{1,0:T(8,128)S(1)} %get-tuple-element.32.own_ref, bf16[400,256]{1,0:T(8,128)(2,1)S(1)} %collective-permute-done.4.g1_ref, bf16[400,256]{1,0:T(8,128)(2,1)S(1)} %collective-permute-done.5.g2_ref, ...), custom_call_target="tpu_custom_call" | custom-call | flops 3000000000 | bytes 100000 | tf_op jit(solution)/shard_map/pack/pallas_call | solution.py:252
  45.7 3.6 %all-to-all-done.in_ref = bf16[16,160,128]{2,1,0:T(8,128)(2,1)S(1)} async-done(((bf16[16,160,128]{2,1,0:T(8,128)(2,1)}), bf16[16,160,128]{2,1,0:T(8,128)(2,1)S(1)}, u32[]{:S(2)}, u32[]{:S(2)}) %all-to-all-start) | async-done | bytes 655392 | tf_op jit(solution)/shard_map/all_to_all | solution.py:435
  49.3 0.1 rel_xy.1.mine_ref.own_ref
  49.4 2.3 %collective-permute-start.7 = (bf16[160,128]{1,0:T(8,128)(2,1)S(1)}, bf16[160,128]{1,0:T(8,128)(2,1)S(1)}, u32[]{:S(2)}, u32[]{:S(2)}) collective-permute-start(bf16[160,128]{1,0:T(8,128)(2,1)S(1)} %rel_xy.1.mine_ref.own_ref), channel_id=1, source_target_pairs={{0,1},{1,0},{2,3},{3,2},{4,5},{5,4},{6,7},{7,6},{8,9},{9,8},{10,11... | collective-permute-start | bytes 122888 | tf_op jit(solution)/shard_map/ppermute | solution.py:408
  51.7 0.9 collective-permute-done.7.other_ref
  52.6 6.5 %collective-permute-start.10 = (bf16[320,128]{1,0:T(8,128)(2,1)S(1)}, bf16[320,128]{1,0:T(8,128)(2,1)S(1)}, u32[]{:S(2)}, u32[]{:S(2)}) collective-permute-start(bf16[320,128]{1,0:T(8,128)(2,1)S(1)} %chip_pair.1), channel_id=1, source_target_pairs={{0,6},{1,11},{2,8},{3,13},{4,10},{5,15},{6,12},{7,1},{8,14},{9,3},... | collective-permute-start | bytes 245768 | tf_op jit(solution)/shard_map/ppermute | solution.py:413
  59.1 0.7 collective-permute-start.8
  59.8 4.5 %collective-permute-start.11 = (bf16[160,128]{1,0:T(8,128)(2,1)S(1)}, bf16[160,128]{1,0:T(8,128)(2,1)S(1)}, u32[]{:S(2)}, u32[]{:S(2)}) collective-permute-start(bf16[160,128]{1,0:T(8,128)(2,1)S(1)} %rel_xy.1.mine_ref.own_ref), channel_id=1, source_target_pairs={{0,8},{2,10},{4,12},{6,14},{8,0},{10,2},{12,4},{14,6},{1,9},{3,11}... | collective-permute-start | bytes 122888 | tf_op jit(solution)/shard_map/ppermute | solution.py:404
  64.3 7.7 %all-to-all-start.1 = ((bf16[256,16,128]{2,1,0:T(8,128)(2,1)}), bf16[256,16,128]{2,1,0:T(8,128)(2,1)S(1)}, u32[]{:S(2)}, u32[]{:S(2)}) async-start(bf16[256,16,128]{2,1,0:T(8,128)(2,1)} %bitcast.8), calls=%async_computation.1 | async-start | bytes 2097152 | tf_op jit(solution)/shard_map/all_to_all | solution.py:443
  72.1 2.2 %collective-permute-start.12 = (bf16[480,128]{1,0:T(8,128)(2,1)S(1)}, bf16[480,128]{1,0:T(8,128)(2,1)S(1)}, u32[]{:S(2)}, u32[]{:S(2)}) collective-permute-start(bf16[480,128]{1,0:T(8,128)(2,1)S(1)} %get-tuple-element.45), channel_id=1, source_target_pairs={{0,1},{1,0},{2,3},{3,2},{4,5},{5,4},{6,7},{7,6},{8,9},{9,8},{10,11... | collective-permute-start | bytes 368648 | tf_op jit(solution)/shard_map/ppermute | solution.py:408
  74.3 1.0 collective-permute-done.12.other_ref
  75.3 0.1 rel_z.1.refs_0_
  75.4 0.1 collective-permute-start.13
  75.5 2.0 %collective-permute-start.14 = (bf16[160,128]{1,0:T(8,128)(2,1)S(1)}, bf16[160,128]{1,0:T(8,128)(2,1)S(1)}, u32[]{:S(2)}, u32[]{:S(2)}) collective-permute-start(bf16[160,128]{1,0:T(8,128)(2,1)S(1)} %rel_z.1.refs_0_), channel_id=1, source_target_pairs={{0,32},{16,48},{32,0},{48,16},{1,33},{17,49},{33,1},{49,17},{2,34}... | collective-permute-start | bytes 122888 | tf_op jit(solution)/shard_map/ppermute | solution.py:404
  77.5 1.1 %collective-permute-start.15 = (bf16[160,128]{1,0:T(8,128)(2,1)S(1)}, bf16[160,128]{1,0:T(8,128)(2,1)S(1)}, u32[]{:S(2)}, u32[]{:S(2)}) collective-permute-start(bf16[160,128]{1,0:T(8,128)(2,1)S(1)} %rel_z.1.refs_0_), channel_id=1, source_target_pairs={{0,48},{16,0},{32,16},{48,32},{1,49},{17,1},{33,17},{49,33},{2,50}... | collective-permute-start | bytes 122888 | tf_op jit(solution)/shard_map/ppermute | solution.py:404
  78.6 3.1 %collective-permute-done.13.refs_1_ = bf16[160,128]{1,0:T(8,128)(2,1)S(1)} collective-permute-done((bf16[160,128]{1,0:T(8,128)(2,1)S(1)}, bf16[160,128]{1,0:T(8,128)(2,1)S(1)}, u32[]{:S(2)}, u32[]{:S(2)}) %collective-permute-start.13) | collective-permute-done | bytes 40992 | tf_op jit(solution)/shard_map/ppermute | solution.py:404
  81.7 0.7 collective-permute-done.15.refs_3_
  82.4 0.1 collective-permute-start.16
  82.5 2.3 %collective-permute-start.17 = (bf16[640,128]{1,0:T(8,128)(2,1)S(1)}, bf16[640,128]{1,0:T(8,128)(2,1)S(1)}, u32[]{:S(2)}, u32[]{:S(2)}) collective-permute-start(bf16[640,128]{1,0:T(8,128)(2,1)S(1)} %place_y.1.refs_0_), channel_id=1, source_target_pairs={{0,128},{64,192},{128,0},{192,64},{1,129},{65,193},{129,1},{193,65... | collective-permute-start | bytes 491528 | tf_op jit(solution)/shard_map/ppermute | solution.py:404
  84.9 1.4 %collective-permute-start.18 = (bf16[640,128]{1,0:T(8,128)(2,1)S(1)}, bf16[640,128]{1,0:T(8,128)(2,1)S(1)}, u32[]{:S(2)}, u32[]{:S(2)}) collective-permute-start(bf16[640,128]{1,0:T(8,128)(2,1)S(1)} %place_y.1.refs_0_), channel_id=1, source_target_pairs={{0,192},{64,0},{128,64},{192,128},{1,193},{65,1},{129,65},{193,129... | collective-permute-start | bytes 491528 | tf_op jit(solution)/shard_map/ppermute | solution.py:404
  86.3 6.2 %collective-permute-done.16.refs_1_ = bf16[640,128]{1,0:T(8,128)(2,1)S(1)} collective-permute-done((bf16[640,128]{1,0:T(8,128)(2,1)S(1)}, bf16[640,128]{1,0:T(8,128)(2,1)S(1)}, u32[]{:S(2)}, u32[]{:S(2)}) %collective-permute-start.16) | collective-permute-done | bytes 163872 | tf_op jit(solution)/shard_map/ppermute | solution.py:404
  92.5 3.8 %collective-permute-done.17.refs_2_ = bf16[640,128]{1,0:T(8,128)(2,1)S(1)} collective-permute-done((bf16[640,128]{1,0:T(8,128)(2,1)S(1)}, bf16[640,128]{1,0:T(8,128)(2,1)S(1)}, u32[]{:S(2)}, u32[]{:S(2)}) %collective-permute-start.17) | collective-permute-done | bytes 163872 | tf_op jit(solution)/shard_map/ppermute | solution.py:404
  96.3 1.0 collective-permute-done.18.refs_3_
  97.3 1.9 %collective-permute-start.19 = (bf16[2560,128]{1,0:T(8,128)(2,1)S(1)}, bf16[2560,128]{1,0:T(8,128)(2,1)S(1)}, u32[]{:S(2)}, u32[]{:S(2)}) collective-permute-start(bf16[2560,128]{1,0:T(8,128)(2,1)S(1)} %place_x.1.mine_ref), channel_id=1, source_target_pairs={{0,1},{1,0},{2,3},{3,2},{4,5},{5,4},{6,7},{7,6},{8,9},{9,8},{10,11... | collective-permute-start | bytes 1966088 | tf_op jit(solution)/shard_map/ppermute | solution.py:408
  99.3 1.7 %collective-permute-done.19.other_ref = bf16[2560,128]{1,0:T(8,128)(2,1)S(1)} collective-permute-done((bf16[2560,128]{1,0:T(8,128)(2,1)S(1)}, bf16[2560,128]{1,0:T(8,128)(2,1)S(1)}, u32[]{:S(2)}, u32[]{:S(2)}) %collective-permute-start.19) | collective-permute-done | bytes 655392 | tf_op jit(solution)/shard_map/ppermute | solution.py:408
  101.0 1.7 %table.1 = f32[400,1500]{1,0:T(8,128)} custom-call(s32[1]{0:T(128)} %bitcast.core_ref, bf16[2560,128]{1,0:T(8,128)(2,1)S(1)} %place_x.1.mine_ref, bf16[2560,128]{1,0:T(8,128)(2,1)S(1)} %collective-permute-done.19.other_ref), custom_call_target="tpu_custom_call" | custom-call | flops 1000000 | bytes 100000 | tf_op jit(solution)/shard_map/table/pallas_call | solution.py:398
  102.7 1.8 %all-to-all-done.1 = bf16[256,16,128]{2,1,0:T(8,128)(2,1)S(1)} async-done(((bf16[256,16,128]{2,1,0:T(8,128)(2,1)}), bf16[256,16,128]{2,1,0:T(8,128)(2,1)S(1)}, u32[]{:S(2)}, u32[]{:S(2)}) %all-to-all-start.1) | async-done | bytes 1048608 | tf_op jit(solution)/shard_map/all_to_all | solution.py:443
  104.5 2.6 %partition.1 = f32[100,1024]{1,0:T(8,128)} custom-call(bf16[4096,128]{1,0:T(8,128)(2,1)S(1)} %bitcast.14), custom_call_target="tpu_custom_call" | custom-call | flops 1000000 | bytes 100000 | tf_op jit(solution)/shard_map/partition/pallas_call | solution.py:288
  (28 shorter events, 0.2 us)
Async XLA Ops:
  0.6 14.7 %collective-permute-start = (bf16[400,256]{1,0:T(8,128)(2,1)}, bf16[400,256]{1,0:T(8,128)(2,1)S(1)}, u32[]{:S(2)}, u32[]{:S(2)}) collective-permute-start(bf16[400,256]{1,0:T(8,128)(2,1)} %bitcast.20), channel_id=1, source_target_pairs={{0,64},{64,128},{128,192},{192,0},{1,65},{65,129},{129,193},{193,1... | collective-permute-start | bytes 614408 | tf_op jit(solution)/shard_map/ppermute | solution.py:404
  2.7 12.6 %collective-permute-start.1 = (bf16[400,256]{1,0:T(8,128)(2,1)}, bf16[400,256]{1,0:T(8,128)(2,1)S(1)}, u32[]{:S(2)}, u32[]{:S(2)}) collective-permute-start(bf16[400,256]{1,0:T(8,128)(2,1)} %bitcast.21), channel_id=1, source_target_pairs={{0,128},{64,192},{128,0},{192,64},{1,129},{65,193},{129,1},{193,65... | collective-permute-start | bytes 614408 | tf_op jit(solution)/shard_map/ppermute | solution.py:404
  5.2 10.2 %collective-permute-start.2 = (bf16[400,256]{1,0:T(8,128)(2,1)}, bf16[400,256]{1,0:T(8,128)(2,1)S(1)}, u32[]{:S(2)}, u32[]{:S(2)}) collective-permute-start(bf16[400,256]{1,0:T(8,128)(2,1)} %bitcast.22), channel_id=1, source_target_pairs={{0,192},{64,0},{128,64},{192,128},{1,193},{65,1},{129,65},{193,129... | collective-permute-start | bytes 614408 | tf_op jit(solution)/shard_map/ppermute | solution.py:404
  7.2 1.7 %copy-start = (f32[1500,400]{0,1:T(8,128)S(1)}, f32[1500,400]{0,1:T(8,128)}, u32[]{:S(2)}) copy-start(f32[1500,400]{0,1:T(8,128)} %param.14) | copy-start | bytes 7200004
  8.9 1.1 %copy-start.1 = (bf16[768,400]{0,1:T(8,128)(2,1)S(1)}, bf16[768,400]{0,1:T(8,128)(2,1)}, u32[]{:S(2)}) copy-start(bf16[768,400]{0,1:T(8,128)(2,1)} %param.10) | copy-start | bytes 1843204
  10.0 1.1 %copy-start.3 = (bf16[768,400]{0,1:T(8,128)(2,1)S(1)}, bf16[768,400]{0,1:T(8,128)(2,1)}, u32[]{:S(2)}) copy-start(bf16[768,400]{0,1:T(8,128)(2,1)} %param.11) | copy-start | bytes 1843204
  11.0 4.3 %copy-start.2 = (bf16[768,400]{0,1:T(8,128)(2,1)S(1)}, bf16[768,400]{0,1:T(8,128)(2,1)}, u32[]{:S(2)}) copy-start(bf16[768,400]{0,1:T(8,128)(2,1)} %param.10) | copy-start | bytes 1843204
  11.0 4.3 %copy-start.4 = (bf16[768,400]{0,1:T(8,128)(2,1)S(1)}, bf16[768,400]{0,1:T(8,128)(2,1)}, u32[]{:S(2)}) copy-start(bf16[768,400]{0,1:T(8,128)(2,1)} %param.11) | copy-start | bytes 1843204
  11.0 4.3 %copy-start.5 = (bf16[256,400]{0,1:T(8,128)(2,1)S(1)}, bf16[256,400]{0,1:T(8,128)(2,1)}, u32[]{:S(2)}) copy-start(bf16[256,400]{0,1:T(8,128)(2,1)} %param.13) | copy-start | bytes 614404
  25.9 5.5 %copy-start.6 = (bf16[400,3072]{1,0:T(8,128)(2,1)}, bf16[400,3072]{1,0:T(8,128)(2,1)S(1)}, u32[]{:S(2)}) copy-start(bf16[400,3072]{1,0:T(8,128)(2,1)S(1)} %get-tuple-element.38.rows_ref) | copy-start | bytes 7372804
  25.9 4.4 %collective-permute-start.3 = (f32[400,768]{1,0:T(8,128)S(1)}, f32[400,768]{1,0:T(8,128)S(1)}, u32[]{:S(2)}, u32[]{:S(2)}) collective-permute-start(f32[400,768]{1,0:T(8,128)S(1)} %get-tuple-element.30), channel_id=1, source_target_pairs={{0,1},{1,0},{2,3},{3,2},{4,5},{5,4},{6,7},{7,6},{8,9},{9,8},{10,11... | collective-permute-start | bytes 3686408 | tf_op jit(solution)/shard_map/ppermute | solution.py:408
  27.5 15.8 %collective-permute-start.4 = (bf16[400,256]{1,0:T(8,128)(2,1)S(1)}, bf16[400,256]{1,0:T(8,128)(2,1)S(1)}, u32[]{:S(2)}, u32[]{:S(2)}) collective-permute-start(bf16[400,256]{1,0:T(8,128)(2,1)S(1)} %get-tuple-element.33), channel_id=1, source_target_pairs={{0,192},{64,0},{128,64},{192,128},{1,193},{65,1},{129,65},{193,129... | collective-permute-start | bytes 614408 | tf_op jit(solution)/shard_map/ppermute | solution.py:404
  28.4 15.0 %collective-permute-start.5 = (bf16[400,256]{1,0:T(8,128)(2,1)S(1)}, bf16[400,256]{1,0:T(8,128)(2,1)S(1)}, u32[]{:S(2)}, u32[]{:S(2)}) collective-permute-start(bf16[400,256]{1,0:T(8,128)(2,1)S(1)} %get-tuple-element.34), channel_id=1, source_target_pairs={{0,128},{64,192},{128,0},{192,64},{1,129},{65,193},{129,1},{193,65... | collective-permute-start | bytes 614408 | tf_op jit(solution)/shard_map/ppermute | solution.py:404
  29.6 13.7 %collective-permute-start.6 = (bf16[400,256]{1,0:T(8,128)(2,1)S(1)}, bf16[400,256]{1,0:T(8,128)(2,1)S(1)}, u32[]{:S(2)}, u32[]{:S(2)}) collective-permute-start(bf16[400,256]{1,0:T(8,128)(2,1)S(1)} %get-tuple-element.35), channel_id=1, source_target_pairs={{0,64},{64,128},{128,192},{192,0},{1,65},{65,129},{129,193},{193,1... | collective-permute-start | bytes 614408 | tf_op jit(solution)/shard_map/ppermute | solution.py:404
  31.4 17.9 %all-to-all-start = ((bf16[16,160,128]{2,1,0:T(8,128)(2,1)}), bf16[16,160,128]{2,1,0:T(8,128)(2,1)S(1)}, u32[]{:S(2)}, u32[]{:S(2)}) async-start(bf16[16,160,128]{2,1,0:T(8,128)(2,1)} %bitcast.7), calls=%async_computation | async-start | bytes 1310720 | tf_op jit(solution)/shard_map/all_to_all | solution.py:435
  37.7 1.7 %copy-start.7 = (bf16[400,3072]{1,0:T(8,128)(2,1)S(1)}, bf16[400,3072]{1,0:T(8,128)(2,1)}, u32[]{:S(2)}) copy-start(bf16[400,3072]{1,0:T(8,128)(2,1)} %copy-done.6) | copy-start | bytes 7372804
  49.4 3.2 %collective-permute-start.7 = (bf16[160,128]{1,0:T(8,128)(2,1)S(1)}, bf16[160,128]{1,0:T(8,128)(2,1)S(1)}, u32[]{:S(2)}, u32[]{:S(2)}) collective-permute-start(bf16[160,128]{1,0:T(8,128)(2,1)S(1)} %rel_xy.1.mine_ref.own_ref), channel_id=1, source_target_pairs={{0,1},{1,0},{2,3},{3,2},{4,5},{5,4},{6,7},{7,6},{8,9},{9,8},{10,11... | collective-permute-start | bytes 122888 | tf_op jit(solution)/shard_map/ppermute | solution.py:408
  52.6 19.5 %collective-permute-start.10 = (bf16[320,128]{1,0:T(8,128)(2,1)S(1)}, bf16[320,128]{1,0:T(8,128)(2,1)S(1)}, u32[]{:S(2)}, u32[]{:S(2)}) collective-permute-start(bf16[320,128]{1,0:T(8,128)(2,1)S(1)} %chip_pair.1), channel_id=1, source_target_pairs={{0,6},{1,11},{2,8},{3,13},{4,10},{5,15},{6,12},{7,1},{8,14},{9,3},... | collective-permute-start | bytes 245768 | tf_op jit(solution)/shard_map/ppermute | solution.py:413
  59.1 12.9 %collective-permute-start.8 = (bf16[320,128]{1,0:T(8,128)(2,1)S(1)}, bf16[320,128]{1,0:T(8,128)(2,1)S(1)}, u32[]{:S(2)}, u32[]{:S(2)}) collective-permute-start(bf16[320,128]{1,0:T(8,128)(2,1)S(1)} %chip_pair.1), channel_id=1, source_target_pairs={{0,2},{1,15},{2,4},{3,1},{4,6},{5,3},{6,8},{7,5},{8,10},{9,7},{10,... | collective-permute-start | bytes 245768 | tf_op jit(solution)/shard_map/ppermute | solution.py:413
  59.8 12.2 %collective-permute-start.9 = (bf16[320,128]{1,0:T(8,128)(2,1)S(1)}, bf16[320,128]{1,0:T(8,128)(2,1)S(1)}, u32[]{:S(2)}, u32[]{:S(2)}) collective-permute-start(bf16[320,128]{1,0:T(8,128)(2,1)S(1)} %chip_pair.1), channel_id=1, source_target_pairs={{0,4},{1,13},{2,6},{3,15},{4,8},{5,1},{6,10},{7,3},{8,12},{9,5},{1... | collective-permute-start | bytes 245768 | tf_op jit(solution)/shard_map/ppermute | solution.py:413
  59.8 12.2 %collective-permute-start.11 = (bf16[160,128]{1,0:T(8,128)(2,1)S(1)}, bf16[160,128]{1,0:T(8,128)(2,1)S(1)}, u32[]{:S(2)}, u32[]{:S(2)}) collective-permute-start(bf16[160,128]{1,0:T(8,128)(2,1)S(1)} %rel_xy.1.mine_ref.own_ref), channel_id=1, source_target_pairs={{0,8},{2,10},{4,12},{6,14},{8,0},{10,2},{12,4},{14,6},{1,9},{3,11}... | collective-permute-start | bytes 122888 | tf_op jit(solution)/shard_map/ppermute | solution.py:404
  64.3 40.2 %all-to-all-start.1 = ((bf16[256,16,128]{2,1,0:T(8,128)(2,1)}), bf16[256,16,128]{2,1,0:T(8,128)(2,1)S(1)}, u32[]{:S(2)}, u32[]{:S(2)}) async-start(bf16[256,16,128]{2,1,0:T(8,128)(2,1)} %bitcast.8), calls=%async_computation.1 | async-start | bytes 2097152 | tf_op jit(solution)/shard_map/all_to_all | solution.py:443
  72.1 3.2 %collective-permute-start.12 = (bf16[480,128]{1,0:T(8,128)(2,1)S(1)}, bf16[480,128]{1,0:T(8,128)(2,1)S(1)}, u32[]{:S(2)}, u32[]{:S(2)}) collective-permute-start(bf16[480,128]{1,0:T(8,128)(2,1)S(1)} %get-tuple-element.45), channel_id=1, source_target_pairs={{0,1},{1,0},{2,3},{3,2},{4,5},{5,4},{6,7},{7,6},{8,9},{9,8},{10,11... | collective-permute-start | bytes 368648 | tf_op jit(solution)/shard_map/ppermute | solution.py:408
  75.4 6.3 %collective-permute-start.13 = (bf16[160,128]{1,0:T(8,128)(2,1)S(1)}, bf16[160,128]{1,0:T(8,128)(2,1)S(1)}, u32[]{:S(2)}, u32[]{:S(2)}) collective-permute-start(bf16[160,128]{1,0:T(8,128)(2,1)S(1)} %rel_z.1.refs_0_), channel_id=1, source_target_pairs={{0,16},{16,32},{32,48},{48,0},{1,17},{17,33},{33,49},{49,1},{2,18}... | collective-permute-start | bytes 122888 | tf_op jit(solution)/shard_map/ppermute | solution.py:404
  75.5 6.3 %collective-permute-start.14 = (bf16[160,128]{1,0:T(8,128)(2,1)S(1)}, bf16[160,128]{1,0:T(8,128)(2,1)S(1)}, u32[]{:S(2)}, u32[]{:S(2)}) collective-permute-start(bf16[160,128]{1,0:T(8,128)(2,1)S(1)} %rel_z.1.refs_0_), channel_id=1, source_target_pairs={{0,32},{16,48},{32,0},{48,16},{1,33},{17,49},{33,1},{49,17},{2,34}... | collective-permute-start | bytes 122888 | tf_op jit(solution)/shard_map/ppermute | solution.py:404
  77.5 4.9 %collective-permute-start.15 = (bf16[160,128]{1,0:T(8,128)(2,1)S(1)}, bf16[160,128]{1,0:T(8,128)(2,1)S(1)}, u32[]{:S(2)}, u32[]{:S(2)}) collective-permute-start(bf16[160,128]{1,0:T(8,128)(2,1)S(1)} %rel_z.1.refs_0_), channel_id=1, source_target_pairs={{0,48},{16,0},{32,16},{48,32},{1,49},{17,1},{33,17},{49,33},{2,50}... | collective-permute-start | bytes 122888 | tf_op jit(solution)/shard_map/ppermute | solution.py:404
  82.4 10.1 %collective-permute-start.16 = (bf16[640,128]{1,0:T(8,128)(2,1)S(1)}, bf16[640,128]{1,0:T(8,128)(2,1)S(1)}, u32[]{:S(2)}, u32[]{:S(2)}) collective-permute-start(bf16[640,128]{1,0:T(8,128)(2,1)S(1)} %place_y.1.refs_0_), channel_id=1, source_target_pairs={{0,64},{64,128},{128,192},{192,0},{1,65},{65,129},{129,193},{193,1... | collective-permute-start | bytes 491528 | tf_op jit(solution)/shard_map/ppermute | solution.py:404
  82.5 13.7 %collective-permute-start.17 = (bf16[640,128]{1,0:T(8,128)(2,1)S(1)}, bf16[640,128]{1,0:T(8,128)(2,1)S(1)}, u32[]{:S(2)}, u32[]{:S(2)}) collective-permute-start(bf16[640,128]{1,0:T(8,128)(2,1)S(1)} %place_y.1.refs_0_), channel_id=1, source_target_pairs={{0,128},{64,192},{128,0},{192,64},{1,129},{65,193},{129,1},{193,65... | collective-permute-start | bytes 491528 | tf_op jit(solution)/shard_map/ppermute | solution.py:404
  84.9 12.4 %collective-permute-start.18 = (bf16[640,128]{1,0:T(8,128)(2,1)S(1)}, bf16[640,128]{1,0:T(8,128)(2,1)S(1)}, u32[]{:S(2)}, u32[]{:S(2)}) collective-permute-start(bf16[640,128]{1,0:T(8,128)(2,1)S(1)} %place_y.1.refs_0_), channel_id=1, source_target_pairs={{0,192},{64,0},{128,64},{192,128},{1,193},{65,1},{129,65},{193,129... | collective-permute-start | bytes 491528 | tf_op jit(solution)/shard_map/ppermute | solution.py:404
  97.3 3.6 %collective-permute-start.19 = (bf16[2560,128]{1,0:T(8,128)(2,1)S(1)}, bf16[2560,128]{1,0:T(8,128)(2,1)S(1)}, u32[]{:S(2)}, u32[]{:S(2)}) collective-permute-start(bf16[2560,128]{1,0:T(8,128)(2,1)S(1)} %place_x.1.mine_ref), channel_id=1, source_target_pairs={{0,1},{1,0},{2,3},{3,2},{4,5},{5,4},{6,7},{7,6},{8,9},{9,8},{10,11... | collective-permute-start | bytes 1966088 | tf_op jit(solution)/shard_map/ppermute | solution.py:408

commit v7 on v6

--- a/solution.py
+++ b/solution.py
@@ -165,7 +165,7 @@
     tail = tail_ref[...].astype(F32)
     firsts = []
     grads = []
-    term = jnp.zeros((D, NEG), F32)
+    terms = []
     for side, (query_ref, positives) in enumerate(((q_ref, tail), (m_ref, head))):
         positive = pos_ref[pl.ds(side, 1), :]
         scores = dot(turned_ref[...], query_ref[...])
@@ -175,9 +175,10 @@
         total = pos_weight + jnp.sum(weight, 0, keepdims=True)
         first = pos_weight / total - 1.0
         probs = (weight * (1.0 / total)).astype(BF16)
-        term = term + dot_nt(query_ref[...], probs)
+        terms.append(dot_nt(query_ref[...], probs))
         grads.append(first * positives + dot(neg_ref[...], probs))
         firsts.append(first)
+    term = terms[0] + terms[1]
     own_ref[...] = term[:, :NEG_DEV]
     for k, ref in enumerate((g1_ref, g2_ref, g3_ref)):
         ref[...] = term[:, (k + 1) * NEG_DEV:(k + 2) * NEG_DEV].astype(BF16)

time: 108 us -> 108 us (level)
  no operation moved by 1% of the time
where the time goes in v7:
time: 108 us; the launch traced here: 107 us
  starting transfers between devices  49.4 us (46%)
  Pallas kernels  26.8 us (25%)
  waiting for transfers between devices  23.8 us (22%)
  local copies, waits for them, and re-layouts  6.38 us (6%)
    ppermute x13, starting transfers between devices, shift(): return lax.ppermute(value, axis, [(i, (i + k) % size) for i in range(size)])  20.1 us
    ppermute x13, waiting for transfers between devices, shift(): return lax.ppermute(value, axis, [(i, (i + k) % size) for i in range(size)])  14.8 us
    pallas_call x1, Pallas kernels, edge(): call(edge_kernel, 'edge', 1, [SMEM] + [full(part)] * 4 + [full(cols)] * 5...  10.6 us
    ppermute x4, starting transfers between devices, pair(): return lax.ppermute(value, 'c', [(0, 1), (1, 0)])  8.07 us
    all_to_all x1, starting transfers between devices, shards(): lax.all_to_all(packed.reshape(N_GRP * N_OWN, CAP, LANES), ALL, 0, 0, tile...  7.69 us
    ppermute x3, starting transfers between devices, shift_zc(): return lax.ppermute(value, ('z', 'c'), pairs)  7.27 us
    all_to_all x1, starting transfers between devices, shards(): chip = lax.all_to_all(chip, ('x', 'y'), 0, 0, tiled=True)  6.23 us
    unnamed x16, local copies, waits for them, and re-layouts  5.54 us
  transfers between devices with their start and end apart: 22, of which 10 were waited for; matrix products, arithmetic and copies ran while one was open for 1% of the time, Pallas kernels for 13%

profile of v7, /device:TPU:1, one launch (start us, length us, event | category | flops | bytes accessed | tf_op | source)
XLA Modules:
  0.0 107.2 jit_solution(4088875670977559448)
XLA Ops:
  0.6 2.1 %collective-permute-start = (bf16[400,256]{1,0:T(8,128)(2,1)}, bf16[400,256]{1,0:T(8,128)(2,1)S(1)}, u32[]{:S(2)}, u32[]{:S(2)}) collective-permute-start(bf16[400,256]{1,0:T(8,128)(2,1)} %bitcast.20), channel_id=1, source_target_pairs={{0,64},{64,128},{128,192},{192,0},{1,65},{65,129},{129,193},{193,1... | collective-permute-start | bytes 614408 | tf_op jit(solution)/shard_map/ppermute | solution.py:405
  2.7 2.5 %collective-permute-start.1 = (bf16[400,256]{1,0:T(8,128)(2,1)}, bf16[400,256]{1,0:T(8,128)(2,1)S(1)}, u32[]{:S(2)}, u32[]{:S(2)}) collective-permute-start(bf16[400,256]{1,0:T(8,128)(2,1)} %bitcast.21), channel_id=1, source_target_pairs={{0,128},{64,192},{128,0},{192,64},{1,129},{65,193},{129,1},{193,65... | collective-permute-start | bytes 614408 | tf_op jit(solution)/shard_map/ppermute | solution.py:405
  5.2 1.2 %collective-permute-start.2 = (bf16[400,256]{1,0:T(8,128)(2,1)}, bf16[400,256]{1,0:T(8,128)(2,1)S(1)}, u32[]{:S(2)}, u32[]{:S(2)}) collective-permute-start(bf16[400,256]{1,0:T(8,128)(2,1)} %bitcast.22), channel_id=1, source_target_pairs={{0,192},{64,0},{128,64},{192,128},{1,193},{65,1},{129,65},{193,129... | collective-permute-start | bytes 614408 | tf_op jit(solution)/shard_map/ppermute | solution.py:405
  6.4 0.8 concatenate.3
  7.2 0.0 copy-start
  7.2 1.7 %copy-done = f32[1500,400]{0,1:T(8,128)S(1)} copy-done((f32[1500,400]{0,1:T(8,128)S(1)}, f32[1500,400]{0,1:T(8,128)}, u32[]{:S(2)}) %copy-start) | copy-done | bytes 2400024
  8.9 1.1 copy-done.1
  10.0 1.1 copy-done.3
  11.0 4.3 %prep.1 = (f32[400,768]{1,0:T(8,128)S(1)}, bf16[400,768]{1,0:T(8,128)(2,1)S(1)}, bf16[400,768]{1,0:T(8,128)(2,1)S(1)}, f32[8,768]{1,0:T(8,128)S(1)}, s32[1,768]{...) custom-call(bf16[400,768]{1,0:T(8,128)(2,1)S(1)} %bitcast.16, ...), custom_call_target="tpu_custom_call" | custom-call | flops 1000000 | bytes 100000 | tf_op jit(solution)/shard_map/prep/pallas_call | solution.py:145
  15.4 10.6 %edge.1 = (f32[400,256]{1,0:T(8,128)S(1)}, bf16[400,256]{1,0:T(8,128)(2,1)S(1)}, bf16[400,256]{1,0:T(8,128)(2,1)S(1)}, bf16[400,256]{1,0:T(8,128)(2,1)S(1)}, bf1...) custom-call(s32[1]{0:T(128)} %bitcast.core_ref, bf16[400,256]{1,0:T(8,128)(2,1)S(1)} %bitcast.23, ...), custom_call_target="tpu_custom_call" | custom-call | flops 10000000000 | bytes 100000 | tf_op jit(solution)/shard_map/edge/pallas_call | solution.py:212
  25.9 0.0 copy-start.6
  26.0 1.6 %collective-permute-start.3 = (f32[400,768]{1,0:T(8,128)S(1)}, f32[400,768]{1,0:T(8,128)S(1)}, u32[]{:S(2)}, u32[]{:S(2)}) collective-permute-start(f32[400,768]{1,0:T(8,128)S(1)} %get-tuple-element.30), channel_id=1, source_target_pairs={{0,1},{1,0},{2,3},{3,2},{4,5},{5,4},{6,7},{7,6},{8,9},{9,8},{10,11... | collective-permute-start | bytes 3686408 | tf_op jit(solution)/shard_map/ppermute | solution.py:409
  27.6 0.8 collective-permute-start.4
  28.4 1.3 %collective-permute-start.5 = (bf16[400,256]{1,0:T(8,128)(2,1)S(1)}, bf16[400,256]{1,0:T(8,128)(2,1)S(1)}, u32[]{:S(2)}, u32[]{:S(2)}) collective-permute-start(bf16[400,256]{1,0:T(8,128)(2,1)S(1)} %get-tuple-element.34), channel_id=1, source_target_pairs={{0,128},{64,192},{128,0},{192,64},{1,129},{65,193},{129,1},{193,65... | collective-permute-start | bytes 614408 | tf_op jit(solution)/shard_map/ppermute | solution.py:405
  29.7 0.7 collective-permute-start.6
  30.4 1.0 rel_chip.1
  31.4 6.2 %all-to-all-start = ((bf16[16,160,128]{2,1,0:T(8,128)(2,1)}), bf16[16,160,128]{2,1,0:T(8,128)(2,1)S(1)}, u32[]{:S(2)}, u32[]{:S(2)}) async-start(bf16[16,160,128]{2,1,0:T(8,128)(2,1)} %bitcast.7), calls=%async_computation | async-start | bytes 1310720 | tf_op jit(solution)/shard_map/all_to_all | solution.py:436
  37.7 0.0 copy-start.7
  37.7 1.7 %copy-done.7 = bf16[400,3072]{1,0:T(8,128)(2,1)S(1)} copy-done((bf16[400,3072]{1,0:T(8,128)(2,1)S(1)}, bf16[400,3072]{1,0:T(8,128)(2,1)}, u32[]{:S(2)}) %copy-start.7) | copy-done | bytes 2457624
  39.4 4.0 %slot.1.part_ref = f32[4,1024,128]{2,1,0:T(8,128)S(1)} custom-call(s32[1,768]{1,0:T(1,128)S(1)} %get-tuple-element.36.target_h_ref, s32[1,768]{1,0:T(1,128)S(1)} %get-tuple-element.37.target_t_ref, bf16[400,3072]{1,0:T(8,128)(2,1)S(1)} %copy-done.7, f32[1024,128]{1,0:T(8,128)S(1)} %get-tuple-element.39.code_ref), custom_call_target="tpu_custom_call" | custom-call | flops 8000000000 | bytes 100000 | tf_op jit(solution)/shard_map/slot/pallas_call | solution.py:234
  43.4 2.3 %pack.1 = bf16[4,1024,128]{2,1,0:T(8,128)(2,1)} custom-call(s32[1,256]{1,0:T(1,128)S(1)} %get-tuple-element.31.target_ref, f32[400,256]{1,0:T(8,128)S(1)} %get-tuple-element.32.own_ref, bf16[400,256]{1,0:T(8,128)(2,1)S(1)} %collective-permute-done.4.g1_ref, bf16[400,256]{1,0:T(8,128)(2,1)S(1)} %collective-permute-done.5.g2_ref, ...), custom_call_target="tpu_custom_call" | custom-call | flops 3000000000 | bytes 100000 | tf_op jit(solution)/shard_map/pack/pallas_call | solution.py:253
  45.7 3.6 %all-to-all-done.in_ref = bf16[16,160,128]{2,1,0:T(8,128)(2,1)S(1)} async-done(((bf16[16,160,128]{2,1,0:T(8,128)(2,1)}), bf16[16,160,128]{2,1,0:T(8,128)(2,1)S(1)}, u32[]{:S(2)}, u32[]{:S(2)}) %all-to-all-start) | async-done | bytes 655392 | tf_op jit(solution)/shard_map/all_to_all | solution.py:436
  49.3 0.1 rel_xy.1.mine_ref.own_ref
  49.4 2.3 %collective-permute-start.7 = (bf16[160,128]{1,0:T(8,128)(2,1)S(1)}, bf16[160,128]{1,0:T(8,128)(2,1)S(1)}, u32[]{:S(2)}, u32[]{:S(2)}) collective-permute-start(bf16[160,128]{1,0:T(8,128)(2,1)S(1)} %rel_xy.1.mine_ref.own_ref), channel_id=1, source_target_pairs={{0,1},{1,0},{2,3},{3,2},{4,5},{5,4},{6,7},{7,6},{8,9},{9,8},{10,11... | collective-permute-start | bytes 122888 | tf_op jit(solution)/shard_map/ppermute | solution.py:409
  51.7 0.9 collective-permute-done.7.other_ref
  52.6 6.5 %collective-permute-start.10 = (bf16[320,128]{1,0:T(8,128)(2,1)S(1)}, bf16[320,128]{1,0:T(8,128)(2,1)S(1)}, u32[]{:S(2)}, u32[]{:S(2)}) collective-permute-start(bf16[320,128]{1,0:T(8,128)(2,1)S(1)} %chip_pair.1), channel_id=1, source_target_pairs={{0,6},{1,11},{2,8},{3,13},{4,10},{5,15},{6,12},{7,1},{8,14},{9,3},... | collective-permute-start | bytes 245768 | tf_op jit(solution)/shard_map/ppermute | solution.py:414
  59.1 0.7 collective-permute-start.8
  59.9 4.5 %collective-permute-start.11 = (bf16[160,128]{1,0:T(8,128)(2,1)S(1)}, bf16[160,128]{1,0:T(8,128)(2,1)S(1)}, u32[]{:S(2)}, u32[]{:S(2)}) collective-permute-start(bf16[160,128]{1,0:T(8,128)(2,1)S(1)} %rel_xy.1.mine_ref.own_ref), channel_id=1, source_target_pairs={{0,8},{2,10},{4,12},{6,14},{8,0},{10,2},{12,4},{14,6},{1,9},{3,11}... | collective-permute-start | bytes 122888 | tf_op jit(solution)/shard_map/ppermute | solution.py:405
  64.4 7.7 %all-to-all-start.1 = ((bf16[256,16,128]{2,1,0:T(8,128)(2,1)}), bf16[256,16,128]{2,1,0:T(8,128)(2,1)S(1)}, u32[]{:S(2)}, u32[]{:S(2)}) async-start(bf16[256,16,128]{2,1,0:T(8,128)(2,1)} %bitcast.8), calls=%async_computation.1 | async-start | bytes 2097152 | tf_op jit(solution)/shard_map/all_to_all | solution.py:444
  72.1 2.2 %collective-permute-start.12 = (bf16[480,128]{1,0:T(8,128)(2,1)S(1)}, bf16[480,128]{1,0:T(8,128)(2,1)S(1)}, u32[]{:S(2)}, u32[]{:S(2)}) collective-permute-start(bf16[480,128]{1,0:T(8,128)(2,1)S(1)} %get-tuple-element.45), channel_id=1, source_target_pairs={{0,1},{1,0},{2,3},{3,2},{4,5},{5,4},{6,7},{7,6},{8,9},{9,8},{10,11... | collective-permute-start | bytes 368648 | tf_op jit(solution)/shard_map/ppermute | solution.py:409
  74.4 1.0 collective-permute-done.12.other_ref
  75.3 0.1 rel_z.1.refs_0_
  75.4 0.1 collective-permute-start.13
  75.5 2.0 %collective-permute-start.14 = (bf16[160,128]{1,0:T(8,128)(2,1)S(1)}, bf16[160,128]{1,0:T(8,128)(2,1)S(1)}, u32[]{:S(2)}, u32[]{:S(2)}) collective-permute-start(bf16[160,128]{1,0:T(8,128)(2,1)S(1)} %rel_z.1.refs_0_), channel_id=1, source_target_pairs={{0,32},{16,48},{32,0},{48,16},{1,33},{17,49},{33,1},{49,17},{2,34}... | collective-permute-start | bytes 122888 | tf_op jit(solution)/shard_map/ppermute | solution.py:405
  77.5 1.1 %collective-permute-start.15 = (bf16[160,128]{1,0:T(8,128)(2,1)S(1)}, bf16[160,128]{1,0:T(8,128)(2,1)S(1)}, u32[]{:S(2)}, u32[]{:S(2)}) collective-permute-start(bf16[160,128]{1,0:T(8,128)(2,1)S(1)} %rel_z.1.refs_0_), channel_id=1, source_target_pairs={{0,48},{16,0},{32,16},{48,32},{1,49},{17,1},{33,17},{49,33},{2,50}... | collective-permute-start | bytes 122888 | tf_op jit(solution)/shard_map/ppermute | solution.py:405
  78.7 3.1 %collective-permute-done.13.refs_1_ = bf16[160,128]{1,0:T(8,128)(2,1)S(1)} collective-permute-done((bf16[160,128]{1,0:T(8,128)(2,1)S(1)}, bf16[160,128]{1,0:T(8,128)(2,1)S(1)}, u32[]{:S(2)}, u32[]{:S(2)}) %collective-permute-start.13) | collective-permute-done | bytes 40992 | tf_op jit(solution)/shard_map/ppermute | solution.py:405
  81.8 0.7 collective-permute-done.15.refs_3_
  82.5 0.1 collective-permute-start.16
  82.5 2.3 %collective-permute-start.17 = (bf16[640,128]{1,0:T(8,128)(2,1)S(1)}, bf16[640,128]{1,0:T(8,128)(2,1)S(1)}, u32[]{:S(2)}, u32[]{:S(2)}) collective-permute-start(bf16[640,128]{1,0:T(8,128)(2,1)S(1)} %place_y.1.refs_0_), channel_id=1, source_target_pairs={{0,128},{64,192},{128,0},{192,64},{1,129},{65,193},{129,1},{193,65... | collective-permute-start | bytes 491528 | tf_op jit(solution)/shard_map/ppermute | solution.py:405
  84.9 1.4 %collective-permute-start.18 = (bf16[640,128]{1,0:T(8,128)(2,1)S(1)}, bf16[640,128]{1,0:T(8,128)(2,1)S(1)}, u32[]{:S(2)}, u32[]{:S(2)}) collective-permute-start(bf16[640,128]{1,0:T(8,128)(2,1)S(1)} %place_y.1.refs_0_), channel_id=1, source_target_pairs={{0,192},{64,0},{128,64},{192,128},{1,193},{65,1},{129,65},{193,129... | collective-permute-start | bytes 491528 | tf_op jit(solution)/shard_map/ppermute | solution.py:405
  86.3 6.2 %collective-permute-done.16.refs_1_ = bf16[640,128]{1,0:T(8,128)(2,1)S(1)} collective-permute-done((bf16[640,128]{1,0:T(8,128)(2,1)S(1)}, bf16[640,128]{1,0:T(8,128)(2,1)S(1)}, u32[]{:S(2)}, u32[]{:S(2)}) %collective-permute-start.16) | collective-permute-done | bytes 163872 | tf_op jit(solution)/shard_map/ppermute | solution.py:405
  92.5 3.8 %collective-permute-done.17.refs_2_ = bf16[640,128]{1,0:T(8,128)(2,1)S(1)} collective-permute-done((bf16[640,128]{1,0:T(8,128)(2,1)S(1)}, bf16[640,128]{1,0:T(8,128)(2,1)S(1)}, u32[]{:S(2)}, u32[]{:S(2)}) %collective-permute-start.17) | collective-permute-done | bytes 163872 | tf_op jit(solution)/shard_map/ppermute | solution.py:405
  96.3 1.0 collective-permute-done.18.refs_3_
  97.4 1.9 %collective-permute-start.19 = (bf16[2560,128]{1,0:T(8,128)(2,1)S(1)}, bf16[2560,128]{1,0:T(8,128)(2,1)S(1)}, u32[]{:S(2)}, u32[]{:S(2)}) collective-permute-start(bf16[2560,128]{1,0:T(8,128)(2,1)S(1)} %place_x.1.mine_ref), channel_id=1, source_target_pairs={{0,1},{1,0},{2,3},{3,2},{4,5},{5,4},{6,7},{7,6},{8,9},{9,8},{10,11... | collective-permute-start | bytes 1966088 | tf_op jit(solution)/shard_map/ppermute | solution.py:409
  99.3 1.7 %collective-permute-done.19.other_ref = bf16[2560,128]{1,0:T(8,128)(2,1)S(1)} collective-permute-done((bf16[2560,128]{1,0:T(8,128)(2,1)S(1)}, bf16[2560,128]{1,0:T(8,128)(2,1)S(1)}, u32[]{:S(2)}, u32[]{:S(2)}) %collective-permute-start.19) | collective-permute-done | bytes 655392 | tf_op jit(solution)/shard_map/ppermute | solution.py:409
  101.0 1.7 %table.1 = f32[400,1500]{1,0:T(8,128)} custom-call(s32[1]{0:T(128)} %bitcast.core_ref, bf16[2560,128]{1,0:T(8,128)(2,1)S(1)} %place_x.1.mine_ref, bf16[2560,128]{1,0:T(8,128)(2,1)S(1)} %collective-permute-done.19.other_ref), custom_call_target="tpu_custom_call" | custom-call | flops 1000000 | bytes 100000 | tf_op jit(solution)/shard_map/table/pallas_call | solution.py:399
  102.8 1.8 %all-to-all-done.1 = bf16[256,16,128]{2,1,0:T(8,128)(2,1)S(1)} async-done(((bf16[256,16,128]{2,1,0:T(8,128)(2,1)}), bf16[256,16,128]{2,1,0:T(8,128)(2,1)S(1)}, u32[]{:S(2)}, u32[]{:S(2)}) %all-to-all-start.1) | async-done | bytes 1048608 | tf_op jit(solution)/shard_map/all_to_all | solution.py:444
  104.6 2.6 %partition.1 = f32[100,1024]{1,0:T(8,128)} custom-call(bf16[4096,128]{1,0:T(8,128)(2,1)S(1)} %bitcast.14), custom_call_target="tpu_custom_call" | custom-call | flops 1000000 | bytes 100000 | tf_op jit(solution)/shard_map/partition/pallas_call | solution.py:289
  (28 shorter events, 0.2 us)
Async XLA Ops:
  0.6 14.7 %collective-permute-start = (bf16[400,256]{1,0:T(8,128)(2,1)}, bf16[400,256]{1,0:T(8,128)(2,1)S(1)}, u32[]{:S(2)}, u32[]{:S(2)}) collective-permute-start(bf16[400,256]{1,0:T(8,128)(2,1)} %bitcast.20), channel_id=1, source_target_pairs={{0,64},{64,128},{128,192},{192,0},{1,65},{65,129},{129,193},{193,1... | collective-permute-start | bytes 614408 | tf_op jit(solution)/shard_map/ppermute | solution.py:405
  2.7 12.6 %collective-permute-start.1 = (bf16[400,256]{1,0:T(8,128)(2,1)}, bf16[400,256]{1,0:T(8,128)(2,1)S(1)}, u32[]{:S(2)}, u32[]{:S(2)}) collective-permute-start(bf16[400,256]{1,0:T(8,128)(2,1)} %bitcast.21), channel_id=1, source_target_pairs={{0,128},{64,192},{128,0},{192,64},{1,129},{65,193},{129,1},{193,65... | collective-permute-start | bytes 614408 | tf_op jit(solution)/shard_map/ppermute | solution.py:405
  5.2 10.2 %collective-permute-start.2 = (bf16[400,256]{1,0:T(8,128)(2,1)}, bf16[400,256]{1,0:T(8,128)(2,1)S(1)}, u32[]{:S(2)}, u32[]{:S(2)}) collective-permute-start(bf16[400,256]{1,0:T(8,128)(2,1)} %bitcast.22), channel_id=1, source_target_pairs={{0,192},{64,0},{128,64},{192,128},{1,193},{65,1},{129,65},{193,129... | collective-permute-start | bytes 614408 | tf_op jit(solution)/shard_map/ppermute | solution.py:405
  7.2 1.7 %copy-start = (f32[1500,400]{0,1:T(8,128)S(1)}, f32[1500,400]{0,1:T(8,128)}, u32[]{:S(2)}) copy-start(f32[1500,400]{0,1:T(8,128)} %param.14) | copy-start | bytes 7200004
  8.9 1.1 %copy-start.1 = (bf16[768,400]{0,1:T(8,128)(2,1)S(1)}, bf16[768,400]{0,1:T(8,128)(2,1)}, u32[]{:S(2)}) copy-start(bf16[768,400]{0,1:T(8,128)(2,1)} %param.10) | copy-start | bytes 1843204
  10.0 1.1 %copy-start.3 = (bf16[768,400]{0,1:T(8,128)(2,1)S(1)}, bf16[768,400]{0,1:T(8,128)(2,1)}, u32[]{:S(2)}) copy-start(bf16[768,400]{0,1:T(8,128)(2,1)} %param.11) | copy-start | bytes 1843204
  11.0 4.3 %copy-start.2 = (bf16[768,400]{0,1:T(8,128)(2,1)S(1)}, bf16[768,400]{0,1:T(8,128)(2,1)}, u32[]{:S(2)}) copy-start(bf16[768,400]{0,1:T(8,128)(2,1)} %param.10) | copy-start | bytes 1843204
  11.0 4.3 %copy-start.4 = (bf16[768,400]{0,1:T(8,128)(2,1)S(1)}, bf16[768,400]{0,1:T(8,128)(2,1)}, u32[]{:S(2)}) copy-start(bf16[768,400]{0,1:T(8,128)(2,1)} %param.11) | copy-start | bytes 1843204
  11.0 4.3 %copy-start.5 = (bf16[256,400]{0,1:T(8,128)(2,1)S(1)}, bf16[256,400]{0,1:T(8,128)(2,1)}, u32[]{:S(2)}) copy-start(bf16[256,400]{0,1:T(8,128)(2,1)} %param.13) | copy-start | bytes 614404
  25.9 5.5 %copy-start.6 = (bf16[400,3072]{1,0:T(8,128)(2,1)}, bf16[400,3072]{1,0:T(8,128)(2,1)S(1)}, u32[]{:S(2)}) copy-start(bf16[400,3072]{1,0:T(8,128)(2,1)S(1)} %get-tuple-element.38.rows_ref) | copy-start | bytes 7372804
  26.0 4.4 %collective-permute-start.3 = (f32[400,768]{1,0:T(8,128)S(1)}, f32[400,768]{1,0:T(8,128)S(1)}, u32[]{:S(2)}, u32[]{:S(2)}) collective-permute-start(f32[400,768]{1,0:T(8,128)S(1)} %get-tuple-element.30), channel_id=1, source_target_pairs={{0,1},{1,0},{2,3},{3,2},{4,5},{5,4},{6,7},{7,6},{8,9},{9,8},{10,11... | collective-permute-start | bytes 3686408 | tf_op jit(solution)/shard_map/ppermute | solution.py:409
  27.6 15.8 %collective-permute-start.4 = (bf16[400,256]{1,0:T(8,128)(2,1)S(1)}, bf16[400,256]{1,0:T(8,128)(2,1)S(1)}, u32[]{:S(2)}, u32[]{:S(2)}) collective-permute-start(bf16[400,256]{1,0:T(8,128)(2,1)S(1)} %get-tuple-element.33), channel_id=1, source_target_pairs={{0,192},{64,0},{128,64},{192,128},{1,193},{65,1},{129,65},{193,129... | collective-permute-start | bytes 614408 | tf_op jit(solution)/shard_map/ppermute | solution.py:405
  28.4 15.0 %collective-permute-start.5 = (bf16[400,256]{1,0:T(8,128)(2,1)S(1)}, bf16[400,256]{1,0:T(8,128)(2,1)S(1)}, u32[]{:S(2)}, u32[]{:S(2)}) collective-permute-start(bf16[400,256]{1,0:T(8,128)(2,1)S(1)} %get-tuple-element.34), channel_id=1, source_target_pairs={{0,128},{64,192},{128,0},{192,64},{1,129},{65,193},{129,1},{193,65... | collective-permute-start | bytes 614408 | tf_op jit(solution)/shard_map/ppermute | solution.py:405
  29.7 13.7 %collective-permute-start.6 = (bf16[400,256]{1,0:T(8,128)(2,1)S(1)}, bf16[400,256]{1,0:T(8,128)(2,1)S(1)}, u32[]{:S(2)}, u32[]{:S(2)}) collective-permute-start(bf16[400,256]{1,0:T(8,128)(2,1)S(1)} %get-tuple-element.35), channel_id=1, source_target_pairs={{0,64},{64,128},{128,192},{192,0},{1,65},{65,129},{129,193},{193,1... | collective-permute-start | bytes 614408 | tf_op jit(solution)/shard_map/ppermute | solution.py:405
  31.4 17.9 %all-to-all-start = ((bf16[16,160,128]{2,1,0:T(8,128)(2,1)}), bf16[16,160,128]{2,1,0:T(8,128)(2,1)S(1)}, u32[]{:S(2)}, u32[]{:S(2)}) async-start(bf16[16,160,128]{2,1,0:T(8,128)(2,1)} %bitcast.7), calls=%async_computation | async-start | bytes 1310720 | tf_op jit(solution)/shard_map/all_to_all | solution.py:436
  37.7 1.7 %copy-start.7 = (bf16[400,3072]{1,0:T(8,128)(2,1)S(1)}, bf16[400,3072]{1,0:T(8,128)(2,1)}, u32[]{:S(2)}) copy-start(bf16[400,3072]{1,0:T(8,128)(2,1)} %copy-done.6) | copy-start | bytes 7372804
  49.4 3.2 %collective-permute-start.7 = (bf16[160,128]{1,0:T(8,128)(2,1)S(1)}, bf16[160,128]{1,0:T(8,128)(2,1)S(1)}, u32[]{:S(2)}, u32[]{:S(2)}) collective-permute-start(bf16[160,128]{1,0:T(8,128)(2,1)S(1)} %rel_xy.1.mine_ref.own_ref), channel_id=1, source_target_pairs={{0,1},{1,0},{2,3},{3,2},{4,5},{5,4},{6,7},{7,6},{8,9},{9,8},{10,11... | collective-permute-start | bytes 122888 | tf_op jit(solution)/shard_map/ppermute | solution.py:409
  52.6 19.5 %collective-permute-start.10 = (bf16[320,128]{1,0:T(8,128)(2,1)S(1)}, bf16[320,128]{1,0:T(8,128)(2,1)S(1)}, u32[]{:S(2)}, u32[]{:S(2)}) collective-permute-start(bf16[320,128]{1,0:T(8,128)(2,1)S(1)} %chip_pair.1), channel_id=1, source_target_pairs={{0,6},{1,11},{2,8},{3,13},{4,10},{5,15},{6,12},{7,1},{8,14},{9,3},... | collective-permute-start | bytes 245768 | tf_op jit(solution)/shard_map/ppermute | solution.py:414
  59.1 12.9 %collective-permute-start.8 = (bf16[320,128]{1,0:T(8,128)(2,1)S(1)}, bf16[320,128]{1,0:T(8,128)(2,1)S(1)}, u32[]{:S(2)}, u32[]{:S(2)}) collective-permute-start(bf16[320,128]{1,0:T(8,128)(2,1)S(1)} %chip_pair.1), channel_id=1, source_target_pairs={{0,2},{1,15},{2,4},{3,1},{4,6},{5,3},{6,8},{7,5},{8,10},{9,7},{10,... | collective-permute-start | bytes 245768 | tf_op jit(solution)/shard_map/ppermute | solution.py:414
  59.9 12.2 %collective-permute-start.9 = (bf16[320,128]{1,0:T(8,128)(2,1)S(1)}, bf16[320,128]{1,0:T(8,128)(2,1)S(1)}, u32[]{:S(2)}, u32[]{:S(2)}) collective-permute-start(bf16[320,128]{1,0:T(8,128)(2,1)S(1)} %chip_pair.1), channel_id=1, source_target_pairs={{0,4},{1,13},{2,6},{3,15},{4,8},{5,1},{6,10},{7,3},{8,12},{9,5},{1... | collective-permute-start | bytes 245768 | tf_op jit(solution)/shard_map/ppermute | solution.py:414
  59.9 12.2 %collective-permute-start.11 = (bf16[160,128]{1,0:T(8,128)(2,1)S(1)}, bf16[160,128]{1,0:T(8,128)(2,1)S(1)}, u32[]{:S(2)}, u32[]{:S(2)}) collective-permute-start(bf16[160,128]{1,0:T(8,128)(2,1)S(1)} %rel_xy.1.mine_ref.own_ref), channel_id=1, source_target_pairs={{0,8},{2,10},{4,12},{6,14},{8,0},{10,2},{12,4},{14,6},{1,9},{3,11}... | collective-permute-start | bytes 122888 | tf_op jit(solution)/shard_map/ppermute | solution.py:405
  64.4 40.2 %all-to-all-start.1 = ((bf16[256,16,128]{2,1,0:T(8,128)(2,1)}), bf16[256,16,128]{2,1,0:T(8,128)(2,1)S(1)}, u32[]{:S(2)}, u32[]{:S(2)}) async-start(bf16[256,16,128]{2,1,0:T(8,128)(2,1)} %bitcast.8), calls=%async_computation.1 | async-start | bytes 2097152 | tf_op jit(solution)/shard_map/all_to_all | solution.py:444
  72.1 3.2 %collective-permute-start.12 = (bf16[480,128]{1,0:T(8,128)(2,1)S(1)}, bf16[480,128]{1,0:T(8,128)(2,1)S(1)}, u32[]{:S(2)}, u32[]{:S(2)}) collective-permute-start(bf16[480,128]{1,0:T(8,128)(2,1)S(1)} %get-tuple-element.45), channel_id=1, source_target_pairs={{0,1},{1,0},{2,3},{3,2},{4,5},{5,4},{6,7},{7,6},{8,9},{9,8},{10,11... | collective-permute-start | bytes 368648 | tf_op jit(solution)/shard_map/ppermute | solution.py:409
  75.4 6.3 %collective-permute-start.13 = (bf16[160,128]{1,0:T(8,128)(2,1)S(1)}, bf16[160,128]{1,0:T(8,128)(2,1)S(1)}, u32[]{:S(2)}, u32[]{:S(2)}) collective-permute-start(bf16[160,128]{1,0:T(8,128)(2,1)S(1)} %rel_z.1.refs_0_), channel_id=1, source_target_pairs={{0,16},{16,32},{32,48},{48,0},{1,17},{17,33},{33,49},{49,1},{2,18}... | collective-permute-start | bytes 122888 | tf_op jit(solution)/shard_map/ppermute | solution.py:405
  75.5 6.3 %collective-permute-start.14 = (bf16[160,128]{1,0:T(8,128)(2,1)S(1)}, bf16[160,128]{1,0:T(8,128)(2,1)S(1)}, u32[]{:S(2)}, u32[]{:S(2)}) collective-permute-start(bf16[160,128]{1,0:T(8,128)(2,1)S(1)} %rel_z.1.refs_0_), channel_id=1, source_target_pairs={{0,32},{16,48},{32,0},{48,16},{1,33},{17,49},{33,1},{49,17},{2,34}... | collective-permute-start | bytes 122888 | tf_op jit(solution)/shard_map/ppermute | solution.py:405
  77.5 4.9 %collective-permute-start.15 = (bf16[160,128]{1,0:T(8,128)(2,1)S(1)}, bf16[160,128]{1,0:T(8,128)(2,1)S(1)}, u32[]{:S(2)}, u32[]{:S(2)}) collective-permute-start(bf16[160,128]{1,0:T(8,128)(2,1)S(1)} %rel_z.1.refs_0_), channel_id=1, source_target_pairs={{0,48},{16,0},{32,16},{48,32},{1,49},{17,1},{33,17},{49,33},{2,50}... | collective-permute-start | bytes 122888 | tf_op jit(solution)/shard_map/ppermute | solution.py:405
  82.5 10.1 %collective-permute-start.16 = (bf16[640,128]{1,0:T(8,128)(2,1)S(1)}, bf16[640,128]{1,0:T(8,128)(2,1)S(1)}, u32[]{:S(2)}, u32[]{:S(2)}) collective-permute-start(bf16[640,128]{1,0:T(8,128)(2,1)S(1)} %place_y.1.refs_0_), channel_id=1, source_target_pairs={{0,64},{64,128},{128,192},{192,0},{1,65},{65,129},{129,193},{193,1... | collective-permute-start | bytes 491528 | tf_op jit(solution)/shard_map/ppermute | solution.py:405
  82.5 13.7 %collective-permute-start.17 = (bf16[640,128]{1,0:T(8,128)(2,1)S(1)}, bf16[640,128]{1,0:T(8,128)(2,1)S(1)}, u32[]{:S(2)}, u32[]{:S(2)}) collective-permute-start(bf16[640,128]{1,0:T(8,128)(2,1)S(1)} %place_y.1.refs_0_), channel_id=1, source_target_pairs={{0,128},{64,192},{128,0},{192,64},{1,129},{65,193},{129,1},{193,65... | collective-permute-start | bytes 491528 | tf_op jit(solution)/shard_map/ppermute | solution.py:405
  84.9 12.4 %collective-permute-start.18 = (bf16[640,128]{1,0:T(8,128)(2,1)S(1)}, bf16[640,128]{1,0:T(8,128)(2,1)S(1)}, u32[]{:S(2)}, u32[]{:S(2)}) collective-permute-start(bf16[640,128]{1,0:T(8,128)(2,1)S(1)} %place_y.1.refs_0_), channel_id=1, source_target_pairs={{0,192},{64,0},{128,64},{192,128},{1,193},{65,1},{129,65},{193,129... | collective-permute-start | bytes 491528 | tf_op jit(solution)/shard_map/ppermute | solution.py:405
  97.4 3.6 %collective-permute-start.19 = (bf16[2560,128]{1,0:T(8,128)(2,1)S(1)}, bf16[2560,128]{1,0:T(8,128)(2,1)S(1)}, u32[]{:S(2)}, u32[]{:S(2)}) collective-permute-start(bf16[2560,128]{1,0:T(8,128)(2,1)S(1)} %place_x.1.mine_ref), channel_id=1, source_target_pairs={{0,1},{1,0},{2,3},{3,2},{4,5},{5,4},{6,7},{7,6},{8,9},{9,8},{10,11... | collective-permute-start | bytes 1966088 | tf_op jit(solution)/shard_map/ppermute | solution.py:409
